TPU v7x, 32 devices: a whole 2x2x4 slice. The times are simulated.
32 devices in a mesh: grp: 2 (over y), sec: 4 (over z), term: 4 (over x, core).
Axes of the slice: x: 2, y: 2, z: 4, core: 2. Of those that a mesh axis runs over, the one named last changes fastest.
Arguments:
- wavefunction: bfloat16 [16, 16, 2, 128, 128], P(('grp', 'sec')), parts along dimension 0, may hold values from -6 to 6
- left_window: bfloat16 [16, 48, 32, 128], P(('grp', 'sec'), 'term'), parts along dimension 0, may hold values from -0.5 to 0.5
- right_blocks: bfloat16 [16, 48, 128, 128], P(('grp', 'sec'), 'term'), parts along dimension 0, may hold values from -0.5 to 0.5
- couplings: float32 [48, 16], P('term'), may hold values from -0.875 to 0.875
- sector_order: int32 [16], P('grp'), parts along dimension 0, may hold values from 64 to 128
- partner: int32 [16, 16], P('grp'), parts along dimension 0, may hold values from 0 to 7, as said below
Outputs:
- products_out: bfloat16 [16, 16, 2, 32, 128], P(('grp', 'sec'), None, None, 'term'), parts along dimension 0
There are 2 independent parts, one for each index of `grp`. A program takes and returns all parts, laid end to end along the dimension named above; an argument that names none is the same for every part. Nothing has to cross between parts.
Inputs may be any that keep to these rules, and one draw needn't show every extreme that they name: The right sector partner[a, s] belongs to index partner[a, s] // 2 of sec. Of the 2 x 16 blocks of the sectors of one index of sec, at most 8 have right sectors of any one index, and that many is reached in every draw.
All inputs are finite; a program needn't handle non-finite values.
Results may differ from a plain program's by a relative error of at most 0.005.
Values may be sent and summed in bfloat16 or wider, within the bound.
No kernel may reach another device: no remote copies, remote signals or barrier semaphores. Data moves between devices by JAX's collectives and lax.ppermute only.
A program may use at most 128 MiB of HBM per device.

v0:
```python
import math

import jax
import jax.numpy as jnp
from jax import lax
from jax.sharding import PartitionSpec as P

SECTOR = 128
STATES = 16
ROWS = 32
SEC_DEV = 2


def lookup(values_table, indices):
    columns = jnp.arange(values_table.shape[0], dtype=jnp.int32)
    matched = (indices[..., None] == columns).astype(jnp.int32)
    return jnp.sum(matched * values_table, axis=-1)


def body(wavefunction, left_window, right_blocks, couplings, sector_order, partner):
    devices = lax.axis_size("sec")
    myself = lax.axis_index("sec")
    block_count = SEC_DEV * STATES
    capacity = max(1, block_count // devices)
    slot_count = devices * capacity
    term_local = left_window.shape[1]
    column_index = jnp.arange(SECTOR, dtype=jnp.int32)
    positions = jnp.arange(block_count, dtype=jnp.int32)
    partner_all = partner.reshape(devices, block_count)
    owner_all = partner_all // SEC_DEV
    earlier = positions[None, :] < positions[:, None]
    same_owner = owner_all[:, :, None] == owner_all[:, None, :]
    rank_all = jnp.sum((same_owner & earlier[None]).astype(jnp.int32), axis=2)
    own_owner = lax.dynamic_index_in_dim(owner_all, myself, 0, keepdims=False)
    own_rank = lax.dynamic_index_in_dim(rank_all, myself, 0, keepdims=False)
    own_partner = lax.dynamic_index_in_dim(partner_all, myself, 0, keepdims=False)
    send_slot = own_owner * capacity + own_rank
    slot_index = jnp.arange(capacity, dtype=jnp.int32)
    matches = (owner_all == myself)[:, :, None] & (
        rank_all[:, :, None] == slot_index[None, None, :]
    )
    hit_int = matches.astype(jnp.int32)
    incoming_partner = jnp.sum(hit_int * partner_all[:, :, None], axis=1).reshape(slot_count)
    incoming_state = jnp.sum(hit_int * (positions % STATES)[None, :, None], axis=1).reshape(
        slot_count
    )
    incoming_local = incoming_partner % SEC_DEV
    incoming_order = lookup(sector_order, incoming_partner)
    column_mask = (column_index[None, :] < incoming_order[:, None]).astype(jnp.float32)
    left_order = lax.dynamic_slice_in_dim(sector_order, myself * SEC_DEV, SEC_DEV)
    right_order = lookup(sector_order, own_partner).reshape(SEC_DEV, STATES)
    row_keep = column_index[None, :] < left_order[:, None]
    col_keep = column_index[None, None, :] < right_order[:, :, None]
    keep_mask = (row_keep[:, None, None, :, None] & col_keep[:, :, None, None, :]).astype(
        jnp.bfloat16
    )
    masked = wavefunction * keep_mask
    groups = math.gcd(slot_count, 8)
    per_group = slot_count // groups

    def right_product(partials, chosen, mask_rows):
        picked = jnp.take(right_blocks, chosen, axis=0)
        result = jnp.einsum(
            "gvtrn,gtnk->gvrk", partials, picked, preferred_element_type=jnp.float32
        )
        return result * mask_rows[:, None, None, :]

    vectors = masked.reshape(block_count, 2, SECTOR, SECTOR)
    left_rows = jnp.take(left_window, positions // STATES, axis=0)
    vector_slots = (
        jnp.zeros((slot_count, 2, SECTOR, SECTOR), jnp.bfloat16).at[send_slot].set(vectors)
    )
    row_slots = (
        jnp.zeros((slot_count, term_local, ROWS, SECTOR), jnp.bfloat16).at[send_slot].set(left_rows)
    )
    vector_in, rows_in = (
        lax.all_to_all(vector_slots, "sec", split_axis=0, concat_axis=0, tiled=True),
        lax.all_to_all(row_slots, "sec", split_axis=0, concat_axis=0, tiled=True),
    )
    slot_coupling = jnp.transpose(jnp.take(couplings, incoming_state, axis=1))

    def grouped_both(inputs):
        vector_group, rows_group, coupling_group, chosen_group, mask_group = inputs
        partials = jnp.einsum(
            "gtrn,gvnj->gvtrj", rows_group, vector_group, preferred_element_type=jnp.float32
        )
        partials = (partials * coupling_group[:, None, :, None, None]).astype(jnp.bfloat16)
        return right_product(partials, chosen_group, mask_group)

    outcome = lax.map(
        grouped_both,
        (
            vector_in.reshape(groups, per_group, 2, SECTOR, SECTOR),
            rows_in.reshape(groups, per_group, term_local, ROWS, SECTOR),
            slot_coupling.reshape(groups, per_group, term_local),
            incoming_local.reshape(groups, per_group),
            column_mask.reshape(groups, per_group, SECTOR),
        ),
    )
    outcome = outcome.reshape(slot_count, 2, ROWS, SECTOR)
    returned_rows = lax.all_to_all(outcome, "sec", split_axis=0, concat_axis=0, tiled=True)
    own_rows = jnp.take(returned_rows, send_slot, axis=0).reshape(SEC_DEV, STATES, 2, ROWS, SECTOR)
    summed = lax.psum_scatter(own_rows, "term", scatter_dimension=3, tiled=True)
    return summed.astype(jnp.bfloat16)


def solution(mesh):
    in_specs = (
        P(("grp", "sec"), None, None, None, None),
        P(("grp", "sec"), "term", None, None),
        P(("grp", "sec"), "term", None, None),
        P("term", None),
        P("grp"),
        P("grp", None),
    )
    out_specs = P(("grp", "sec"), None, None, "term", None)
    return jax.shard_map(body, mesh=mesh, in_specs=in_specs, out_specs=out_specs, check_vma=False)
```

profile of v0, /device:TPU:0, one launch (start us, length us, event | category | flops | bytes accessed | tf_op | source)
XLA Modules:
  0.0 238.9 jit_solution(7948931828745940383)
XLA Ops:
  6.6 0.8 reshape.331
  7.4 0.2 convert_reduce_fusion
  7.6 0.6 broadcast.386
  8.2 0.7 fusion.42
  8.9 0.2 select_reduce_fusion
  9.1 0.1 eq.81
  9.2 0.7 select_reduce_fusion.2
  10.0 0.1 lt.179
  10.1 0.7 dynamic_slice.35
  10.9 0.3 and_convert_fusion
  11.3 1.8 broadcast_multiply_fusion
  13.1 1.9 broadcast_in_dim.51
  15.0 5.5 %scatter_fusion = bf16[32,2,128,128]{3,2,1,0:T(8,128)(2,1)} fusion(bf16[32,2,128,128]{3,2,1,0:T(8,128)(2,1)} %broadcast_in_dim.51, s32[32]{0:T(128)S(1)} %get-tuple-element.75, bf16[32,2,128,128]{3,2,1,0:T(8,128)(2,1)S(1)} %bitcast.100), kind=kCustom, calls=%fused_computation.4 | custom fusion | bytes 6291584 | tf_op jit(solution)/shard_map/scatter | solution.py:71
  20.4 6.3 %all-to-all-start = ((bf16[32,2,128,128]{3,2,1,0:T(8,128)(2,1)}), bf16[32,2,128,128]{3,2,1,0:T(8,128)(2,1)}, u32[]{:S(2)}, u32[]{:S(2)}) async-start(bf16[32,2,128,128]{3,2,1,0:T(8,128)(2,1)} %scatter_fusion), calls=%async_computation | async-start | bytes 4194304 | tf_op jit(solution)/shard_map/all_to_all | solution.py:77
  26.7 0.1 reshape.335
  26.8 1.2 gather_fusion.1
  28.0 2.0 broadcast_select_fusion
  30.0 2.4 %broadcast_in_dim.52 = bf16[32,12,32,128]{3,2,1,0:T(8,128)(2,1)} broadcast(bf16[]{:T(256)} %constant.146.clone.1), dimensions={} | broadcast | bytes 3145730 | tf_op jit(solution)/shard_map/broadcast_in_dim | solution.py:74
  32.5 9.2 %scatter_fusion.1 = bf16[32,12,32,128]{3,2,1,0:T(8,128)(2,1)} fusion(bf16[32,12,32,128]{3,2,1,0:T(8,128)(2,1)} %broadcast_in_dim.52, s32[32]{0:T(128)S(1)} %get-tuple-element.75, bf16[32,12,32,128]{3,2,1,0:T(8,128)(2,1)S(1)} %copy-done.2), kind=kCustom, calls=%fused_computation.5 | custom fusion | bytes 9437312 | tf_op jit(solution)/shard_map/scatter | solution.py:74
  41.7 33.3 %all-to-all-done = bf16[32,2,128,128]{3,2,1,0:T(8,128)(2,1)} async-done(((bf16[32,2,128,128]{3,2,1,0:T(8,128)(2,1)}), bf16[32,2,128,128]{3,2,1,0:T(8,128)(2,1)}, u32[]{:S(2)}, u32[]{:S(2)}) %all-to-all-start) | async-done | bytes 2097184 | tf_op jit(solution)/shard_map/all_to_all | solution.py:77
  75.0 4.6 %all-to-all-start.1 = ((bf16[32,12,32,128]{3,2,1,0:T(8,128)(2,1)}), bf16[32,12,32,128]{3,2,1,0:T(8,128)(2,1)}, u32[]{:S(2)}, u32[]{:S(2)}) async-start(bf16[32,12,32,128]{3,2,1,0:T(8,128)(2,1)} %scatter_fusion.1), calls=%async_computation.1 | async-start | bytes 6291456 | tf_op jit(solution)/shard_map/all_to_all | solution.py:78
  79.7 0.1 reshape.336
  80.0 0.6 gather_fusion.2
  80.7 69.2 %all-to-all-done.1 = bf16[32,12,32,128]{3,2,1,0:T(8,128)(2,1)} async-done(((bf16[32,12,32,128]{3,2,1,0:T(8,128)(2,1)}), bf16[32,12,32,128]{3,2,1,0:T(8,128)(2,1)}, u32[]{:S(2)}, u32[]{:S(2)}) %all-to-all-start.1) | async-done | bytes 3145760 | tf_op jit(solution)/shard_map/all_to_all | solution.py:78
  149.9 26.0 %while.10 = (s32[]{:T(128)}, f32[8,4,2,32,128]{4,3,2,1,0:T(8,128)}, bf16[8,4,2,128,128]{4,3,2,1,0:T(8,128)(2,1)}, bf16[8,4,12,32,128]{4,3,2,1,0:T(8,128)(2,1)}, ...) while((s32[]{:T(128)}, f32[8,4,2,32,128]{4,3,2,1,0:T(8,128)}, ...), condition=%wide.region_8.9_spmd, body=%wide.region_7.8_spmd.sunk | while | flops 202933280 | bytes 5517573 | solution.py:90
  149.9 0.9 gather_fusion
  150.8 2.3 fusion.53
  153.2 0.8 gather_fusion
  154.1 2.3 fusion.53
  156.4 0.8 gather_fusion
  157.3 2.3 fusion.53
  159.7 0.8 gather_fusion
  160.6 2.3 fusion.53
  162.9 0.8 gather_fusion
  163.8 2.3 fusion.53
  166.1 0.8 gather_fusion
  167.1 2.3 fusion.53
  169.4 0.8 gather_fusion
  170.3 2.3 fusion.53
  172.6 0.8 gather_fusion
  173.6 2.3 fusion.53
  175.9 3.5 %all-to-all-start.2 = ((f32[32,2,32,128]{3,2,1,0:T(8,128)}), f32[32,2,32,128]{3,2,1,0:T(8,128)S(1)}, u32[]{:S(2)}, u32[]{:S(2)}) async-start(f32[32,2,32,128]{3,2,1,0:T(8,128)} %bitcast.102), calls=%async_computation.2 | async-start | bytes 2097152 | tf_op jit(solution)/shard_map/all_to_all | solution.py:101
  179.5 0.1 add.149
  179.6 25.0 %all-to-all-done.2 = f32[32,2,32,128]{3,2,1,0:T(8,128)S(1)} async-done(((f32[32,2,32,128]{3,2,1,0:T(8,128)}), f32[32,2,32,128]{3,2,1,0:T(8,128)S(1)}, u32[]{:S(2)}, u32[]{:S(2)}) %all-to-all-start.2) | async-done | bytes 1048608 | tf_op jit(solution)/shard_map/all_to_all | solution.py:101
  204.6 0.6 gather_fusion.3
  205.2 1.1 broadcast_select_fusion.1
  206.3 24.1 %reduce-scatter.2.cloned.1.call-done = f32[2,16,2,8,128]{4,3,2,1,0:T(8,128)} async-done(((f32[2,16,2,32,128]{4,3,2,1,0:T(8,128)}), f32[2,16,2,8,128]{4,3,2,1,0:T(8,128)}) %reduce-scatter.2.cloned.1.call-update) | async-done | bytes 262160 | tf_op jit(solution)/shard_map/reduce_scatter | solution.py:103
  230.5 1.6 convert_element_type.30
  (70 shorter events, 1.1 us)
Async XLA Ops:
  6.5 20.3 %copy-start = (bf16[2,12,32,128]{3,2,1,0:T(8,128)(2,1)S(1)}, bf16[2,12,32,128]{3,2,1,0:T(8,128)(2,1)}, u32[]{:S(2)}) copy-start(bf16[2,12,32,128]{3,2,1,0:T(8,128)(2,1)} %param.9) | copy-start | bytes 589828
  20.4 54.6 %all-to-all-start = ((bf16[32,2,128,128]{3,2,1,0:T(8,128)(2,1)}), bf16[32,2,128,128]{3,2,1,0:T(8,128)(2,1)}, u32[]{:S(2)}, u32[]{:S(2)}) async-start(bf16[32,2,128,128]{3,2,1,0:T(8,128)(2,1)} %scatter_fusion), calls=%async_computation | async-start | bytes 4194304 | tf_op jit(solution)/shard_map/all_to_all | solution.py:77
  30.0 2.4 %copy-start.2 = (bf16[32,12,32,128]{3,2,1,0:T(8,128)(2,1)S(1)}, bf16[32,12,32,128]{3,2,1,0:T(8,128)(2,1)}, u32[]{:S(2)}) copy-start(bf16[32,12,32,128]{3,2,1,0:T(8,128)(2,1)} %broadcast_select_fusion) | copy-start | bytes 9437188
  41.7 38.2 %copy-start.3 = (f32[12,16]{1,0:T(8,128)S(1)}, f32[12,16]{1,0:T(8,128)}, u32[]{:S(2)}) copy-start(f32[12,16]{1,0:T(8,128)} %param.11) | copy-start | bytes 2308
  41.7 108.2 %copy-start.1 = (bf16[2,12,128,128]{3,2,1,0:T(8,128)(2,1)S(1)}, bf16[2,12,128,128]{3,2,1,0:T(8,128)(2,1)}, u32[]{:S(2)}) copy-start(bf16[2,12,128,128]{3,2,1,0:T(8,128)(2,1)} %param.10) | copy-start | bytes 2359300
  75.0 74.9 %all-to-all-start.1 = ((bf16[32,12,32,128]{3,2,1,0:T(8,128)(2,1)}), bf16[32,12,32,128]{3,2,1,0:T(8,128)(2,1)}, u32[]{:S(2)}, u32[]{:S(2)}) async-start(bf16[32,12,32,128]{3,2,1,0:T(8,128)(2,1)} %scatter_fusion.1), calls=%async_computation.1 | async-start | bytes 6291456 | tf_op jit(solution)/shard_map/all_to_all | solution.py:78
  175.9 28.7 %all-to-all-start.2 = ((f32[32,2,32,128]{3,2,1,0:T(8,128)}), f32[32,2,32,128]{3,2,1,0:T(8,128)S(1)}, u32[]{:S(2)}, u32[]{:S(2)}) async-start(f32[32,2,32,128]{3,2,1,0:T(8,128)} %bitcast.102), calls=%async_computation.2 | async-start | bytes 2097152 | tf_op jit(solution)/shard_map/all_to_all | solution.py:101
  179.4 51.1 %reduce-scatter.2.cloned.1.call-start = ((), (), s32[]{:S(2)}) async-start(), calls=%async_computation.4 | async-start | bytes 1310720 | tf_op jit(solution)/shard_map/reduce_scatter | solution.py:103
Sparse Core Ops, SparseCore 0:
  206.5 23.9 reduce-scatter.1
where the time goes:
time: 240 us; the launch traced here: 239 us
  waiting for transfers between devices  152 us (63%)
  local copies, waits for them, and re-layouts  31.1 us (13%)
  matrix products  18.5 us (8%)
  starting transfers between devices  14.5 us (6%)
  between operations  13.5 us (6%)
  other arithmetic  9.41 us (4%)
    all_to_all x1, waiting for transfers between devices, body(): lax.all_to_all(row_slots, 'sec', split_axis=0, concat_axis=0, tiled=True)  69.2 us
    all_to_all x1, waiting for transfers between devices, body(): lax.all_to_all(vector_slots, 'sec', split_axis=0, concat_axis=0, tiled=True)  33.3 us
    all_to_all x1, waiting for transfers between devices, body(): lax.all_to_all(outcome, 'sec', split_axis=0, concat_axis=0, tiled=True)  25 us
    reduce_scatter x1, waiting for transfers between devices, body(): summed = lax.psum_scatter(own_rows, 'term', scatter_dimension=3, tiled=True)  24.1 us
    dot_general x8, matrix products, right_product(): jnp.einsum('gvtrn,gtnk->gvrk', partials, picked, preferred_element_type=j...  18.5 us
    scatter x1, local copies, waits for them, and re-layouts, body(): jnp.zeros((slot_count, term_local, ROWS, SECTOR), jnp.bfloat16)  9.22 us
    gather x8, local copies, waits for them, and re-layouts, right_product(): picked = jnp.take(right_blocks, chosen, axis=0)  6.79 us
    all_to_all x1, starting transfers between devices, body(): lax.all_to_all(vector_slots, 'sec', split_axis=0, concat_axis=0, tiled=True)  6.3 us
  transfers between devices with their start and end apart: 4, of which 4 were waited for; matrix products, arithmetic and copies ran while one was open for 7% of the time, Pallas kernels for 0%

commit v1 on v0

--- a/solution.py
+++ b/solution.py
@@ -1,8 +1,11 @@
+import functools
 import math
 
 import jax
 import jax.numpy as jnp
 from jax import lax
+from jax.experimental import pallas as pl
+from jax.experimental.pallas import tpu as pltpu
 from jax.sharding import PartitionSpec as P
 
 SECTOR = 128
@@ -17,7 +20,7 @@
     return jnp.sum(matched * values_table, axis=-1)
 
 
-def body(wavefunction, left_window, right_blocks, couplings, sector_order, partner):
+def general_body(wavefunction, left_window, right_blocks, couplings, sector_order, partner):
     devices = lax.axis_size("sec")
     myself = lax.axis_index("sec")
     block_count = SEC_DEV * STATES
@@ -104,6 +107,282 @@
     return summed.astype(jnp.bfloat16)
 
 
+ANY = pl.BlockSpec(memory_space=pl.ANY)
+VMEM = pl.BlockSpec(memory_space=pltpu.VMEM)
+SMEM = pl.BlockSpec(memory_space=pltpu.SMEM)
+
+
+def exchange(x, axis, step):
+    size = lax.axis_size(axis)
+    return lax.ppermute(x, axis, [(i, i ^ step) for i in range(size)])
+
+
+def gather_pieces(x, axis):
+    pieces = [x]
+    bit = lax.axis_size(axis) // 2
+    while bit:
+        pieces = pieces + [exchange(piece, axis, bit) for piece in pieces]
+        bit //= 2
+    return pieces
+
+
+def piece_order(size):
+    order = [0]
+    bit = size // 2
+    while bit:
+        order = order + [j ^ bit for j in order]
+        bit //= 2
+    return order
+
+
+def pack_kernel(devices, terms, partner, wave, left, *refs):
+    sends = refs[: devices - 1]
+    left_out, counts, table, sems = refs[devices - 1 :]
+    capacity = SEC_DEV * STATES // devices
+    share = capacity // terms
+    me, term = lax.axis_index("sec"), lax.axis_index("term")
+    for owner in range(devices):
+        counts[owner] = 0
+
+    def place(n, carry):
+        owner = partner[me * SEC_DEV + n // STATES, n % STATES] // SEC_DEV
+        rank = counts[owner]
+        counts[owner] = rank + 1
+        table[owner * capacity + rank] = n
+        return carry
+
+    lax.fori_loop(0, SEC_DEV * STATES, place, 0)
+    copies = []
+    for step in range(1, devices):
+        target = me ^ step
+        for sub in range(share):
+            n = table[target * capacity + term * share + sub]
+            copy = pltpu.make_async_copy(
+                wave.at[n], sends[step - 1].at[sub], sems.at[(step - 1) * share + sub]
+            )
+            copy.start()
+            copies.append(copy)
+    local = left.shape[1]
+    group = ROWS // terms
+    for a in range(SEC_DEV):
+        for t in range(0, local, 2):
+            first = left[a, t].astype(jnp.float32)
+            second = left[a, t + 1].astype(jnp.float32)
+            for piece in range(terms):
+                rows = slice(piece * group, (piece + 1) * group)
+                pair = jnp.concatenate([first[rows], second[rows]], axis=0)
+                left_out[piece, a, t * group : (t + 2) * group, :] = pair.astype(jnp.bfloat16)
+    for copy in copies:
+        copy.wait()
+
+
+def pack(wave, left, partner, devices, terms):
+    capacity = SEC_DEV * STATES // devices
+    share = capacity // terms
+    local = left.shape[1]
+    piece = jax.ShapeDtypeStruct((share, 2, SECTOR, SECTOR), jnp.bfloat16)
+    rows = jax.ShapeDtypeStruct((terms, SEC_DEV, local * (ROWS // terms), SECTOR), jnp.bfloat16)
+    outs = pl.pallas_call(
+        functools.partial(pack_kernel, devices, terms),
+        out_shape=[piece] * (devices - 1) + [rows],
+        in_specs=[SMEM, ANY, VMEM],
+        out_specs=[ANY] * (devices - 1) + [VMEM],
+        scratch_shapes=[
+            pltpu.SMEM((devices,), jnp.int32),
+            pltpu.SMEM((SEC_DEV * STATES,), jnp.int32),
+            pltpu.SemaphoreType.DMA(((devices - 1) * share,)),
+        ],
+        cost_estimate=pl.CostEstimate(flops=0, bytes_accessed=4 << 20, transcendentals=0),
+        name="pack",
+    )(partner, wave, left)
+    return outs[: devices - 1], outs[devices - 1]
+
+
+def compute_kernel(step, devices, terms, partner, order, coef, *refs):
+    pieces = refs[: 1 if step == 0 else terms]
+    refs = refs[len(pieces) :]
+    left, rights, out = refs[0], refs[1 : 1 + terms], refs[1 + terms]
+    table, partials = refs[2 + terms : 4 + terms]
+    capacity = SEC_DEV * STATES // devices
+    share = capacity // terms
+    js = piece_order(terms)
+    me, term = lax.axis_index("sec"), lax.axis_index("term")
+    source = me ^ step
+    local = left.shape[2] // (ROWS // terms)
+    depth = local * SECTOR
+
+    def place(n, count):
+        table[count] = n
+        owner = partner[source * SEC_DEV + n // STATES, n % STATES] // SEC_DEV
+        return count + jnp.where(owner == me, 1, 0)
+
+    lax.fori_loop(0, SEC_DEV * STATES, place, 0)
+    if step == 0:
+        wave, (blocks, sems) = pieces[0], refs[4 + terms :]
+        copies = []
+        for slot in range(capacity):
+            copy = pltpu.make_async_copy(wave.at[table[slot]], blocks.at[slot], sems.at[slot])
+            copy.start()
+            copies.append(copy)
+        for copy in copies:
+            copy.wait()
+    row_index = lax.broadcasted_iota(jnp.int32, (SECTOR, SECTOR), 0)
+    col_index = lax.broadcasted_iota(jnp.int32, (SECTOR, SECTOR), 1)
+    group = ROWS // terms
+
+    def slot_of(j, sub):
+        return (term ^ js[j]) * share + sub
+
+    def first(j, sub):
+        slot = slot_of(j, sub)
+        n = table[slot]
+        sector, state = n // STATES, n % STATES
+        left_id = source * SEC_DEV + sector
+        left_order = order[left_id]
+        right_order = order[partner[left_id, state]]
+        keep = (row_index < left_order) & (col_index < right_order)
+        block = blocks.at[slot] if step == 0 else pieces[j].at[sub]
+        vectors = [
+            jnp.where(keep, block[v].astype(jnp.float32), 0.0).astype(jnp.bfloat16)
+            for v in range(2)
+        ]
+        both = jnp.concatenate(vectors, axis=1)
+        place_row = pl.multiple_of((j * share + sub) * 2 * group, 2 * group)
+        for i in range(terms):
+            origin = term ^ js[i]
+            product = jnp.dot(left[origin, sector], both, preferred_element_type=jnp.float32)
+            for t in range(local):
+                rows = product[t * group : (t + 1) * group]
+                pair = jnp.concatenate([rows[:, :SECTOR], rows[:, SECTOR:]], axis=0)
+                pair = pair * coef[origin * local + t, state]
+                start = (i * local + t) * SECTOR
+                partials[pl.ds(place_row, 2 * group), start : start + SECTOR] = pair.astype(
+                    jnp.bfloat16
+                )
+
+    for j in range(terms):
+
+        def inner(sub, carry, j=j):
+            first(j, sub)
+            return carry
+
+        lax.fori_loop(0, share, inner, 0)
+
+    total = jnp.zeros((capacity * 2 * group, SEC_DEV * SECTOR), jnp.float32)
+    for i in range(terms):
+        right = [rights[i][p].reshape(depth, SECTOR) for p in range(SEC_DEV)]
+        total = total + jnp.dot(
+            partials[:, i * depth : (i + 1) * depth],
+            jnp.concatenate(right, axis=1),
+            preferred_element_type=jnp.float32,
+        )
+    column = lax.broadcasted_iota(jnp.int32, (2 * group, SECTOR), 1)
+    for j in range(terms):
+        for sub in range(share):
+            slot = slot_of(j, sub)
+            n = table[slot]
+            right_id = partner[source * SEC_DEV + n // STATES, n % STATES]
+            start = (j * share + sub) * 2 * group
+            mine = total[start : start + 2 * group]
+            result = mine[:, :SECTOR]
+            for p in range(1, SEC_DEV):
+                result = jnp.where(
+                    right_id % SEC_DEV == p, mine[:, p * SECTOR : (p + 1) * SECTOR], result
+                )
+            result = jnp.where(column < order[right_id], result, 0.0)
+            for v in range(2):
+                out[slot, v] = result[v * group : (v + 1) * group].astype(jnp.bfloat16)
+
+
+def compute(step, pieces, left, rights, coef, order, partner, devices, terms):
+    capacity = SEC_DEV * STATES // devices
+    group = ROWS // terms
+    local = left.shape[2] // group
+    scratch = [
+        pltpu.SMEM((SEC_DEV * STATES + 1,), jnp.int32),
+        pltpu.VMEM((capacity * 2 * group, terms * local * SECTOR), jnp.bfloat16),
+    ]
+    if step == 0:
+        scratch += [
+            pltpu.VMEM((capacity, 2, SECTOR, SECTOR), jnp.bfloat16),
+            pltpu.SemaphoreType.DMA((capacity,)),
+        ]
+    return pl.pallas_call(
+        functools.partial(compute_kernel, step, devices, terms),
+        out_shape=jax.ShapeDtypeStruct((capacity, 2, group, SECTOR), jnp.bfloat16),
+        in_specs=[SMEM] * 3 + [ANY if step == 0 else VMEM] * len(pieces) + [VMEM] * (1 + terms),
+        out_specs=VMEM,
+        scratch_shapes=scratch,
+        compiler_params=pltpu.CompilerParams(vmem_limit_bytes=32 << 20),
+        cost_estimate=pl.CostEstimate(
+            flops=3 << 30, bytes_accessed=4 << 20, transcendentals=0
+        ),
+        name=f"products_{step}",
+    )(partner, order, coef, *pieces, left, *rights)
+
+
+def unpack_kernel(devices, partner, *refs):
+    chunks, out, counts = refs[:devices], refs[devices], refs[devices + 1]
+    me = lax.axis_index("sec")
+    for owner in range(devices):
+        counts[owner] = 0
+
+    def place(n, carry):
+        owner = partner[me * SEC_DEV + n // STATES, n % STATES] // SEC_DEV
+        rank = counts[owner]
+        counts[owner] = rank + 1
+        for step in range(devices):
+
+            @pl.when((me ^ step) == owner)
+            def _():
+                out[n] = chunks[step][rank]
+
+        return carry
+
+    lax.fori_loop(0, SEC_DEV * STATES, place, 0)
+
+
+def unpack(chunks, partner, devices):
+    return pl.pallas_call(
+        functools.partial(unpack_kernel, devices),
+        out_shape=jax.ShapeDtypeStruct((SEC_DEV * STATES,) + chunks[0].shape[1:], jnp.bfloat16),
+        in_specs=[SMEM] + [VMEM] * devices,
+        out_specs=VMEM,
+        scratch_shapes=[pltpu.SMEM((devices,), jnp.int32)],
+        cost_estimate=pl.CostEstimate(flops=0, bytes_accessed=1 << 20, transcendentals=0),
+        name="unpack",
+    )(partner, *chunks)
+
+
+def paired_body(wavefunction, left_window, right_blocks, couplings, sector_order, partner):
+    devices, terms = lax.axis_size("sec"), lax.axis_size("term")
+    block_count = SEC_DEV * STATES
+    wave = wavefunction.reshape(block_count, 2, SECTOR, SECTOR)
+    steps = list(range(devices - 1, 0, -1))
+    coef = lax.all_gather(couplings, "term", axis=0, tiled=True)
+    rights = gather_pieces(right_blocks, "term")
+    sends, left_cut = pack(wave, left_window, partner, devices, terms)
+    arrived = {step: exchange(sends[step - 1], "sec", step) for step in steps}
+    left_all = lax.all_to_all(left_cut, "term", split_axis=0, concat_axis=0, tiled=True)
+    lefts = {step: exchange(left_all, "sec", step) for step in steps}
+    lefts[0] = left_all
+    vectors = {step: gather_pieces(arrived[step], "term") for step in steps}
+    vectors[0] = [wave]
+    results = {
+        step: compute(
+            step, vectors[step], lefts[step], rights, coef, sector_order, partner, devices, terms
+        )
+        for step in [0] + steps
+    }
+    chunks = [results[0]] + [exchange(results[step], "sec", step) for step in range(1, devices)]
+    out = unpack(chunks, partner, devices)
+    return out.reshape(SEC_DEV, STATES, 2, ROWS // terms, SECTOR)
+
+
+def power_of_two(number):
+    return number & (number - 1) == 0
+
+
 def solution(mesh):
     in_specs = (
         P(("grp", "sec"), None, None, None, None),
@@ -114,4 +393,13 @@
         P("grp", None),
     )
     out_specs = P(("grp", "sec"), None, None, "term", None)
+    devices, terms = mesh.shape["sec"], mesh.shape["term"]
+    paired = (
+        power_of_two(devices)
+        and power_of_two(terms)
+        and devices <= 8
+        and SEC_DEV * STATES % (devices * terms) == 0
+        and ROWS == 8 * terms
+    )
+    body = paired_body if paired else general_body
     return jax.shard_map(body, mesh=mesh, in_specs=in_specs, out_specs=out_specs, check_vma=False)

time: 240 us -> 98.9 us (0.41)
  waiting for transfers between devices: 152 us -> 29.7 us
  Pallas kernels: 0 us -> 35.7 us
  local copies, waits for them, and re-layouts: 31.1 us -> 1.86 us
  matrix products: 18.5 us -> 0 us
  between operations: 13.5 us -> 0.13 us
  starting transfers between devices: 14.5 us -> 26 us
  other arithmetic: 9.41 us -> 0 us
  blocking collectives: 0 us -> 5.19 us
    all_to_all x3 -> x1, waiting for transfers between devices: 128 us -> 0.01 us  [paired_body(): lax.all_to_all(left_cut, 'term', split_axis=0, concat_axis=0, tiled=True)]
    pallas_call x0 -> x6, Pallas kernels: none -> 35.7 us  [the longest x4 17.1 us: compute(): pl.pallas_call(functools.partial(compute_kernel, step, devices, terms), o...]
    ppermute x0 -> x21, waiting for transfers between devices: none -> 29.7 us  [exchange(): return lax.ppermute(x, axis, [(i, i ^ step) for i in range(size)])]
    reduce_scatter x1 -> x0, waiting for transfers between devices: 24.1 us -> none  [body(): summed = lax.psum_scatter(own_rows, 'term', scatter_dimension=3, tiled=True)]
    ppermute x0 -> x21, starting transfers between devices: none -> 22.6 us  [exchange(): return lax.ppermute(x, axis, [(i, i ^ step) for i in range(size)])]
    dot_general x8 -> x0, matrix products: 18.5 us -> none  [right_product(): jnp.einsum('gvtrn,gtnk->gvrk', partials, picked, preferred_element_type=j...]
    scatter x2 -> x0, local copies, waits for them, and re-layouts: 14.7 us -> none  [the longest x1 9.22 us: body(): jnp.zeros((slot_count, term_local, ROWS, SECTOR), jnp.bfloat16)]
    all_to_all x3 -> x1, starting transfers between devices: 14.4 us -> 3.36 us  [paired_body(): lax.all_to_all(left_cut, 'term', split_axis=0, concat_axis=0, tiled=True)]
  transfers between devices with their start and end apart: 4 -> 22, of which waited for: 4 -> 5; matrix products, arithmetic and copies ran while one was open for 7% -> 0% of each run, Pallas kernels for 0% -> 33%
where the time goes in v1:
time: 98.9 us; the launch traced here: 98.6 us
  Pallas kernels  35.7 us (36%)
  waiting for transfers between devices  29.7 us (30%)
  starting transfers between devices  26 us (26%)
  blocking collectives  5.19 us (5%)
  local copies, waits for them, and re-layouts  1.86 us (2%)
    ppermute x21, waiting for transfers between devices, exchange(): return lax.ppermute(x, axis, [(i, i ^ step) for i in range(size)])  29.7 us
    ppermute x21, starting transfers between devices, exchange(): return lax.ppermute(x, axis, [(i, i ^ step) for i in range(size)])  22.6 us
    pallas_call x4, Pallas kernels, compute(): pl.pallas_call(functools.partial(compute_kernel, step, devices, terms), o...  17.1 us
    pallas_call x1, Pallas kernels, pack(): pl.pallas_call(functools.partial(pack_kernel, devices, terms), out_shape=...  15.6 us
    all_gather x1, blocking collectives, paired_body(): coef = lax.all_gather(couplings, 'term', axis=0, tiled=True)  5.19 us
    all_to_all x1, starting transfers between devices, paired_body(): lax.all_to_all(left_cut, 'term', split_axis=0, concat_axis=0, tiled=True)  3.36 us
    pallas_call x1, Pallas kernels, unpack(): pl.pallas_call(functools.partial(unpack_kernel, devices), out_shape=jax.S...  2.97 us
  transfers between devices with their start and end apart: 22, of which 5 were waited for; matrix products, arithmetic and copies ran while one was open for 0% of the time, Pallas kernels for 33%

profile of v1, /device:TPU:0, one launch (start us, length us, event | category | flops | bytes accessed | tf_op | source)
XLA Modules:
  0.0 98.6 jit_solution(16156358481592468342)
XLA Ops:
  0.0 3.0 %collective-permute-start = (bf16[2,12,128,128]{3,2,1,0:T(8,128)(2,1)}, bf16[2,12,128,128]{3,2,1,0:T(8,128)(2,1)S(1)}, u32[]{:S(2)}, u32[]{:S(2)}) collective-permute-start(bf16[2,12,128,128]{3,2,1,0:T(8,128)(2,1)} %refs_5_.5), channel_id=1, source_target_pairs={{0,2},{1,3},{2,0},{3,1},{4,6},{5,7},{6,4},{7,5},{8,10},{9,11},{10,... | collective-permute-start | bytes 2359304 | tf_op jit(solution)/shard_map/ppermute | solution.py:117
  3.0 0.0 collective-permute-start.1
  3.0 17.7 %collective-permute-done.refs_3_.refs_6_ = bf16[2,12,128,128]{3,2,1,0:T(8,128)(2,1)S(1)} collective-permute-done((bf16[2,12,128,128]{3,2,1,0:T(8,128)(2,1)}, bf16[2,12,128,128]{3,2,1,0:T(8,128)(2,1)S(1)}, u32[]{:S(2)}, u32[]{:S(2)}) %collective-permute-start) | collective-permute-done | bytes 786464 | tf_op jit(solution)/shard_map/ppermute | solution.py:117
  20.8 0.0 collective-permute-start.2
  20.8 15.6 %pack.1 = (bf16[2,2,128,128]{3,2,1,0:T(8,128)(2,1)}, bf16[2,2,128,128]{3,2,1,0:T(8,128)(2,1)}, bf16[2,2,128,128]{3,2,1,0:T(8,128)(2,1)}, bf16[4,2,96,128]{3,2,1,0:T(8,128)(2,1)}) custom-call(s32[8,16]{1,0:T(8,128)} %partner.11, bf16[32,2,128,128]{3,2,1,0:T(8,128)(2,1)} %bitcast.3, bf16[2,12,32,128]{3,2,1,0:T(8,128)(2,1)} %left.1), custom_call_target="tpu_custom_call" | custom-call | bytes 4194304 | tf_op jit(solution)/shard_map/pack/pallas_call | solution.py:185
  36.3 3.9 %collective-permute-start.15 = (bf16[2,2,128,128]{3,2,1,0:T(8,128)(2,1)}, bf16[2,2,128,128]{3,2,1,0:T(8,128)(2,1)}, u32[]{:S(2)}, u32[]{:S(2)}) collective-permute-start(bf16[2,2,128,128]{3,2,1,0:T(8,128)(2,1)} %get-tuple-element.12), channel_id=1, source_target_pairs={{0,12},{4,8},{8,4},{12,0},{1,13},{5,9},{9,5},{13,1},{2,14},{6,10},... | collective-permute-start | bytes 393224 | tf_op jit(solution)/shard_map/ppermute | solution.py:117
  40.3 0.0 collective-permute-start.9
  40.3 3.4 %all-to-all-start = ((bf16[4,2,96,128]{3,2,1,0:T(8,128)(2,1)}), bf16[4,2,96,128]{3,2,1,0:T(8,128)(2,1)S(1)}, u32[]{:S(2)}, u32[]{:S(2)}) async-start(bf16[4,2,96,128]{3,2,1,0:T(8,128)(2,1)} %get-tuple-element.9), calls=%async_computation | async-start | bytes 393216 | tf_op jit(solution)/shard_map/all_to_all | solution.py:366
  43.6 0.7 collective-permute-start.3
  44.3 0.7 collective-permute-done.15.refs_0_
  45.0 1.6 %collective-permute-start.16 = (bf16[2,2,128,128]{3,2,1,0:T(8,128)(2,1)}, bf16[2,2,128,128]{3,2,1,0:T(8,128)(2,1)}, u32[]{:S(2)}, u32[]{:S(2)}) collective-permute-start(bf16[2,2,128,128]{3,2,1,0:T(8,128)(2,1)} %collective-permute-done.15.refs_0_), channel_id=1, source_target_pairs={{0,2},{1,3},{2,0},{3,1},{4,6},{5,7},{6,4},{7,5},{8,10},{9,11},{10,... | collective-permute-start | bytes 393224 | tf_op jit(solution)/shard_map/ppermute | solution.py:117
  46.6 5.8 %collective-permute-done.9.refs_0_ = bf16[2,2,128,128]{3,2,1,0:T(8,128)(2,1)} collective-permute-done((bf16[2,2,128,128]{3,2,1,0:T(8,128)(2,1)}, bf16[2,2,128,128]{3,2,1,0:T(8,128)(2,1)}, u32[]{:S(2)}, u32[]{:S(2)}) %collective-permute-start.9) | collective-permute-done | bytes 131104 | tf_op jit(solution)/shard_map/ppermute | solution.py:117
  52.4 0.0 collective-permute-start.17
  52.4 0.1 collective-permute-done.3.refs_0_
  52.6 2.6 %collective-permute-start.19 = (bf16[4,2,96,128]{3,2,1,0:T(8,128)(2,1)S(1)}, bf16[4,2,96,128]{3,2,1,0:T(8,128)(2,1)}, u32[]{:S(2)}, u32[]{:S(2)}) collective-permute-start(bf16[4,2,96,128]{3,2,1,0:T(8,128)(2,1)S(1)} %all-to-all-done.refs_1_), channel_id=1, source_target_pairs={{0,12},{4,8},{8,4},{12,0},{1,13},{5,9},{9,5},{13,1},{2,14},{6,10},... | collective-permute-start | bytes 589832 | tf_op jit(solution)/shard_map/ppermute | solution.py:117
  55.2 0.0 collective-permute-done.16.refs_1_
  55.2 1.7 %collective-permute-start.10 = (bf16[2,2,128,128]{3,2,1,0:T(8,128)(2,1)}, bf16[2,2,128,128]{3,2,1,0:T(8,128)(2,1)}, u32[]{:S(2)}, u32[]{:S(2)}) collective-permute-start(bf16[2,2,128,128]{3,2,1,0:T(8,128)(2,1)} %collective-permute-done.9.refs_0_), channel_id=1, source_target_pairs={{0,2},{1,3},{2,0},{3,1},{4,6},{5,7},{6,4},{7,5},{8,10},{9,11},{10,... | collective-permute-start | bytes 393224 | tf_op jit(solution)/shard_map/ppermute | solution.py:117
  56.8 0.0 collective-permute-done.17.refs_2_
  56.9 5.2 %all-gather = f32[4,12,16]{2,1,0:T(8,128)S(1)} all-gather(f32[1,12,16]{2,1,0:T(8,128)S(1)} %bitcast.5), channel_id=1, replica_groups=mesh['grp'=2,'sec'=4,'term'=4] {'term'}, dimensions={0}, use_global_device_ids=true | all-gather | bytes 3840 | tf_op jit(solution)/shard_map/all_gather | solution.py:362
  62.1 0.0 collective-permute-done.10.refs_1_
  62.1 0.4 collective-permute-start.11
  62.4 0.0 collective-permute-done.19.refs_4_
  62.5 1.3 %collective-permute-start.4 = (bf16[2,2,128,128]{3,2,1,0:T(8,128)(2,1)S(1)}, bf16[2,2,128,128]{3,2,1,0:T(8,128)(2,1)S(1)}, u32[]{:S(2)}, u32[]{:S(2)}) collective-permute-start(bf16[2,2,128,128]{3,2,1,0:T(8,128)(2,1)S(1)} %collective-permute-done.3.refs_0_), channel_id=1, source_target_pairs={{0,2},{1,3},{2,0},{3,1},{4,6},{5,7},{6,4},{7,5},{8,10},{9,11},{10,... | collective-permute-start | bytes 393224 | tf_op jit(solution)/shard_map/ppermute | solution.py:117
  63.7 0.0 collective-permute-done.18.refs_3_
  63.7 1.5 %collective-permute-start.13 = (bf16[4,2,96,128]{3,2,1,0:T(8,128)(2,1)S(1)}, bf16[4,2,96,128]{3,2,1,0:T(8,128)(2,1)S(1)}, u32[]{:S(2)}, u32[]{:S(2)}) collective-permute-start(bf16[4,2,96,128]{3,2,1,0:T(8,128)(2,1)S(1)} %all-to-all-done.refs_1_), channel_id=1, source_target_pairs={{0,8},{4,12},{8,0},{12,4},{1,9},{5,13},{9,1},{13,5},{2,10},{6,14},... | collective-permute-start | bytes 589832 | tf_op jit(solution)/shard_map/ppermute | solution.py:117
  65.2 0.0 collective-permute-done.2.refs_5_.refs_8_
  65.2 0.2 collective-permute-start.12
  65.4 4.2 %products_3.1 = bf16[8,2,8,128]{3,2,1,0:T(8,128)(2,1)S(1)} custom-call(s32[8,16]{1,0:T(8,128)S(1)} %copy-done.2, s32[8]{0:T(128)S(1)} %copy-done.4, f32[48,16]{1,0:T(8,128)S(1)} %reshape.10.coef, bf16[2,2,128,128]{3,2,1,0:T(8,128)(2,1)} %collective-permute-done.15.refs_0_, bf16[2,2,128,128]{3,2,1,0:T(8,128)(2,1)} %collective-permute-done.16.refs_1_, ...), custom_call_target="tpu_custom_call" | custom-call | flops 3221225472 | bytes 4194304 | tf_op jit(solution)/shard_map/products_3/pallas_call | solution.py:310
  69.6 0.0 collective-permute-done.11.refs_2_
  69.6 1.2 %collective-permute-start.7 = (bf16[4,2,96,128]{3,2,1,0:T(8,128)(2,1)S(1)}, bf16[4,2,96,128]{3,2,1,0:T(8,128)(2,1)S(1)}, u32[]{:S(2)}, u32[]{:S(2)}) collective-permute-start(bf16[4,2,96,128]{3,2,1,0:T(8,128)(2,1)S(1)} %all-to-all-done.refs_1_), channel_id=1, source_target_pairs={{0,4},{4,0},{8,12},{12,8},{1,5},{5,1},{9,13},{13,9},{2,6},{6,2},{1... | collective-permute-start | bytes 589832 | tf_op jit(solution)/shard_map/ppermute | solution.py:117
  70.9 0.0 collective-permute-done.4.refs_1_
  70.9 0.1 collective-permute-start.6
  70.9 5.3 %collective-permute-done.13.refs_4_ = bf16[4,2,96,128]{3,2,1,0:T(8,128)(2,1)S(1)} collective-permute-done((bf16[4,2,96,128]{3,2,1,0:T(8,128)(2,1)S(1)}, bf16[4,2,96,128]{3,2,1,0:T(8,128)(2,1)S(1)}, u32[]{:S(2)}, u32[]{:S(2)}) %collective-permute-start.13) | collective-permute-done | bytes 196640 | tf_op jit(solution)/shard_map/ppermute | solution.py:117
  76.3 2.0 %collective-permute-start.20 = (bf16[8,2,8,128]{3,2,1,0:T(8,128)(2,1)S(1)}, bf16[8,2,8,128]{3,2,1,0:T(8,128)(2,1)S(1)}, u32[]{:S(2)}, u32[]{:S(2)}) collective-permute-start(bf16[8,2,8,128]{3,2,1,0:T(8,128)(2,1)S(1)} %products_3.1), channel_id=1, source_target_pairs={{0,12},{4,8},{8,4},{12,0},{1,13},{5,9},{9,5},{13,1},{2,14},{6,10},... | collective-permute-start | bytes 98312 | tf_op jit(solution)/shard_map/ppermute | solution.py:117
  78.3 4.0 %products_2.1 = bf16[8,2,8,128]{3,2,1,0:T(8,128)(2,1)S(1)} custom-call(s32[8,16]{1,0:T(8,128)S(1)} %copy-done.2, s32[8]{0:T(128)S(1)} %copy-done.4, f32[48,16]{1,0:T(8,128)S(1)} %reshape.10.coef, bf16[2,2,128,128]{3,2,1,0:T(8,128)(2,1)} %collective-permute-done.9.refs_0_, bf16[2,2,128,128]{3,2,1,0:T(8,128)(2,1)} %collective-permute-done.10.refs_1_, ...), custom_call_target="tpu_custom_call" | custom-call | flops 3221225472 | bytes 4194304 | tf_op jit(solution)/shard_map/products_2/pallas_call | solution.py:310
  82.3 0.0 copy-start
  82.3 0.1 collective-permute-start.14
  82.4 0.0 collective-permute-done.5.refs_2_
  82.4 0.0 collective-permute-done.7.refs_4_
  82.4 4.0 %products_1.1 = bf16[8,2,8,128]{3,2,1,0:T(8,128)(2,1)S(1)} custom-call(s32[8,16]{1,0:T(8,128)S(1)} %copy-done.2, s32[8]{0:T(128)S(1)} %copy-done.4, f32[48,16]{1,0:T(8,128)S(1)} %reshape.10.coef, bf16[2,2,128,128]{3,2,1,0:T(8,128)(2,1)S(1)} %collective-permute-done.3.refs_0_, bf16[2,2,128,128]{3,2,1,0:T(8,128)(2,1)S(1)} %collective-permute-done.4.refs_1_, ...), custom_call_target="tpu_custom_call" | custom-call | flops 3221225472 | bytes 4194304 | tf_op jit(solution)/shard_map/products_1/pallas_call | solution.py:310
  86.5 2.4 %collective-permute-start.8 = (bf16[8,2,8,128]{3,2,1,0:T(8,128)(2,1)S(1)}, bf16[8,2,8,128]{3,2,1,0:T(8,128)(2,1)S(1)}, u32[]{:S(2)}, u32[]{:S(2)}) collective-permute-start(bf16[8,2,8,128]{3,2,1,0:T(8,128)(2,1)S(1)} %products_1.1), channel_id=1, source_target_pairs={{0,4},{4,0},{8,12},{12,8},{1,5},{5,1},{9,13},{13,9},{2,6},{6,2},{1... | collective-permute-start | bytes 98312 | tf_op jit(solution)/shard_map/ppermute | solution.py:117
  88.9 4.8 %products_0.1.refs_0_ = bf16[8,2,8,128]{3,2,1,0:T(8,128)(2,1)S(1)} custom-call(s32[8,16]{1,0:T(8,128)S(1)} %copy-done.2, s32[8]{0:T(128)S(1)} %copy-done.4, f32[48,16]{1,0:T(8,128)S(1)} %reshape.10.coef, bf16[32,2,128,128]{3,2,1,0:T(8,128)(2,1)S(1)} %bitcast.4, bf16[4,2,96,128]{3,2,1,0:T(8,128)(2,1)S(1)} %all-to-all-done.refs_1_, ...), custom_call_target="tpu_custom_call" | custom-call | flops 3221225472 | bytes 4194304 | tf_op jit(solution)/shard_map/products_0/pallas_call | solution.py:310
  93.7 0.6 copy-done.1
  94.3 0.0 collective-permute-done.20.refs_3_
  94.4 0.6 copy-done.6
  95.0 0.0 collective-permute-done.8.refs_1_
  95.0 0.6 copy-done.7
  95.6 3.0 %unpack.1 = bf16[32,2,8,128]{3,2,1,0:T(8,128)(2,1)} custom-call(s32[8,16]{1,0:T(8,128)} %partner.11, bf16[8,2,8,128]{3,2,1,0:T(8,128)(2,1)} %copy-done.1, bf16[8,2,8,128]{3,2,1,0:T(8,128)(2,1)} %copy-done.7, bf16[8,2,8,128]{3,2,1,0:T(8,128)(2,1)} %copy-done.6, bf16[8,2,8,128]{3,2,1,0:T(8,128)(2,1)} %copy-done.5), custom_call_target="tpu_custom_call" | custom-call | bytes 1048576 | tf_op jit(solution)/shard_map/unpack/pallas_call | solution.py:346
  (22 shorter events, 0.0 us)
Async XLA Ops:
  0.0 65.4 %copy-start.3 = (bf16[2,12,128,128]{3,2,1,0:T(8,128)(2,1)S(1)}, bf16[2,12,128,128]{3,2,1,0:T(8,128)(2,1)}, u32[]{:S(2)}) copy-start(bf16[2,12,128,128]{3,2,1,0:T(8,128)(2,1)} %refs_5_.5) | copy-start | bytes 2359300
  0.0 65.4 %copy-start.2 = (s32[8,16]{1,0:T(8,128)S(1)}, s32[8,16]{1,0:T(8,128)}, u32[]{:S(2)}) copy-start(s32[8,16]{1,0:T(8,128)} %partner.11) | copy-start | bytes 1540
  0.0 56.9 %copy-start.8 = (f32[12,16]{1,0:T(8,128)S(1)}, f32[12,16]{1,0:T(8,128)}, u32[]{:S(2)}) copy-start(f32[12,16]{1,0:T(8,128)} %param.9) | copy-start | bytes 2308
  0.0 65.4 %copy-start.4 = (s32[8]{0:T(128)S(1)}, s32[8]{0:T(128)}, u32[]{:S(2)}) copy-start(s32[8]{0:T(128)} %order.7) | copy-start | bytes 100
  0.0 20.8 %collective-permute-start = (bf16[2,12,128,128]{3,2,1,0:T(8,128)(2,1)}, bf16[2,12,128,128]{3,2,1,0:T(8,128)(2,1)S(1)}, u32[]{:S(2)}, u32[]{:S(2)}) collective-permute-start(bf16[2,12,128,128]{3,2,1,0:T(8,128)(2,1)} %refs_5_.5), channel_id=1, source_target_pairs={{0,2},{1,3},{2,0},{3,1},{4,6},{5,7},{6,4},{7,5},{8,10},{9,11},{10,... | collective-permute-start | bytes 2359304 | tf_op jit(solution)/shard_map/ppermute | solution.py:117
  3.0 60.7 %collective-permute-start.1 = (bf16[2,12,128,128]{3,2,1,0:T(8,128)(2,1)}, bf16[2,12,128,128]{3,2,1,0:T(8,128)(2,1)S(1)}, u32[]{:S(2)}, u32[]{:S(2)}) collective-permute-start(bf16[2,12,128,128]{3,2,1,0:T(8,128)(2,1)} %refs_5_.5), channel_id=1, source_target_pairs={{0,1},{1,0},{2,3},{3,2},{4,5},{5,4},{6,7},{7,6},{8,9},{9,8},{10,11... | collective-permute-start | bytes 2359304 | tf_op jit(solution)/shard_map/ppermute | solution.py:117
  20.8 44.5 %collective-permute-start.2 = (bf16[2,12,128,128]{3,2,1,0:T(8,128)(2,1)S(1)}, bf16[2,12,128,128]{3,2,1,0:T(8,128)(2,1)S(1)}, u32[]{:S(2)}, u32[]{:S(2)}) collective-permute-start(bf16[2,12,128,128]{3,2,1,0:T(8,128)(2,1)S(1)} %collective-permute-done.refs_3_.refs_6_), channel_id=1, source_target_pairs={{0,1},{1,0},{2,3},{3,2},{4,5},{5,4},{6,7},{7,6},{8,9},{9,8},{10,11... | collective-permute-start | bytes 2359304 | tf_op jit(solution)/shard_map/ppermute | solution.py:117
  36.3 8.7 %collective-permute-start.15 = (bf16[2,2,128,128]{3,2,1,0:T(8,128)(2,1)}, bf16[2,2,128,128]{3,2,1,0:T(8,128)(2,1)}, u32[]{:S(2)}, u32[]{:S(2)}) collective-permute-start(bf16[2,2,128,128]{3,2,1,0:T(8,128)(2,1)} %get-tuple-element.12), channel_id=1, source_target_pairs={{0,12},{4,8},{8,4},{12,0},{1,13},{5,9},{9,5},{13,1},{2,14},{6,10},... | collective-permute-start | bytes 393224 | tf_op jit(solution)/shard_map/ppermute | solution.py:117
  40.3 12.2 %collective-permute-start.9 = (bf16[2,2,128,128]{3,2,1,0:T(8,128)(2,1)}, bf16[2,2,128,128]{3,2,1,0:T(8,128)(2,1)}, u32[]{:S(2)}, u32[]{:S(2)}) collective-permute-start(bf16[2,2,128,128]{3,2,1,0:T(8,128)(2,1)} %get-tuple-element.11), channel_id=1, source_target_pairs={{0,8},{4,12},{8,0},{12,4},{1,9},{5,13},{9,1},{13,5},{2,10},{6,14},... | collective-permute-start | bytes 393224 | tf_op jit(solution)/shard_map/ppermute | solution.py:117
  40.3 12.3 %all-to-all-start = ((bf16[4,2,96,128]{3,2,1,0:T(8,128)(2,1)}), bf16[4,2,96,128]{3,2,1,0:T(8,128)(2,1)S(1)}, u32[]{:S(2)}, u32[]{:S(2)}) async-start(bf16[4,2,96,128]{3,2,1,0:T(8,128)(2,1)} %get-tuple-element.9), calls=%async_computation | async-start | bytes 393216 | tf_op jit(solution)/shard_map/all_to_all | solution.py:366
  43.6 8.9 %collective-permute-start.3 = (bf16[2,2,128,128]{3,2,1,0:T(8,128)(2,1)}, bf16[2,2,128,128]{3,2,1,0:T(8,128)(2,1)S(1)}, u32[]{:S(2)}, u32[]{:S(2)}) collective-permute-start(bf16[2,2,128,128]{3,2,1,0:T(8,128)(2,1)} %get-tuple-element.10), channel_id=1, source_target_pairs={{0,4},{4,0},{8,12},{12,8},{1,5},{5,1},{9,13},{13,9},{2,6},{6,2},{1... | collective-permute-start | bytes 393224 | tf_op jit(solution)/shard_map/ppermute | solution.py:117
  45.0 10.1 %collective-permute-start.16 = (bf16[2,2,128,128]{3,2,1,0:T(8,128)(2,1)}, bf16[2,2,128,128]{3,2,1,0:T(8,128)(2,1)}, u32[]{:S(2)}, u32[]{:S(2)}) collective-permute-start(bf16[2,2,128,128]{3,2,1,0:T(8,128)(2,1)} %collective-permute-done.15.refs_0_), channel_id=1, source_target_pairs={{0,2},{1,3},{2,0},{3,1},{4,6},{5,7},{6,4},{7,5},{8,10},{9,11},{10,... | collective-permute-start | bytes 393224 | tf_op jit(solution)/shard_map/ppermute | solution.py:117
  52.4 4.4 %collective-permute-start.17 = (bf16[2,2,128,128]{3,2,1,0:T(8,128)(2,1)}, bf16[2,2,128,128]{3,2,1,0:T(8,128)(2,1)}, u32[]{:S(2)}, u32[]{:S(2)}) collective-permute-start(bf16[2,2,128,128]{3,2,1,0:T(8,128)(2,1)} %collective-permute-done.15.refs_0_), channel_id=1, source_target_pairs={{0,1},{1,0},{2,3},{3,2},{4,5},{5,4},{6,7},{7,6},{8,9},{9,8},{10,11... | collective-permute-start | bytes 393224 | tf_op jit(solution)/shard_map/ppermute | solution.py:117
  52.6 9.9 %collective-permute-start.19 = (bf16[4,2,96,128]{3,2,1,0:T(8,128)(2,1)S(1)}, bf16[4,2,96,128]{3,2,1,0:T(8,128)(2,1)}, u32[]{:S(2)}, u32[]{:S(2)}) collective-permute-start(bf16[4,2,96,128]{3,2,1,0:T(8,128)(2,1)S(1)} %all-to-all-done.refs_1_), channel_id=1, source_target_pairs={{0,12},{4,8},{8,4},{12,0},{1,13},{5,9},{9,5},{13,1},{2,14},{6,10},... | collective-permute-start | bytes 589832 | tf_op jit(solution)/shard_map/ppermute | solution.py:117
  55.2 6.9 %collective-permute-start.10 = (bf16[2,2,128,128]{3,2,1,0:T(8,128)(2,1)}, bf16[2,2,128,128]{3,2,1,0:T(8,128)(2,1)}, u32[]{:S(2)}, u32[]{:S(2)}) collective-permute-start(bf16[2,2,128,128]{3,2,1,0:T(8,128)(2,1)} %collective-permute-done.9.refs_0_), channel_id=1, source_target_pairs={{0,2},{1,3},{2,0},{3,1},{4,6},{5,7},{6,4},{7,5},{8,10},{9,11},{10,... | collective-permute-start | bytes 393224 | tf_op jit(solution)/shard_map/ppermute | solution.py:117
  56.9 6.9 %collective-permute-start.18 = (bf16[2,2,128,128]{3,2,1,0:T(8,128)(2,1)}, bf16[2,2,128,128]{3,2,1,0:T(8,128)(2,1)}, u32[]{:S(2)}, u32[]{:S(2)}) collective-permute-start(bf16[2,2,128,128]{3,2,1,0:T(8,128)(2,1)} %collective-permute-done.16.refs_1_), channel_id=1, source_target_pairs={{0,1},{1,0},{2,3},{3,2},{4,5},{5,4},{6,7},{7,6},{8,9},{9,8},{10,11... | collective-permute-start | bytes 393224 | tf_op jit(solution)/shard_map/ppermute | solution.py:117
  62.1 7.6 %collective-permute-start.11 = (bf16[2,2,128,128]{3,2,1,0:T(8,128)(2,1)}, bf16[2,2,128,128]{3,2,1,0:T(8,128)(2,1)S(1)}, u32[]{:S(2)}, u32[]{:S(2)}) collective-permute-start(bf16[2,2,128,128]{3,2,1,0:T(8,128)(2,1)} %collective-permute-done.9.refs_0_), channel_id=1, source_target_pairs={{0,1},{1,0},{2,3},{3,2},{4,5},{5,4},{6,7},{7,6},{8,9},{9,8},{10,11... | collective-permute-start | bytes 393224 | tf_op jit(solution)/shard_map/ppermute | solution.py:117
  62.5 8.4 %collective-permute-start.4 = (bf16[2,2,128,128]{3,2,1,0:T(8,128)(2,1)S(1)}, bf16[2,2,128,128]{3,2,1,0:T(8,128)(2,1)S(1)}, u32[]{:S(2)}, u32[]{:S(2)}) collective-permute-start(bf16[2,2,128,128]{3,2,1,0:T(8,128)(2,1)S(1)} %collective-permute-done.3.refs_0_), channel_id=1, source_target_pairs={{0,2},{1,3},{2,0},{3,1},{4,6},{5,7},{6,4},{7,5},{8,10},{9,11},{10,... | collective-permute-start | bytes 393224 | tf_op jit(solution)/shard_map/ppermute | solution.py:117
  63.7 18.7 %collective-permute-start.5 = (bf16[2,2,128,128]{3,2,1,0:T(8,128)(2,1)S(1)}, bf16[2,2,128,128]{3,2,1,0:T(8,128)(2,1)S(1)}, u32[]{:S(2)}, u32[]{:S(2)}) collective-permute-start(bf16[2,2,128,128]{3,2,1,0:T(8,128)(2,1)S(1)} %collective-permute-done.3.refs_0_), channel_id=1, source_target_pairs={{0,1},{1,0},{2,3},{3,2},{4,5},{5,4},{6,7},{7,6},{8,9},{9,8},{10,11... | collective-permute-start | bytes 393224 | tf_op jit(solution)/shard_map/ppermute | solution.py:117
  63.7 12.5 %collective-permute-start.13 = (bf16[4,2,96,128]{3,2,1,0:T(8,128)(2,1)S(1)}, bf16[4,2,96,128]{3,2,1,0:T(8,128)(2,1)S(1)}, u32[]{:S(2)}, u32[]{:S(2)}) collective-permute-start(bf16[4,2,96,128]{3,2,1,0:T(8,128)(2,1)S(1)} %all-to-all-done.refs_1_), channel_id=1, source_target_pairs={{0,8},{4,12},{8,0},{12,4},{1,9},{5,13},{9,1},{13,5},{2,10},{6,14},... | collective-permute-start | bytes 589832 | tf_op jit(solution)/shard_map/ppermute | solution.py:117
  65.2 13.1 %collective-permute-start.12 = (bf16[2,2,128,128]{3,2,1,0:T(8,128)(2,1)}, bf16[2,2,128,128]{3,2,1,0:T(8,128)(2,1)S(1)}, u32[]{:S(2)}, u32[]{:S(2)}) collective-permute-start(bf16[2,2,128,128]{3,2,1,0:T(8,128)(2,1)} %collective-permute-done.10.refs_1_), channel_id=1, source_target_pairs={{0,1},{1,0},{2,3},{3,2},{4,5},{5,4},{6,7},{7,6},{8,9},{9,8},{10,11... | collective-permute-start | bytes 393224 | tf_op jit(solution)/shard_map/ppermute | solution.py:117
  69.6 12.8 %collective-permute-start.7 = (bf16[4,2,96,128]{3,2,1,0:T(8,128)(2,1)S(1)}, bf16[4,2,96,128]{3,2,1,0:T(8,128)(2,1)S(1)}, u32[]{:S(2)}, u32[]{:S(2)}) collective-permute-start(bf16[4,2,96,128]{3,2,1,0:T(8,128)(2,1)S(1)} %all-to-all-done.refs_1_), channel_id=1, source_target_pairs={{0,4},{4,0},{8,12},{12,8},{1,5},{5,1},{9,13},{13,9},{2,6},{6,2},{1... | collective-permute-start | bytes 589832 | tf_op jit(solution)/shard_map/ppermute | solution.py:117
  70.9 11.6 %collective-permute-start.6 = (bf16[2,2,128,128]{3,2,1,0:T(8,128)(2,1)S(1)}, bf16[2,2,128,128]{3,2,1,0:T(8,128)(2,1)S(1)}, u32[]{:S(2)}, u32[]{:S(2)}) collective-permute-start(bf16[2,2,128,128]{3,2,1,0:T(8,128)(2,1)S(1)} %collective-permute-done.4.refs_1_), channel_id=1, source_target_pairs={{0,1},{1,0},{2,3},{3,2},{4,5},{5,4},{6,7},{7,6},{8,9},{9,8},{10,11... | collective-permute-start | bytes 393224 | tf_op jit(solution)/shard_map/ppermute | solution.py:117
  76.3 18.1 %collective-permute-start.20 = (bf16[8,2,8,128]{3,2,1,0:T(8,128)(2,1)S(1)}, bf16[8,2,8,128]{3,2,1,0:T(8,128)(2,1)S(1)}, u32[]{:S(2)}, u32[]{:S(2)}) collective-permute-start(bf16[8,2,8,128]{3,2,1,0:T(8,128)(2,1)S(1)} %products_3.1), channel_id=1, source_target_pairs={{0,12},{4,8},{8,4},{12,0},{1,13},{5,9},{9,5},{13,1},{2,14},{6,10},... | collective-permute-start | bytes 98312 | tf_op jit(solution)/shard_map/ppermute | solution.py:117
  82.3 6.6 %copy-start = (bf16[2,16,2,128,128]{4,3,2,1,0:T(8,128)(2,1)S(1)}, bf16[2,16,2,128,128]{4,3,2,1,0:T(8,128)(2,1)}, u32[]{:S(2)}) copy-start(bf16[2,16,2,128,128]{4,3,2,1,0:T(8,128)(2,1)} %param.6) | copy-start | bytes 6291460
  82.3 12.0 %collective-permute-start.14 = (bf16[8,2,8,128]{3,2,1,0:T(8,128)(2,1)S(1)}, bf16[8,2,8,128]{3,2,1,0:T(8,128)(2,1)S(1)}, u32[]{:S(2)}, u32[]{:S(2)}) collective-permute-start(bf16[8,2,8,128]{3,2,1,0:T(8,128)(2,1)S(1)} %products_2.1), channel_id=1, source_target_pairs={{0,8},{4,12},{8,0},{12,4},{1,9},{5,13},{9,1},{13,5},{2,10},{6,14},... | collective-permute-start | bytes 98312 | tf_op jit(solution)/shard_map/ppermute | solution.py:117
  86.5 8.5 %collective-permute-start.8 = (bf16[8,2,8,128]{3,2,1,0:T(8,128)(2,1)S(1)}, bf16[8,2,8,128]{3,2,1,0:T(8,128)(2,1)S(1)}, u32[]{:S(2)}, u32[]{:S(2)}) collective-permute-start(bf16[8,2,8,128]{3,2,1,0:T(8,128)(2,1)S(1)} %products_1.1), channel_id=1, source_target_pairs={{0,4},{4,0},{8,12},{12,8},{1,5},{5,1},{9,13},{13,9},{2,6},{6,2},{1... | collective-permute-start | bytes 98312 | tf_op jit(solution)/shard_map/ppermute | solution.py:117
  93.7 0.6 copy-start.1
  94.4 0.6 copy-start.5
  94.4 0.6 copy-start.6
  95.0 0.6 copy-start.7

commit v2 on v1

--- a/solution.py
+++ b/solution.py
@@ -12,6 +12,8 @@
 STATES = 16
 ROWS = 32
 SEC_DEV = 2
+NEAR = 2
+RETURNED = jnp.bfloat16
 
 
 def lookup(values_table, indices):
@@ -107,6 +109,18 @@
     return summed.astype(jnp.bfloat16)
 
 
+def after(value, *earlier):
+    return lax.optimization_barrier((value,) + earlier)[0]
+
+
+def partner_of(partner, device, n):
+    return partner[device * SEC_DEV + lax.shift_right_logical(n, 4), n & (STATES - 1)]
+
+
+def owner_of(sector):
+    return lax.shift_right_logical(sector, 1)
+
+
 ANY = pl.BlockSpec(memory_space=pl.ANY)
 VMEM = pl.BlockSpec(memory_space=pltpu.VMEM)
 SMEM = pl.BlockSpec(memory_space=pltpu.SMEM)
@@ -117,13 +131,16 @@
     return lax.ppermute(x, axis, [(i, i ^ step) for i in range(size)])
 
 
-def gather_pieces(x, axis):
-    pieces = [x]
-    bit = lax.axis_size(axis) // 2
-    while bit:
-        pieces = pieces + [exchange(piece, axis, bit) for piece in pieces]
-        bit //= 2
-    return pieces
+def exchange_both(x, step, term_step):
+    devices, terms = lax.axis_size("sec"), lax.axis_size("term")
+    if step == 0:
+        return exchange(x, "term", term_step)
+    pairs = [
+        (s * terms + t, (s ^ step) * terms + (t ^ term_step))
+        for s in range(devices)
+        for t in range(terms)
+    ]
+    return lax.ppermute(x, ("sec", "term"), pairs)
 
 
 def piece_order(size):
@@ -137,7 +154,7 @@
 
 def pack_kernel(devices, terms, partner, wave, left, *refs):
     sends = refs[: devices - 1]
-    left_out, counts, table, sems = refs[devices - 1 :]
+    keep, give, counts, table, sems = refs[devices - 1 :]
     capacity = SEC_DEV * STATES // devices
     share = capacity // terms
     me, term = lax.axis_index("sec"), lax.axis_index("term")
@@ -145,13 +162,13 @@
         counts[owner] = 0
 
     def place(n, carry):
-        owner = partner[me * SEC_DEV + n // STATES, n % STATES] // SEC_DEV
+        owner = owner_of(partner_of(partner, me, n))
         rank = counts[owner]
         counts[owner] = rank + 1
         table[owner * capacity + rank] = n
         return carry
 
-    lax.fori_loop(0, SEC_DEV * STATES, place, 0)
+    lax.fori_loop(0, SEC_DEV * STATES, place, 0, unroll=True)
     copies = []
     for step in range(1, devices):
         target = me ^ step
@@ -162,16 +179,24 @@
             )
             copy.start()
             copies.append(copy)
-    local = left.shape[1]
     group = ROWS // terms
+    first_core = (term & (NEAR - 1)) == 0
     for a in range(SEC_DEV):
-        for t in range(0, local, 2):
-            first = left[a, t].astype(jnp.float32)
-            second = left[a, t + 1].astype(jnp.float32)
-            for piece in range(terms):
-                rows = slice(piece * group, (piece + 1) * group)
-                pair = jnp.concatenate([first[rows], second[rows]], axis=0)
-                left_out[piece, a, t * group : (t + 2) * group, :] = pair.astype(jnp.bfloat16)
+        for t in range(left.shape[1]):
+            rows = left[a, t].astype(jnp.float32)
+            tiles = [
+                jnp.concatenate(
+                    [
+                        rows[(far * NEAR + near) * group : (far * NEAR + near + 1) * group]
+                        for far in range(terms // NEAR)
+                    ],
+                    axis=0,
+                )
+                for near in range(NEAR)
+            ]
+            place_rows = slice(t * 2 * group, (t + 1) * 2 * group)
+            keep[a, place_rows, :] = jnp.where(first_core, tiles[0], tiles[1]).astype(jnp.bfloat16)
+            give[a, place_rows, :] = jnp.where(first_core, tiles[1], tiles[0]).astype(jnp.bfloat16)
     for copy in copies:
         copy.wait()
 
@@ -181,12 +206,12 @@
     share = capacity // terms
     local = left.shape[1]
     piece = jax.ShapeDtypeStruct((share, 2, SECTOR, SECTOR), jnp.bfloat16)
-    rows = jax.ShapeDtypeStruct((terms, SEC_DEV, local * (ROWS // terms), SECTOR), jnp.bfloat16)
+    rows = jax.ShapeDtypeStruct((SEC_DEV, local * (ROWS // NEAR), SECTOR), jnp.bfloat16)
     outs = pl.pallas_call(
         functools.partial(pack_kernel, devices, terms),
-        out_shape=[piece] * (devices - 1) + [rows],
+        out_shape=[piece] * (devices - 1) + [rows] * 2,
         in_specs=[SMEM, ANY, VMEM],
-        out_specs=[ANY] * (devices - 1) + [VMEM],
+        out_specs=[VMEM] * (devices + 1),
         scratch_shapes=[
             pltpu.SMEM((devices,), jnp.int32),
             pltpu.SMEM((SEC_DEV * STATES,), jnp.int32),
@@ -195,30 +220,33 @@
         cost_estimate=pl.CostEstimate(flops=0, bytes_accessed=4 << 20, transcendentals=0),
         name="pack",
     )(partner, wave, left)
-    return outs[: devices - 1], outs[devices - 1]
-
-
-def compute_kernel(step, devices, terms, partner, order, coef, *refs):
+    return outs[: devices - 1], outs[devices - 1], outs[devices]
+
+
+def compute_kernel(step, devices, terms, partner, order, *refs):
+    coefs, refs = refs[:NEAR], refs[NEAR:]
     pieces = refs[: 1 if step == 0 else terms]
     refs = refs[len(pieces) :]
-    left, rights, out = refs[0], refs[1 : 1 + terms], refs[1 + terms]
-    table, partials = refs[2 + terms : 4 + terms]
+    left, rights, (keep, give) = refs[0], refs[1 : 1 + NEAR], refs[1 + NEAR : 3 + NEAR]
+    table, partials = refs[3 + NEAR : 5 + NEAR]
     capacity = SEC_DEV * STATES // devices
     share = capacity // terms
     js = piece_order(terms)
     me, term = lax.axis_index("sec"), lax.axis_index("term")
     source = me ^ step
-    local = left.shape[2] // (ROWS // terms)
+    group = ROWS // terms
+    rows = ROWS // NEAR
+    local = left.shape[2] // rows
     depth = local * SECTOR
 
     def place(n, count):
         table[count] = n
-        owner = partner[source * SEC_DEV + n // STATES, n % STATES] // SEC_DEV
+        owner = owner_of(partner_of(partner, source, n))
         return count + jnp.where(owner == me, 1, 0)
 
-    lax.fori_loop(0, SEC_DEV * STATES, place, 0)
+    lax.fori_loop(0, SEC_DEV * STATES, place, 0, unroll=True)
     if step == 0:
-        wave, (blocks, sems) = pieces[0], refs[4 + terms :]
+        wave, (blocks, sems) = pieces[0], refs[5 + NEAR :]
         copies = []
         for slot in range(capacity):
             copy = pltpu.make_async_copy(wave.at[table[slot]], blocks.at[slot], sems.at[slot])
@@ -228,7 +256,6 @@
             copy.wait()
     row_index = lax.broadcasted_iota(jnp.int32, (SECTOR, SECTOR), 0)
     col_index = lax.broadcasted_iota(jnp.int32, (SECTOR, SECTOR), 1)
-    group = ROWS // terms
 
     def slot_of(j, sub):
         return (term ^ js[j]) * share + sub
@@ -236,119 +263,132 @@
     def first(j, sub):
         slot = slot_of(j, sub)
         n = table[slot]
-        sector, state = n // STATES, n % STATES
-        left_id = source * SEC_DEV + sector
-        left_order = order[left_id]
-        right_order = order[partner[left_id, state]]
-        keep = (row_index < left_order) & (col_index < right_order)
+        sector, state = lax.shift_right_logical(n, 4), n & (STATES - 1)
+        left_order = order[source * SEC_DEV + sector]
+        right_order = order[partner_of(partner, source, n)]
+        keep_mask = (row_index < left_order) & (col_index < right_order)
         block = blocks.at[slot] if step == 0 else pieces[j].at[sub]
         vectors = [
-            jnp.where(keep, block[v].astype(jnp.float32), 0.0).astype(jnp.bfloat16)
+            jnp.where(keep_mask, block[v].astype(jnp.float32), 0.0).astype(jnp.bfloat16)
             for v in range(2)
         ]
         both = jnp.concatenate(vectors, axis=1)
-        place_row = pl.multiple_of((j * share + sub) * 2 * group, 2 * group)
-        for i in range(terms):
-            origin = term ^ js[i]
-            product = jnp.dot(left[origin, sector], both, preferred_element_type=jnp.float32)
+        place_row = (j * share + sub) * 2 * rows
+        for i in range(NEAR):
+            product = jnp.dot(left[i, sector], both, preferred_element_type=jnp.float32)
             for t in range(local):
-                rows = product[t * group : (t + 1) * group]
-                pair = jnp.concatenate([rows[:, :SECTOR], rows[:, SECTOR:]], axis=0)
-                pair = pair * coef[origin * local + t, state]
+                scaled = product[t * rows : (t + 1) * rows] * coefs[i][t, state]
                 start = (i * local + t) * SECTOR
-                partials[pl.ds(place_row, 2 * group), start : start + SECTOR] = pair.astype(
-                    jnp.bfloat16
-                )
+                for v in range(2):
+                    partials[
+                        place_row + v * rows : place_row + (v + 1) * rows, start : start + SECTOR
+                    ] = scaled[:, v * SECTOR : (v + 1) * SECTOR].astype(jnp.bfloat16)
 
     for j in range(terms):
-
-        def inner(sub, carry, j=j):
+        for sub in range(share):
             first(j, sub)
-            return carry
-
-        lax.fori_loop(0, share, inner, 0)
-
-    total = jnp.zeros((capacity * 2 * group, SEC_DEV * SECTOR), jnp.float32)
-    for i in range(terms):
+
+    total = jnp.zeros((capacity * 2 * rows, SEC_DEV * SECTOR), jnp.float32)
+    for i in range(NEAR):
         right = [rights[i][p].reshape(depth, SECTOR) for p in range(SEC_DEV)]
         total = total + jnp.dot(
             partials[:, i * depth : (i + 1) * depth],
             jnp.concatenate(right, axis=1),
             preferred_element_type=jnp.float32,
         )
-    column = lax.broadcasted_iota(jnp.int32, (2 * group, SECTOR), 1)
+    column = lax.broadcasted_iota(jnp.int32, (2 * rows, SECTOR), 1)
+    near_first = term < NEAR
     for j in range(terms):
         for sub in range(share):
             slot = slot_of(j, sub)
             n = table[slot]
-            right_id = partner[source * SEC_DEV + n // STATES, n % STATES]
-            start = (j * share + sub) * 2 * group
-            mine = total[start : start + 2 * group]
+            right_id = partner_of(partner, source, n)
+            start = (j * share + sub) * 2 * rows
+            mine = total[start : start + 2 * rows]
             result = mine[:, :SECTOR]
             for p in range(1, SEC_DEV):
                 result = jnp.where(
-                    right_id % SEC_DEV == p, mine[:, p * SECTOR : (p + 1) * SECTOR], result
+                    (right_id & (SEC_DEV - 1)) == p, mine[:, p * SECTOR : (p + 1) * SECTOR], result
                 )
             result = jnp.where(column < order[right_id], result, 0.0)
             for v in range(2):
-                out[slot, v] = result[v * group : (v + 1) * group].astype(jnp.bfloat16)
-
-
-def compute(step, pieces, left, rights, coef, order, partner, devices, terms):
+                low = result[v * rows : v * rows + group]
+                high = result[v * rows + group : (v + 1) * rows]
+                keep[slot, v] = jnp.where(near_first, low, high).astype(keep.dtype)
+                give[slot, v] = jnp.where(near_first, high, low).astype(give.dtype)
+
+
+def compute(step, pieces, left, rights, coefs, order, partner, devices, terms):
     capacity = SEC_DEV * STATES // devices
-    group = ROWS // terms
-    local = left.shape[2] // group
+    rows = ROWS // NEAR
+    local = left.shape[2] // rows
     scratch = [
         pltpu.SMEM((SEC_DEV * STATES + 1,), jnp.int32),
-        pltpu.VMEM((capacity * 2 * group, terms * local * SECTOR), jnp.bfloat16),
+        pltpu.VMEM((capacity * 2 * rows, NEAR * local * SECTOR), jnp.bfloat16),
     ]
     if step == 0:
         scratch += [
             pltpu.VMEM((capacity, 2, SECTOR, SECTOR), jnp.bfloat16),
             pltpu.SemaphoreType.DMA((capacity,)),
         ]
+    part = jax.ShapeDtypeStruct((capacity, 2, ROWS // terms, SECTOR), RETURNED)
     return pl.pallas_call(
         functools.partial(compute_kernel, step, devices, terms),
-        out_shape=jax.ShapeDtypeStruct((capacity, 2, group, SECTOR), jnp.bfloat16),
-        in_specs=[SMEM] * 3 + [ANY if step == 0 else VMEM] * len(pieces) + [VMEM] * (1 + terms),
-        out_specs=VMEM,
+        out_shape=[part, part],
+        in_specs=[SMEM] * (2 + NEAR)
+        + [ANY if step == 0 else VMEM] * len(pieces)
+        + [VMEM] * (1 + NEAR),
+        out_specs=[VMEM, VMEM],
         scratch_shapes=scratch,
         compiler_params=pltpu.CompilerParams(vmem_limit_bytes=32 << 20),
         cost_estimate=pl.CostEstimate(
             flops=3 << 30, bytes_accessed=4 << 20, transcendentals=0
         ),
         name=f"products_{step}",
-    )(partner, order, coef, *pieces, left, *rights)
+    )(partner, order, *coefs, *pieces, left, *rights)
 
 
 def unpack_kernel(devices, partner, *refs):
-    chunks, out, counts = refs[:devices], refs[devices], refs[devices + 1]
+    chunks, (out, held, counts, table, sems) = refs[: 2 * devices], refs[2 * devices :]
+    capacity = SEC_DEV * STATES // devices
     me = lax.axis_index("sec")
+    copies = []
+    for i in range(2 * devices):
+        copy = pltpu.make_async_copy(chunks[i], held.at[i], sems.at[i])
+        copy.start()
+        copies.append(copy)
     for owner in range(devices):
         counts[owner] = 0
 
     def place(n, carry):
-        owner = partner[me * SEC_DEV + n // STATES, n % STATES] // SEC_DEV
+        owner = owner_of(partner_of(partner, me, n))
         rank = counts[owner]
         counts[owner] = rank + 1
-        for step in range(devices):
-
-            @pl.when((me ^ step) == owner)
-            def _():
-                out[n] = chunks[step][rank]
-
+        table[owner * capacity + rank] = n
         return carry
 
-    lax.fori_loop(0, SEC_DEV * STATES, place, 0)
+    lax.fori_loop(0, SEC_DEV * STATES, place, 0, unroll=True)
+    for copy in copies:
+        copy.wait()
+    for step in range(devices):
+        for rank in range(capacity):
+            near = held[2 * step, rank].astype(jnp.float32)
+            far = held[2 * step + 1, rank].astype(jnp.float32)
+            out[table[(me ^ step) * capacity + rank]] = (near + far).astype(jnp.bfloat16)
 
 
 def unpack(chunks, partner, devices):
     return pl.pallas_call(
         functools.partial(unpack_kernel, devices),
         out_shape=jax.ShapeDtypeStruct((SEC_DEV * STATES,) + chunks[0].shape[1:], jnp.bfloat16),
-        in_specs=[SMEM] + [VMEM] * devices,
+        in_specs=[SMEM] + [ANY] * (2 * devices),
         out_specs=VMEM,
-        scratch_shapes=[pltpu.SMEM((devices,), jnp.int32)],
+        scratch_shapes=[
+            pltpu.VMEM((2 * devices,) + chunks[0].shape, RETURNED),
+            pltpu.SMEM((devices,), jnp.int32),
+            pltpu.SMEM((SEC_DEV * STATES,), jnp.int32),
+            pltpu.SemaphoreType.DMA((2 * devices,)),
+        ],
         cost_estimate=pl.CostEstimate(flops=0, bytes_accessed=1 << 20, transcendentals=0),
         name="unpack",
     )(partner, *chunks)
@@ -359,22 +399,38 @@
     block_count = SEC_DEV * STATES
     wave = wavefunction.reshape(block_count, 2, SECTOR, SECTOR)
     steps = list(range(devices - 1, 0, -1))
-    coef = lax.all_gather(couplings, "term", axis=0, tiled=True)
-    rights = gather_pieces(right_blocks, "term")
-    sends, left_cut = pack(wave, left_window, partner, devices, terms)
+    sends, left_keep, left_give = pack(wave, left_window, partner, devices, terms)
+    coefs = [couplings, exchange(couplings, "term", 1)]
+    rights = [right_blocks, exchange(right_blocks, "term", 1)]
+    left_all = jnp.stack([left_keep, exchange(left_give, "term", 1)])
     arrived = {step: exchange(sends[step - 1], "sec", step) for step in steps}
-    left_all = lax.all_to_all(left_cut, "term", split_axis=0, concat_axis=0, tiled=True)
     lefts = {step: exchange(left_all, "sec", step) for step in steps}
     lefts[0] = left_all
-    vectors = {step: gather_pieces(arrived[step], "term") for step in steps}
-    vectors[0] = [wave]
-    results = {
-        step: compute(
-            step, vectors[step], lefts[step], rights, coef, sector_order, partner, devices, terms
+    vectors = {0: [wave]}
+    for step in steps:
+        x = exchange(arrived[step], "term", NEAR)
+        both = jnp.concatenate([arrived[step], x])
+        both = jnp.concatenate([both, exchange(both, "term", 1)])
+        vectors[step] = jnp.split(both, terms)
+    chunks = {}
+    waits = []
+    for step in [0] + steps:
+        keep, give = compute(
+            step,
+            vectors[step],
+            after(lefts[step], *waits),
+            rights,
+            coefs,
+            sector_order,
+            partner,
+            devices,
+            terms,
         )
-        for step in [0] + steps
-    }
-    chunks = [results[0]] + [exchange(results[step], "sec", step) for step in range(1, devices)]
+        waits = [keep] + [part for value in list(chunks.values())[-1:] for part in value]
+        if step:
+            keep = exchange(keep, "sec", step)
+        chunks[step] = (keep, exchange_both(give, step, NEAR))
+    chunks = [part for step in range(devices) for part in chunks[step]]
     out = unpack(chunks, partner, devices)
     return out.reshape(SEC_DEV, STATES, 2, ROWS // terms, SECTOR)
 
@@ -396,7 +452,7 @@
     devices, terms = mesh.shape["sec"], mesh.shape["term"]
     paired = (
         power_of_two(devices)
-        and power_of_two(terms)
+        and terms == 2 * NEAR
         and devices <= 8
         and SEC_DEV * STATES % (devices * terms) == 0
         and ROWS == 8 * terms

time: 98.9 us -> 65.9 us (0.67)
  Pallas kernels: 35.7 us -> 14.1 us
  waiting for transfers between devices: 29.7 us -> 21.7 us
  blocking collectives: 5.19 us -> 0 us
  starting transfers between devices: 26 us -> 27.8 us
  local copies, waits for them, and re-layouts: 1.86 us -> 0.71 us
  other arithmetic: 0 us -> 0.99 us
    ppermute x21 -> x19, waiting for transfers between devices: 29.7 us -> 17.1 us  [exchange(): return lax.ppermute(x, axis, [(i, i ^ step) for i in range(size)])]
    pallas_call x1, Pallas kernels: 15.6 us -> 3.02 us  [pack(): pl.pallas_call(functools.partial(pack_kernel, devices, terms), out_shape=...]
    pallas_call x4, Pallas kernels: 17.1 us -> 8.76 us  [compute(): pl.pallas_call(functools.partial(compute_kernel, step, devices, terms), o...]
    all_gather x1 -> x0, blocking collectives: 5.19 us -> none  [paired_body(): coef = lax.all_gather(couplings, 'term', axis=0, tiled=True)]
    ppermute x0 -> x3, starting transfers between devices: none -> 4.85 us  [exchange_both(): return lax.ppermute(x, ('sec', 'term'), pairs)]
    ppermute x0 -> x3, waiting for transfers between devices: none -> 4.6 us  [exchange_both(): return lax.ppermute(x, ('sec', 'term'), pairs)]
    all_to_all x1 -> x0, starting transfers between devices: 3.36 us -> none  [paired_body(): lax.all_to_all(left_cut, 'term', split_axis=0, concat_axis=0, tiled=True)]
    unnamed x19 -> x26, local copies, waits for them, and re-layouts: 1.86 us -> 0.66 us
  transfers between devices with their start and end apart: 22 -> 22, of which waited for: 5 -> 7; matrix products, arithmetic and copies ran while one was open for 0% -> 2% of each run, Pallas kernels for 33% -> 13%
where the time goes in v2:
time: 65.9 us; the launch traced here: 65.6 us
  starting transfers between devices  27.8 us (42%)
  waiting for transfers between devices  21.7 us (33%)
  Pallas kernels  14.1 us (21%)
  other arithmetic  0.99 us (2%)
  local copies, waits for them, and re-layouts  0.71 us (1%)
    ppermute x19, starting transfers between devices, exchange(): return lax.ppermute(x, axis, [(i, i ^ step) for i in range(size)])  22.9 us
    ppermute x19, waiting for transfers between devices, exchange(): return lax.ppermute(x, axis, [(i, i ^ step) for i in range(size)])  17.1 us
    pallas_call x4, Pallas kernels, compute(): pl.pallas_call(functools.partial(compute_kernel, step, devices, terms), o...  8.76 us
    ppermute x3, starting transfers between devices, exchange_both(): return lax.ppermute(x, ('sec', 'term'), pairs)  4.85 us
    ppermute x3, waiting for transfers between devices, exchange_both(): return lax.ppermute(x, ('sec', 'term'), pairs)  4.6 us
    pallas_call x1, Pallas kernels, pack(): pl.pallas_call(functools.partial(pack_kernel, devices, terms), out_shape=...  3.02 us
    pallas_call x1, Pallas kernels, unpack(): pl.pallas_call(functools.partial(unpack_kernel, devices), out_shape=jax.S...  2.35 us
  transfers between devices with their start and end apart: 22, of which 7 were waited for; matrix products, arithmetic and copies ran while one was open for 2% of the time, Pallas kernels for 13%

profile of v2, /device:TPU:0, one launch (start us, length us, event | category | flops | bytes accessed | tf_op | source)
XLA Modules:
  0.0 65.6 jit_solution(1242011344098816663)
XLA Ops:
  0.0 3.0 %pack.1 = (bf16[2,2,128,128]{3,2,1,0:T(8,128)(2,1)}, bf16[2,2,128,128]{3,2,1,0:T(8,128)(2,1)}, bf16[2,2,128,128]{3,2,1,0:T(8,128)(2,1)}, bf16[2,192,128]{2,1,0:T(8,128)(2,1)}, bf16[2,192,128]{2,1,0:T(8,128)(2,1)}) custom-call(s32[8,16]{1,0:T(8,128)} %partner.11, bf16[32,2,128,128]{3,2,1,0:T(8,128)(2,1)} %bitcast.4, bf16[2,12,32,128]{3,2,1,0:T(8,128)(2,1)} %left.1), custom_call_target="tpu_custom_call" | custom-call | bytes 4194304 | tf_op jit(solution)/shard_map/pack/pallas_call | solution.py:210
  3.0 0.0 copy-start
  3.0 0.0 copy-start.2
  3.1 0.0 copy-start.5
  3.1 5.1 %collective-permute-start.12 = (bf16[2,2,128,128]{3,2,1,0:T(8,128)(2,1)}, bf16[2,2,128,128]{3,2,1,0:T(8,128)(2,1)S(1)}, u32[]{:S(2)}, u32[]{:S(2)}) collective-permute-start(bf16[2,2,128,128]{3,2,1,0:T(8,128)(2,1)} %get-tuple-element.27), channel_id=1, source_target_pairs={{0,12},{4,8},{8,4},{12,0},{1,13},{5,9},{9,5},{13,1},{2,14},{6,10},... | collective-permute-start | bytes 393224 | tf_op jit(solution)/shard_map/ppermute | solution.py:131
  8.2 0.0 collective-permute-start.8
  8.2 0.6 collective-permute-start.4
  8.8 4.0 %collective-permute-done.12.refs_2_ = bf16[2,2,128,128]{3,2,1,0:T(8,128)(2,1)S(1)} collective-permute-done((bf16[2,2,128,128]{3,2,1,0:T(8,128)(2,1)}, bf16[2,2,128,128]{3,2,1,0:T(8,128)(2,1)S(1)}, u32[]{:S(2)}, u32[]{:S(2)}) %collective-permute-start.12) | collective-permute-done | bytes 131104 | tf_op jit(solution)/shard_map/ppermute | solution.py:131
  12.8 1.7 %collective-permute-start.13 = (bf16[2,2,128,128]{3,2,1,0:T(8,128)(2,1)S(1)}, bf16[2,2,128,128]{3,2,1,0:T(8,128)(2,1)S(1)}, u32[]{:S(2)}, u32[]{:S(2)}) collective-permute-start(bf16[2,2,128,128]{3,2,1,0:T(8,128)(2,1)S(1)} %collective-permute-done.12.refs_2_), channel_id=1, source_target_pairs={{0,2},{1,3},{2,0},{3,1},{4,6},{5,7},{6,4},{7,5},{8,10},{9,11},{10,... | collective-permute-start | bytes 393224 | tf_op jit(solution)/shard_map/ppermute | solution.py:131
  14.5 0.0 collective-permute-start.1
  14.5 0.5 collective-permute-start.2
  15.0 4.4 %collective-permute-done.8.refs_2_ = bf16[2,2,128,128]{3,2,1,0:T(8,128)(2,1)S(1)} collective-permute-done((bf16[2,2,128,128]{3,2,1,0:T(8,128)(2,1)}, bf16[2,2,128,128]{3,2,1,0:T(8,128)(2,1)S(1)}, u32[]{:S(2)}, u32[]{:S(2)}) %collective-permute-start.8) | collective-permute-done | bytes 131104 | tf_op jit(solution)/shard_map/ppermute | solution.py:131
  19.5 0.0 collective-permute-start
  19.5 0.0 collective-permute-done.4.refs_2_
  19.5 1.6 %collective-permute-start.9 = (bf16[2,2,128,128]{3,2,1,0:T(8,128)(2,1)S(1)}, bf16[2,2,128,128]{3,2,1,0:T(8,128)(2,1)S(1)}, u32[]{:S(2)}, u32[]{:S(2)}) collective-permute-start(bf16[2,2,128,128]{3,2,1,0:T(8,128)(2,1)S(1)} %collective-permute-done.8.refs_2_), channel_id=1, source_target_pairs={{0,2},{1,3},{2,0},{3,1},{4,6},{5,7},{6,4},{7,5},{8,10},{9,11},{10,... | collective-permute-start | bytes 393224 | tf_op jit(solution)/shard_map/ppermute | solution.py:131
  21.0 0.0 collective-permute-done.13.refs_3_
  21.0 0.5 collective-permute-start.5
  21.6 0.0 collective-permute-done.1
  21.6 0.1 collective-permute-start.14
  21.7 0.9 %pad_maximum_fusion.3.refs_3_ = bf16[2,2,192,128]{3,2,1,0:T(8,128)(2,1)S(1)} fusion(bf16[1,2,192,128]{3,2,1,0:T(8,128)(2,1)S(1)} %bitcast.7, bf16[1,2,192,128]{3,2,1,0:T(8,128)(2,1)} %bitcast.6), kind=kLoop, calls=%fused_computation.3 | loop fusion | flops 98304 | bytes 393216 | tf_op jit(solution)/shard_map/stack | solution.py:405
  22.6 3.2 %collective-permute-done.9.refs_3_ = bf16[2,2,128,128]{3,2,1,0:T(8,128)(2,1)S(1)} collective-permute-done((bf16[2,2,128,128]{3,2,1,0:T(8,128)(2,1)S(1)}, bf16[2,2,128,128]{3,2,1,0:T(8,128)(2,1)S(1)}, u32[]{:S(2)}, u32[]{:S(2)}) %collective-permute-start.9) | collective-permute-done | bytes 131104 | tf_op jit(solution)/shard_map/ppermute | solution.py:131
  25.9 2.5 %collective-permute-start.15 = (bf16[2,2,192,128]{3,2,1,0:T(8,128)(2,1)S(1)}, bf16[2,2,192,128]{3,2,1,0:T(8,128)(2,1)S(1)}, u32[]{:S(2)}, u32[]{:S(2)}) collective-permute-start(bf16[2,2,192,128]{3,2,1,0:T(8,128)(2,1)S(1)} %pad_maximum_fusion.3.refs_3_), channel_id=1, source_target_pairs={{0,12},{4,8},{8,4},{12,0},{1,13},{5,9},{9,5},{13,1},{2,14},{6,10},... | collective-permute-start | bytes 589832 | tf_op jit(solution)/shard_map/ppermute | solution.py:131
  28.4 0.1 collective-permute-start.10
  28.5 0.6 collective-permute-start.6
  29.1 0.9 %collective-permute-done.10 = bf16[4,2,128,128]{3,2,1,0:T(8,128)(2,1)S(1)} collective-permute-done((bf16[4,2,128,128]{3,2,1,0:T(8,128)(2,1)S(1)}, bf16[4,2,128,128]{3,2,1,0:T(8,128)(2,1)S(1)}, u32[]{:S(2)}, u32[]{:S(2)}) %collective-permute-start.10) | collective-permute-done | bytes 262176 | tf_op jit(solution)/shard_map/ppermute | solution.py:131
  30.0 1.7 %collective-permute-start.11 = (bf16[2,2,192,128]{3,2,1,0:T(8,128)(2,1)S(1)}, bf16[2,2,192,128]{3,2,1,0:T(8,128)(2,1)S(1)}, u32[]{:S(2)}, u32[]{:S(2)}) collective-permute-start(bf16[2,2,192,128]{3,2,1,0:T(8,128)(2,1)S(1)} %pad_maximum_fusion.3.refs_3_), channel_id=1, source_target_pairs={{0,8},{4,12},{8,0},{12,4},{1,9},{5,13},{9,1},{13,5},{2,10},{6,14},... | collective-permute-start | bytes 589832 | tf_op jit(solution)/shard_map/ppermute | solution.py:131
  31.7 1.2 %collective-permute-start.7 = (bf16[2,2,192,128]{3,2,1,0:T(8,128)(2,1)S(1)}, bf16[2,2,192,128]{3,2,1,0:T(8,128)(2,1)S(1)}, u32[]{:S(2)}, u32[]{:S(2)}) collective-permute-start(bf16[2,2,192,128]{3,2,1,0:T(8,128)(2,1)S(1)} %pad_maximum_fusion.3.refs_3_), channel_id=1, source_target_pairs={{0,4},{4,0},{8,12},{12,8},{1,5},{5,1},{9,13},{13,9},{2,6},{6,2},{1... | collective-permute-start | bytes 589832 | tf_op jit(solution)/shard_map/ppermute | solution.py:131
  33.0 2.8 %products_0.1 = (bf16[8,2,8,128]{3,2,1,0:T(8,128)(2,1)S(1)}, bf16[8,2,8,128]{3,2,1,0:T(8,128)(2,1)S(1)}) custom-call(s32[8,16]{1,0:T(8,128)S(1)} %copy-done.2, s32[8]{0:T(128)S(1)} %copy-done.5, f32[12,16]{1,0:T(8,128)S(1)} %copy-done.4, f32[12,16]{1,0:T(8,128)S(1)} %collective-permute-done.refs_1_, bf16[32,2,128,128]{3,2,1,0:T(8,128)(2,1)S(1)} %bitcast.5, ...), custom_call_target="tpu_custom_call" | custom-call | flops 3221225472 | bytes 4194304 | tf_op jit(solution)/shard_map/products_0/pallas_call | solution.py:335
  35.8 1.6 %collective-permute-start.3 = (bf16[8,2,8,128]{3,2,1,0:T(8,128)(2,1)S(1)}, bf16[8,2,8,128]{3,2,1,0:T(8,128)(2,1)S(1)}, u32[]{:S(2)}, u32[]{:S(2)}) collective-permute-start(bf16[8,2,8,128]{3,2,1,0:T(8,128)(2,1)S(1)} %get-tuple-element.24), channel_id=1, source_target_pairs={{0,2},{1,3},{2,0},{3,1},{4,6},{5,7},{6,4},{7,5},{8,10},{9,11},{10,... | collective-permute-start | bytes 98312 | tf_op jit(solution)/shard_map/ppermute | solution.py:131
  37.3 2.0 %products_3.1 = (bf16[8,2,8,128]{3,2,1,0:T(8,128)(2,1)S(1)}, bf16[8,2,8,128]{3,2,1,0:T(8,128)(2,1)S(1)}) custom-call(s32[8,16]{1,0:T(8,128)S(1)} %copy-done.2, s32[8]{0:T(128)S(1)} %copy-done.5, f32[12,16]{1,0:T(8,128)S(1)} %copy-done.4, f32[12,16]{1,0:T(8,128)S(1)} %collective-permute-done.refs_1_, ...), custom_call_target="tpu_custom_call" | custom-call | flops 3221225472 | bytes 4194304 | tf_op jit(solution)/shard_map/products_3/pallas_call | solution.py:335
  39.3 1.6 %collective-permute-start.16 = (bf16[8,2,8,128]{3,2,1,0:T(8,128)(2,1)S(1)}, bf16[8,2,8,128]{3,2,1,0:T(8,128)(2,1)S(1)}, u32[]{:S(2)}, u32[]{:S(2)}) collective-permute-start(bf16[8,2,8,128]{3,2,1,0:T(8,128)(2,1)S(1)} %get-tuple-element.29), channel_id=1, source_target_pairs={{0,12},{4,8},{8,4},{12,0},{1,13},{5,9},{9,5},{13,1},{2,14},{6,10},... | collective-permute-start | bytes 98312 | tf_op jit(solution)/shard_map/ppermute | solution.py:131
  41.0 2.2 %collective-permute-start.17 = (bf16[8,2,8,128]{3,2,1,0:T(8,128)(2,1)S(1)}, bf16[8,2,8,128]{3,2,1,0:T(8,128)(2,1)S(1)}, u32[]{:S(2)}, u32[]{:S(2)}) collective-permute-start(bf16[8,2,8,128]{3,2,1,0:T(8,128)(2,1)S(1)} %get-tuple-element.32), channel_id=1, source_target_pairs={{0,14},{1,15},{2,12},{3,13},{4,10},{5,11},{6,8},{7,9},{8,6},{9,7},... | collective-permute-start | bytes 98312 | tf_op jit(solution)/shard_map/ppermute | solution.py:143
  43.2 4.5 %collective-permute-done.11.refs_6_ = bf16[2,2,192,128]{3,2,1,0:T(8,128)(2,1)S(1)} collective-permute-done((bf16[2,2,192,128]{3,2,1,0:T(8,128)(2,1)S(1)}, bf16[2,2,192,128]{3,2,1,0:T(8,128)(2,1)S(1)}, u32[]{:S(2)}, u32[]{:S(2)}) %collective-permute-start.11) | collective-permute-done | bytes 196640 | tf_op jit(solution)/shard_map/ppermute | solution.py:131
  47.7 2.0 %products_2.1 = (bf16[8,2,8,128]{3,2,1,0:T(8,128)(2,1)S(1)}, bf16[8,2,8,128]{3,2,1,0:T(8,128)(2,1)S(1)}) custom-call(s32[8,16]{1,0:T(8,128)S(1)} %copy-done.2, s32[8]{0:T(128)S(1)} %copy-done.5, f32[12,16]{1,0:T(8,128)S(1)} %copy-done.4, f32[12,16]{1,0:T(8,128)S(1)} %collective-permute-done.refs_1_, ...), custom_call_target="tpu_custom_call" | custom-call | flops 3221225472 | bytes 4194304 | tf_op jit(solution)/shard_map/products_2/pallas_call | solution.py:335
  49.7 1.7 %collective-permute-start.20 = (bf16[8,2,8,128]{3,2,1,0:T(8,128)(2,1)S(1)}, bf16[8,2,8,128]{3,2,1,0:T(8,128)(2,1)S(1)}, u32[]{:S(2)}, u32[]{:S(2)}) collective-permute-start(bf16[8,2,8,128]{3,2,1,0:T(8,128)(2,1)S(1)} %get-tuple-element.31), channel_id=1, source_target_pairs={{0,8},{4,12},{8,0},{12,4},{1,9},{5,13},{9,1},{13,5},{2,10},{6,14},... | collective-permute-start | bytes 98312 | tf_op jit(solution)/shard_map/ppermute | solution.py:131
  51.4 0.0 collective-permute-done.7.refs_6_
  51.4 0.0 collective-permute-done.16.refs_6_
  51.4 0.0 collective-permute-done.17.refs_7_
  51.4 2.0 %products_1.1 = (bf16[8,2,8,128]{3,2,1,0:T(8,128)(2,1)S(1)}, bf16[8,2,8,128]{3,2,1,0:T(8,128)(2,1)S(1)}) custom-call(s32[8,16]{1,0:T(8,128)S(1)} %copy-done.2, s32[8]{0:T(128)S(1)} %copy-done.5, f32[12,16]{1,0:T(8,128)S(1)} %copy-done.4, f32[12,16]{1,0:T(8,128)S(1)} %collective-permute-done.refs_1_, ...), custom_call_target="tpu_custom_call" | custom-call | flops 3221225472 | bytes 4194304 | tf_op jit(solution)/shard_map/products_1/pallas_call | solution.py:335
  53.5 1.9 %collective-permute-start.18 = (bf16[8,2,8,128]{3,2,1,0:T(8,128)(2,1)S(1)}, bf16[8,2,8,128]{3,2,1,0:T(8,128)(2,1)S(1)}, u32[]{:S(2)}, u32[]{:S(2)}) collective-permute-start(bf16[8,2,8,128]{3,2,1,0:T(8,128)(2,1)S(1)} %get-tuple-element.34), channel_id=1, source_target_pairs={{0,4},{4,0},{8,12},{12,8},{1,5},{5,1},{9,13},{13,9},{2,6},{6,2},{1... | collective-permute-start | bytes 98312 | tf_op jit(solution)/shard_map/ppermute | solution.py:131
  55.4 1.5 %collective-permute-start.19 = (bf16[8,2,8,128]{3,2,1,0:T(8,128)(2,1)S(1)}, bf16[8,2,8,128]{3,2,1,0:T(8,128)(2,1)S(1)}, u32[]{:S(2)}, u32[]{:S(2)}) collective-permute-start(bf16[8,2,8,128]{3,2,1,0:T(8,128)(2,1)S(1)} %get-tuple-element.35), channel_id=1, source_target_pairs={{0,6},{1,7},{2,4},{3,5},{4,2},{5,3},{6,0},{7,1},{8,14},{9,15},{10,... | collective-permute-start | bytes 98312 | tf_op jit(solution)/shard_map/ppermute | solution.py:143
  56.9 1.1 %collective-permute-start.21 = (bf16[8,2,8,128]{3,2,1,0:T(8,128)(2,1)S(1)}, bf16[8,2,8,128]{3,2,1,0:T(8,128)(2,1)S(1)}, u32[]{:S(2)}, u32[]{:S(2)}) collective-permute-start(bf16[8,2,8,128]{3,2,1,0:T(8,128)(2,1)S(1)} %get-tuple-element.36), channel_id=1, source_target_pairs={{0,10},{1,11},{2,8},{3,9},{4,14},{5,15},{6,12},{7,13},{8,2},{9,3},... | collective-permute-start | bytes 98312 | tf_op jit(solution)/shard_map/ppermute | solution.py:143
  58.0 0.0 collective-permute-done.18.refs_2_
  58.0 2.2 %collective-permute-done.19.refs_3_ = bf16[8,2,8,128]{3,2,1,0:T(8,128)(2,1)S(1)} collective-permute-done((bf16[8,2,8,128]{3,2,1,0:T(8,128)(2,1)S(1)}, bf16[8,2,8,128]{3,2,1,0:T(8,128)(2,1)S(1)}, u32[]{:S(2)}, u32[]{:S(2)}) %collective-permute-start.19) | collective-permute-done | bytes 32800 | tf_op jit(solution)/shard_map/ppermute | solution.py:143
  60.2 0.0 collective-permute-done.20.refs_4_
  60.2 2.4 %collective-permute-done.21.refs_5_ = bf16[8,2,8,128]{3,2,1,0:T(8,128)(2,1)S(1)} collective-permute-done((bf16[8,2,8,128]{3,2,1,0:T(8,128)(2,1)S(1)}, bf16[8,2,8,128]{3,2,1,0:T(8,128)(2,1)S(1)}, u32[]{:S(2)}, u32[]{:S(2)}) %collective-permute-start.21) | collective-permute-done | bytes 32800 | tf_op jit(solution)/shard_map/ppermute | solution.py:143
  62.6 0.6 copy-done.12
  63.2 2.4 %unpack.1 = bf16[32,2,8,128]{3,2,1,0:T(8,128)(2,1)} custom-call(s32[8,16]{1,0:T(8,128)} %partner.11, bf16[8,2,8,128]{3,2,1,0:T(8,128)(2,1)} %copy-done.1, bf16[8,2,8,128]{3,2,1,0:T(8,128)(2,1)} %copy-done.6, bf16[8,2,8,128]{3,2,1,0:T(8,128)(2,1)} %copy-done.10, bf16[8,2,8,128]{3,2,1,0:T(8,128)(2,1)} %copy-done.11, bf16[8,2,8,128]{3,2,1,0:T(8,128)(2,1)} %copy-done.9, ...), custom_call_target="tpu_custom_call" | custom-call | bytes 1048576 | tf_op jit(solution)/shard_map/unpack/pallas_call | solution.py:381
  (35 shorter events, 0.2 us)
Async XLA Ops:
  0.0 14.5 %copy-start.3 = (bf16[2,12,128,128]{3,2,1,0:T(8,128)(2,1)S(1)}, bf16[2,12,128,128]{3,2,1,0:T(8,128)(2,1)}, u32[]{:S(2)}) copy-start(bf16[2,12,128,128]{3,2,1,0:T(8,128)(2,1)} %refs_7_.5) | copy-start | bytes 2359300
  0.0 19.5 %copy-start.4 = (f32[12,16]{1,0:T(8,128)S(1)}, f32[12,16]{1,0:T(8,128)}, u32[]{:S(2)}) copy-start(f32[12,16]{1,0:T(8,128)} %refs_0_.7) | copy-start | bytes 2308
  3.0 29.9 %copy-start = (bf16[2,16,2,128,128]{4,3,2,1,0:T(8,128)(2,1)S(1)}, bf16[2,16,2,128,128]{4,3,2,1,0:T(8,128)(2,1)}, u32[]{:S(2)}) copy-start(bf16[2,16,2,128,128]{4,3,2,1,0:T(8,128)(2,1)} %param.6) | copy-start | bytes 6291460
  3.0 29.9 %copy-start.2 = (s32[8,16]{1,0:T(8,128)S(1)}, s32[8,16]{1,0:T(8,128)}, u32[]{:S(2)}) copy-start(s32[8,16]{1,0:T(8,128)} %partner.11) | copy-start | bytes 1540
  3.1 29.9 %copy-start.5 = (s32[8]{0:T(128)S(1)}, s32[8]{0:T(128)}, u32[]{:S(2)}) copy-start(s32[8]{0:T(128)} %order.7) | copy-start | bytes 100
  3.1 9.8 %collective-permute-start.12 = (bf16[2,2,128,128]{3,2,1,0:T(8,128)(2,1)}, bf16[2,2,128,128]{3,2,1,0:T(8,128)(2,1)S(1)}, u32[]{:S(2)}, u32[]{:S(2)}) collective-permute-start(bf16[2,2,128,128]{3,2,1,0:T(8,128)(2,1)} %get-tuple-element.27), channel_id=1, source_target_pairs={{0,12},{4,8},{8,4},{12,0},{1,13},{5,9},{9,5},{13,1},{2,14},{6,10},... | collective-permute-start | bytes 393224 | tf_op jit(solution)/shard_map/ppermute | solution.py:131
  8.2 11.3 %collective-permute-start.8 = (bf16[2,2,128,128]{3,2,1,0:T(8,128)(2,1)}, bf16[2,2,128,128]{3,2,1,0:T(8,128)(2,1)S(1)}, u32[]{:S(2)}, u32[]{:S(2)}) collective-permute-start(bf16[2,2,128,128]{3,2,1,0:T(8,128)(2,1)} %get-tuple-element.26), channel_id=1, source_target_pairs={{0,8},{4,12},{8,0},{12,4},{1,9},{5,13},{9,1},{13,5},{2,10},{6,14},... | collective-permute-start | bytes 393224 | tf_op jit(solution)/shard_map/ppermute | solution.py:131
  8.2 11.3 %collective-permute-start.4 = (bf16[2,2,128,128]{3,2,1,0:T(8,128)(2,1)}, bf16[2,2,128,128]{3,2,1,0:T(8,128)(2,1)S(1)}, u32[]{:S(2)}, u32[]{:S(2)}) collective-permute-start(bf16[2,2,128,128]{3,2,1,0:T(8,128)(2,1)} %get-tuple-element.25), channel_id=1, source_target_pairs={{0,4},{4,0},{8,12},{12,8},{1,5},{5,1},{9,13},{13,9},{2,6},{6,2},{1... | collective-permute-start | bytes 393224 | tf_op jit(solution)/shard_map/ppermute | solution.py:131
  12.8 8.2 %collective-permute-start.13 = (bf16[2,2,128,128]{3,2,1,0:T(8,128)(2,1)S(1)}, bf16[2,2,128,128]{3,2,1,0:T(8,128)(2,1)S(1)}, u32[]{:S(2)}, u32[]{:S(2)}) collective-permute-start(bf16[2,2,128,128]{3,2,1,0:T(8,128)(2,1)S(1)} %collective-permute-done.12.refs_2_), channel_id=1, source_target_pairs={{0,2},{1,3},{2,0},{3,1},{4,6},{5,7},{6,4},{7,5},{8,10},{9,11},{10,... | collective-permute-start | bytes 393224 | tf_op jit(solution)/shard_map/ppermute | solution.py:131
  14.5 7.1 %collective-permute-start.1 = (bf16[2,192,128]{2,1,0:T(8,128)(2,1)}, bf16[2,192,128]{2,1,0:T(8,128)(2,1)S(1)}, u32[]{:S(2)}, u32[]{:S(2)}) collective-permute-start(bf16[2,192,128]{2,1,0:T(8,128)(2,1)} %get-tuple-element.22), channel_id=1, source_target_pairs={{0,1},{1,0},{2,3},{3,2},{4,5},{5,4},{6,7},{7,6},{8,9},{9,8},{10,11... | collective-permute-start | bytes 294920 | tf_op jit(solution)/shard_map/ppermute | solution.py:131
  14.5 18.4 %collective-permute-start.2 = (bf16[2,12,128,128]{3,2,1,0:T(8,128)(2,1)S(1)}, bf16[2,12,128,128]{3,2,1,0:T(8,128)(2,1)S(1)}, u32[]{:S(2)}, u32[]{:S(2)}) collective-permute-start(bf16[2,12,128,128]{3,2,1,0:T(8,128)(2,1)S(1)} %copy-done.3), channel_id=1, source_target_pairs={{0,1},{1,0},{2,3},{3,2},{4,5},{5,4},{6,7},{7,6},{8,9},{9,8},{10,11... | collective-permute-start | bytes 2359304 | tf_op jit(solution)/shard_map/ppermute | solution.py:131
  19.5 13.4 %collective-permute-start = (f32[12,16]{1,0:T(8,128)S(1)}, f32[12,16]{1,0:T(8,128)S(1)}, u32[]{:S(2)}, u32[]{:S(2)}) collective-permute-start(f32[12,16]{1,0:T(8,128)S(1)} %copy-done.4), channel_id=1, source_target_pairs={{0,1},{1,0},{2,3},{3,2},{4,5},{5,4},{6,7},{7,6},{8,9},{9,8},{10,11... | collective-permute-start | bytes 2312 | tf_op jit(solution)/shard_map/ppermute | solution.py:131
  19.5 6.4 %collective-permute-start.9 = (bf16[2,2,128,128]{3,2,1,0:T(8,128)(2,1)S(1)}, bf16[2,2,128,128]{3,2,1,0:T(8,128)(2,1)S(1)}, u32[]{:S(2)}, u32[]{:S(2)}) collective-permute-start(bf16[2,2,128,128]{3,2,1,0:T(8,128)(2,1)S(1)} %collective-permute-done.8.refs_2_), channel_id=1, source_target_pairs={{0,2},{1,3},{2,0},{3,1},{4,6},{5,7},{6,4},{7,5},{8,10},{9,11},{10,... | collective-permute-start | bytes 393224 | tf_op jit(solution)/shard_map/ppermute | solution.py:131
  21.0 7.3 %collective-permute-start.5 = (bf16[2,2,128,128]{3,2,1,0:T(8,128)(2,1)S(1)}, bf16[2,2,128,128]{3,2,1,0:T(8,128)(2,1)S(1)}, u32[]{:S(2)}, u32[]{:S(2)}) collective-permute-start(bf16[2,2,128,128]{3,2,1,0:T(8,128)(2,1)S(1)} %collective-permute-done.4.refs_2_), channel_id=1, source_target_pairs={{0,2},{1,3},{2,0},{3,1},{4,6},{5,7},{6,4},{7,5},{8,10},{9,11},{10,... | collective-permute-start | bytes 393224 | tf_op jit(solution)/shard_map/ppermute | solution.py:131
  21.6 6.9 %collective-permute-start.14 = (bf16[4,2,128,128]{3,2,1,0:T(8,128)(2,1)S(1)}, bf16[4,2,128,128]{3,2,1,0:T(8,128)(2,1)S(1)}, u32[]{:S(2)}, u32[]{:S(2)}) collective-permute-start(bf16[4,2,128,128]{3,2,1,0:T(8,128)(2,1)S(1)} %pad_maximum_fusion.2), channel_id=1, source_target_pairs={{0,1},{1,0},{2,3},{3,2},{4,5},{5,4},{6,7},{7,6},{8,9},{9,8},{10,11... | collective-permute-start | bytes 786440 | tf_op jit(solution)/shard_map/ppermute | solution.py:131
  25.9 9.9 %collective-permute-start.15 = (bf16[2,2,192,128]{3,2,1,0:T(8,128)(2,1)S(1)}, bf16[2,2,192,128]{3,2,1,0:T(8,128)(2,1)S(1)}, u32[]{:S(2)}, u32[]{:S(2)}) collective-permute-start(bf16[2,2,192,128]{3,2,1,0:T(8,128)(2,1)S(1)} %pad_maximum_fusion.3.refs_3_), channel_id=1, source_target_pairs={{0,12},{4,8},{8,4},{12,0},{1,13},{5,9},{9,5},{13,1},{2,14},{6,10},... | collective-permute-start | bytes 589832 | tf_op jit(solution)/shard_map/ppermute | solution.py:131
  28.4 1.6 %collective-permute-start.10 = (bf16[4,2,128,128]{3,2,1,0:T(8,128)(2,1)S(1)}, bf16[4,2,128,128]{3,2,1,0:T(8,128)(2,1)S(1)}, u32[]{:S(2)}, u32[]{:S(2)}) collective-permute-start(bf16[4,2,128,128]{3,2,1,0:T(8,128)(2,1)S(1)} %pad_maximum_fusion.1), channel_id=1, source_target_pairs={{0,1},{1,0},{2,3},{3,2},{4,5},{5,4},{6,7},{7,6},{8,9},{9,8},{10,11... | collective-permute-start | bytes 786440 | tf_op jit(solution)/shard_map/ppermute | solution.py:131
  28.5 3.2 %collective-permute-start.6 = (bf16[4,2,128,128]{3,2,1,0:T(8,128)(2,1)S(1)}, bf16[4,2,128,128]{3,2,1,0:T(8,128)(2,1)S(1)}, u32[]{:S(2)}, u32[]{:S(2)}) collective-permute-start(bf16[4,2,128,128]{3,2,1,0:T(8,128)(2,1)S(1)} %pad_maximum_fusion), channel_id=1, source_target_pairs={{0,1},{1,0},{2,3},{3,2},{4,5},{5,4},{6,7},{7,6},{8,9},{9,8},{10,11... | collective-permute-start | bytes 786440 | tf_op jit(solution)/shard_map/ppermute | solution.py:131
  30.0 17.7 %collective-permute-start.11 = (bf16[2,2,192,128]{3,2,1,0:T(8,128)(2,1)S(1)}, bf16[2,2,192,128]{3,2,1,0:T(8,128)(2,1)S(1)}, u32[]{:S(2)}, u32[]{:S(2)}) collective-permute-start(bf16[2,2,192,128]{3,2,1,0:T(8,128)(2,1)S(1)} %pad_maximum_fusion.3.refs_3_), channel_id=1, source_target_pairs={{0,8},{4,12},{8,0},{12,4},{1,9},{5,13},{9,1},{13,5},{2,10},{6,14},... | collective-permute-start | bytes 589832 | tf_op jit(solution)/shard_map/ppermute | solution.py:131
  31.7 19.7 %collective-permute-start.7 = (bf16[2,2,192,128]{3,2,1,0:T(8,128)(2,1)S(1)}, bf16[2,2,192,128]{3,2,1,0:T(8,128)(2,1)S(1)}, u32[]{:S(2)}, u32[]{:S(2)}) collective-permute-start(bf16[2,2,192,128]{3,2,1,0:T(8,128)(2,1)S(1)} %pad_maximum_fusion.3.refs_3_), channel_id=1, source_target_pairs={{0,4},{4,0},{8,12},{12,8},{1,5},{5,1},{9,13},{13,9},{2,6},{6,2},{1... | collective-permute-start | bytes 589832 | tf_op jit(solution)/shard_map/ppermute | solution.py:131
  35.7 3.6 %copy-start.1 = (bf16[8,2,8,128]{3,2,1,0:T(8,128)(2,1)}, bf16[8,2,8,128]{3,2,1,0:T(8,128)(2,1)S(1)}, u32[]{:S(2)}) copy-start(bf16[8,2,8,128]{3,2,1,0:T(8,128)(2,1)S(1)} %get-tuple-element.23.refs_0_) | copy-start | bytes 98308
  35.8 11.9 %collective-permute-start.3 = (bf16[8,2,8,128]{3,2,1,0:T(8,128)(2,1)S(1)}, bf16[8,2,8,128]{3,2,1,0:T(8,128)(2,1)S(1)}, u32[]{:S(2)}, u32[]{:S(2)}) collective-permute-start(bf16[8,2,8,128]{3,2,1,0:T(8,128)(2,1)S(1)} %get-tuple-element.24), channel_id=1, source_target_pairs={{0,2},{1,3},{2,0},{3,1},{4,6},{5,7},{6,4},{7,5},{8,10},{9,11},{10,... | collective-permute-start | bytes 98312 | tf_op jit(solution)/shard_map/ppermute | solution.py:131
  39.3 12.1 %collective-permute-start.16 = (bf16[8,2,8,128]{3,2,1,0:T(8,128)(2,1)S(1)}, bf16[8,2,8,128]{3,2,1,0:T(8,128)(2,1)S(1)}, u32[]{:S(2)}, u32[]{:S(2)}) collective-permute-start(bf16[8,2,8,128]{3,2,1,0:T(8,128)(2,1)S(1)} %get-tuple-element.29), channel_id=1, source_target_pairs={{0,12},{4,8},{8,4},{12,0},{1,13},{5,9},{9,5},{13,1},{2,14},{6,10},... | collective-permute-start | bytes 98312 | tf_op jit(solution)/shard_map/ppermute | solution.py:131
  41.0 10.4 %collective-permute-start.17 = (bf16[8,2,8,128]{3,2,1,0:T(8,128)(2,1)S(1)}, bf16[8,2,8,128]{3,2,1,0:T(8,128)(2,1)S(1)}, u32[]{:S(2)}, u32[]{:S(2)}) collective-permute-start(bf16[8,2,8,128]{3,2,1,0:T(8,128)(2,1)S(1)} %get-tuple-element.32), channel_id=1, source_target_pairs={{0,14},{1,15},{2,12},{3,13},{4,10},{5,11},{6,8},{7,9},{8,6},{9,7},... | collective-permute-start | bytes 98312 | tf_op jit(solution)/shard_map/ppermute | solution.py:143
  47.7 2.0 %copy-start.6 = (bf16[8,2,8,128]{3,2,1,0:T(8,128)(2,1)}, bf16[8,2,8,128]{3,2,1,0:T(8,128)(2,1)S(1)}, u32[]{:S(2)}) copy-start(bf16[8,2,8,128]{3,2,1,0:T(8,128)(2,1)S(1)} %collective-permute-done.3.refs_1_) | copy-start | bytes 98308
  49.7 10.5 %collective-permute-start.20 = (bf16[8,2,8,128]{3,2,1,0:T(8,128)(2,1)S(1)}, bf16[8,2,8,128]{3,2,1,0:T(8,128)(2,1)S(1)}, u32[]{:S(2)}, u32[]{:S(2)}) collective-permute-start(bf16[8,2,8,128]{3,2,1,0:T(8,128)(2,1)S(1)} %get-tuple-element.31), channel_id=1, source_target_pairs={{0,8},{4,12},{8,0},{12,4},{1,9},{5,13},{9,1},{13,5},{2,10},{6,14},... | collective-permute-start | bytes 98312 | tf_op jit(solution)/shard_map/ppermute | solution.py:131
  51.4 2.0 %copy-start.7 = (bf16[8,2,8,128]{3,2,1,0:T(8,128)(2,1)}, bf16[8,2,8,128]{3,2,1,0:T(8,128)(2,1)S(1)}, u32[]{:S(2)}) copy-start(bf16[8,2,8,128]{3,2,1,0:T(8,128)(2,1)S(1)} %collective-permute-done.16.refs_6_) | copy-start | bytes 98308
  51.4 2.0 %copy-start.8 = (bf16[8,2,8,128]{3,2,1,0:T(8,128)(2,1)}, bf16[8,2,8,128]{3,2,1,0:T(8,128)(2,1)S(1)}, u32[]{:S(2)}) copy-start(bf16[8,2,8,128]{3,2,1,0:T(8,128)(2,1)S(1)} %collective-permute-done.17.refs_7_) | copy-start | bytes 98308
  53.5 4.5 %collective-permute-start.18 = (bf16[8,2,8,128]{3,2,1,0:T(8,128)(2,1)S(1)}, bf16[8,2,8,128]{3,2,1,0:T(8,128)(2,1)S(1)}, u32[]{:S(2)}, u32[]{:S(2)}) collective-permute-start(bf16[8,2,8,128]{3,2,1,0:T(8,128)(2,1)S(1)} %get-tuple-element.34), channel_id=1, source_target_pairs={{0,4},{4,0},{8,12},{12,8},{1,5},{5,1},{9,13},{13,9},{2,6},{6,2},{1... | collective-permute-start | bytes 98312 | tf_op jit(solution)/shard_map/ppermute | solution.py:131
  55.4 4.8 %collective-permute-start.19 = (bf16[8,2,8,128]{3,2,1,0:T(8,128)(2,1)S(1)}, bf16[8,2,8,128]{3,2,1,0:T(8,128)(2,1)S(1)}, u32[]{:S(2)}, u32[]{:S(2)}) collective-permute-start(bf16[8,2,8,128]{3,2,1,0:T(8,128)(2,1)S(1)} %get-tuple-element.35), channel_id=1, source_target_pairs={{0,6},{1,7},{2,4},{3,5},{4,2},{5,3},{6,0},{7,1},{8,14},{9,15},{10,... | collective-permute-start | bytes 98312 | tf_op jit(solution)/shard_map/ppermute | solution.py:143
  56.9 5.7 %collective-permute-start.21 = (bf16[8,2,8,128]{3,2,1,0:T(8,128)(2,1)S(1)}, bf16[8,2,8,128]{3,2,1,0:T(8,128)(2,1)S(1)}, u32[]{:S(2)}, u32[]{:S(2)}) collective-permute-start(bf16[8,2,8,128]{3,2,1,0:T(8,128)(2,1)S(1)} %get-tuple-element.36), channel_id=1, source_target_pairs={{0,10},{1,11},{2,8},{3,9},{4,14},{5,15},{6,12},{7,13},{8,2},{9,3},... | collective-permute-start | bytes 98312 | tf_op jit(solution)/shard_map/ppermute | solution.py:143
  58.0 4.6 %copy-start.10 = (bf16[8,2,8,128]{3,2,1,0:T(8,128)(2,1)}, bf16[8,2,8,128]{3,2,1,0:T(8,128)(2,1)S(1)}, u32[]{:S(2)}) copy-start(bf16[8,2,8,128]{3,2,1,0:T(8,128)(2,1)S(1)} %collective-permute-done.18.refs_2_) | copy-start | bytes 98308
  60.2 2.5 %copy-start.11 = (bf16[8,2,8,128]{3,2,1,0:T(8,128)(2,1)}, bf16[8,2,8,128]{3,2,1,0:T(8,128)(2,1)S(1)}, u32[]{:S(2)}) copy-start(bf16[8,2,8,128]{3,2,1,0:T(8,128)(2,1)S(1)} %collective-permute-done.19.refs_3_) | copy-start | bytes 98308
  60.2 2.4 %copy-start.9 = (bf16[8,2,8,128]{3,2,1,0:T(8,128)(2,1)}, bf16[8,2,8,128]{3,2,1,0:T(8,128)(2,1)S(1)}, u32[]{:S(2)}) copy-start(bf16[8,2,8,128]{3,2,1,0:T(8,128)(2,1)S(1)} %collective-permute-done.20.refs_4_) | copy-start | bytes 98308
  62.6 0.6 copy-start.12

commit v3 on v2

--- a/solution.py
+++ b/solution.py
@@ -152,9 +152,9 @@
     return order
 
 
-def pack_kernel(devices, terms, partner, wave, left, *refs):
+def pack_kernel(devices, terms, partner, wave, *refs):
     sends = refs[: devices - 1]
-    keep, give, counts, table, sems = refs[devices - 1 :]
+    counts, table, sems = refs[devices - 1 :]
     capacity = SEC_DEV * STATES // devices
     share = capacity // terms
     me, term = lax.axis_index("sec"), lax.axis_index("term")
@@ -179,39 +179,19 @@
             )
             copy.start()
             copies.append(copy)
-    group = ROWS // terms
-    first_core = (term & (NEAR - 1)) == 0
-    for a in range(SEC_DEV):
-        for t in range(left.shape[1]):
-            rows = left[a, t].astype(jnp.float32)
-            tiles = [
-                jnp.concatenate(
-                    [
-                        rows[(far * NEAR + near) * group : (far * NEAR + near + 1) * group]
-                        for far in range(terms // NEAR)
-                    ],
-                    axis=0,
-                )
-                for near in range(NEAR)
-            ]
-            place_rows = slice(t * 2 * group, (t + 1) * 2 * group)
-            keep[a, place_rows, :] = jnp.where(first_core, tiles[0], tiles[1]).astype(jnp.bfloat16)
-            give[a, place_rows, :] = jnp.where(first_core, tiles[1], tiles[0]).astype(jnp.bfloat16)
     for copy in copies:
         copy.wait()
 
 
-def pack(wave, left, partner, devices, terms):
+def pack(wave, partner, devices, terms):
     capacity = SEC_DEV * STATES // devices
     share = capacity // terms
-    local = left.shape[1]
     piece = jax.ShapeDtypeStruct((share, 2, SECTOR, SECTOR), jnp.bfloat16)
-    rows = jax.ShapeDtypeStruct((SEC_DEV, local * (ROWS // NEAR), SECTOR), jnp.bfloat16)
-    outs = pl.pallas_call(
+    return pl.pallas_call(
         functools.partial(pack_kernel, devices, terms),
-        out_shape=[piece] * (devices - 1) + [rows] * 2,
-        in_specs=[SMEM, ANY, VMEM],
-        out_specs=[VMEM] * (devices + 1),
+        out_shape=[piece] * (devices - 1),
+        in_specs=[SMEM, ANY],
+        out_specs=[VMEM] * (devices - 1),
         scratch_shapes=[
             pltpu.SMEM((devices,), jnp.int32),
             pltpu.SMEM((SEC_DEV * STATES,), jnp.int32),
@@ -219,16 +199,16 @@
         ],
         cost_estimate=pl.CostEstimate(flops=0, bytes_accessed=4 << 20, transcendentals=0),
         name="pack",
-    )(partner, wave, left)
-    return outs[: devices - 1], outs[devices - 1], outs[devices]
+    )(partner, wave)
 
 
 def compute_kernel(step, devices, terms, partner, order, *refs):
     coefs, refs = refs[:NEAR], refs[NEAR:]
     pieces = refs[: 1 if step == 0 else terms]
     refs = refs[len(pieces) :]
-    left, rights, (keep, give) = refs[0], refs[1 : 1 + NEAR], refs[1 + NEAR : 3 + NEAR]
-    table, partials = refs[3 + NEAR : 5 + NEAR]
+    lefts, refs = refs[:NEAR], refs[NEAR:]
+    rights, (keep, give) = refs[:NEAR], refs[NEAR : 2 + NEAR]
+    table, partials, cut = refs[2 + NEAR : 5 + NEAR]
     capacity = SEC_DEV * STATES // devices
     share = capacity // terms
     js = piece_order(terms)
@@ -236,7 +216,7 @@
     source = me ^ step
     group = ROWS // terms
     rows = ROWS // NEAR
-    local = left.shape[2] // rows
+    local = lefts[0].shape[1]
     depth = local * SECTOR
 
     def place(n, count):
@@ -254,6 +234,17 @@
             copies.append(copy)
         for copy in copies:
             copy.wait()
+    first_core = (term & (NEAR - 1)) == 0
+    for i in range(NEAR):
+        for a in range(SEC_DEV):
+            for t in range(local):
+                whole = lefts[i][a, t].astype(jnp.float32)
+                parts = [whole[r * group : (r + 1) * group] for r in range(terms)]
+                tile = jnp.concatenate(
+                    [jnp.where(first_core, parts[r], parts[r + 1]) for r in range(0, terms, NEAR)],
+                    axis=0,
+                )
+                cut[i, a, t * rows : (t + 1) * rows, :] = tile.astype(jnp.bfloat16)
     row_index = lax.broadcasted_iota(jnp.int32, (SECTOR, SECTOR), 0)
     col_index = lax.broadcasted_iota(jnp.int32, (SECTOR, SECTOR), 1)
 
@@ -275,7 +266,7 @@
         both = jnp.concatenate(vectors, axis=1)
         place_row = (j * share + sub) * 2 * rows
         for i in range(NEAR):
-            product = jnp.dot(left[i, sector], both, preferred_element_type=jnp.float32)
+            product = jnp.dot(cut[i, sector], both, preferred_element_type=jnp.float32)
             for t in range(local):
                 scaled = product[t * rows : (t + 1) * rows] * coefs[i][t, state]
                 start = (i * local + t) * SECTOR
@@ -318,13 +309,14 @@
                 give[slot, v] = jnp.where(near_first, high, low).astype(give.dtype)
 
 
-def compute(step, pieces, left, rights, coefs, order, partner, devices, terms):
+def compute(step, pieces, lefts, rights, coefs, order, partner, devices, terms):
     capacity = SEC_DEV * STATES // devices
     rows = ROWS // NEAR
-    local = left.shape[2] // rows
+    local = lefts[0].shape[1]
     scratch = [
         pltpu.SMEM((SEC_DEV * STATES + 1,), jnp.int32),
         pltpu.VMEM((capacity * 2 * rows, NEAR * local * SECTOR), jnp.bfloat16),
+        pltpu.VMEM((NEAR, SEC_DEV, local * rows, SECTOR), jnp.bfloat16),
     ]
     if step == 0:
         scratch += [
@@ -337,7 +329,7 @@
         out_shape=[part, part],
         in_specs=[SMEM] * (2 + NEAR)
         + [ANY if step == 0 else VMEM] * len(pieces)
-        + [VMEM] * (1 + NEAR),
+        + [VMEM] * (2 * NEAR),
         out_specs=[VMEM, VMEM],
         scratch_shapes=scratch,
         compiler_params=pltpu.CompilerParams(vmem_limit_bytes=32 << 20),
@@ -345,7 +337,7 @@
             flops=3 << 30, bytes_accessed=4 << 20, transcendentals=0
         ),
         name=f"products_{step}",
-    )(partner, order, *coefs, *pieces, left, *rights)
+    )(partner, order, *coefs, *pieces, *lefts, *rights)
 
 
 def unpack_kernel(devices, partner, *refs):
@@ -398,38 +390,38 @@
     devices, terms = lax.axis_size("sec"), lax.axis_size("term")
     block_count = SEC_DEV * STATES
     wave = wavefunction.reshape(block_count, 2, SECTOR, SECTOR)
-    steps = list(range(devices - 1, 0, -1))
-    sends, left_keep, left_give = pack(wave, left_window, partner, devices, terms)
+    steps = [2, 3, 1]
     coefs = [couplings, exchange(couplings, "term", 1)]
     rights = [right_blocks, exchange(right_blocks, "term", 1)]
-    left_all = jnp.stack([left_keep, exchange(left_give, "term", 1)])
+    sends = pack(wave, partner, devices, terms)
     arrived = {step: exchange(sends[step - 1], "sec", step) for step in steps}
-    lefts = {step: exchange(left_all, "sec", step) for step in steps}
-    lefts[0] = left_all
-    vectors = {0: [wave]}
+    every = list(arrived.values())
+
+    def products(step, vectors, lefts):
+        return compute(
+            step, vectors, lefts, rights, coefs, sector_order, partner, devices, terms
+        )
+
+    left_in = {}
+    held = {0: after(left_window, *every)}
+    bit = devices // 2
+    while bit:
+        for step in list(held):
+            held[step ^ bit] = left_in[step ^ bit] = exchange(held[step], "sec", bit)
+        bit //= 2
+    keep, give = products(0, [wave], [left_window, exchange(left_window, "term", 1)])
+    chunks = {0: (keep, exchange_both(give, 0, NEAR))}
+    waits = [keep]
     for step in steps:
-        x = exchange(arrived[step], "term", NEAR)
+        x = exchange(after(arrived[step], *every), "term", NEAR)
         both = jnp.concatenate([arrived[step], x])
+        both, left = lax.optimization_barrier((both, left_in[step], waits[0]))[:2]
+        lefts = [left, exchange(left, "term", 1)]
         both = jnp.concatenate([both, exchange(both, "term", 1)])
-        vectors[step] = jnp.split(both, terms)
-    chunks = {}
-    waits = []
-    for step in [0] + steps:
-        keep, give = compute(
-            step,
-            vectors[step],
-            after(lefts[step], *waits),
-            rights,
-            coefs,
-            sector_order,
-            partner,
-            devices,
-            terms,
-        )
+        lefts[0] = after(lefts[0], *waits)
+        keep, give = products(step, jnp.split(both, terms), lefts)
         waits = [keep] + [part for value in list(chunks.values())[-1:] for part in value]
-        if step:
-            keep = exchange(keep, "sec", step)
-        chunks[step] = (keep, exchange_both(give, step, NEAR))
+        chunks[step] = (exchange(keep, "sec", step), exchange_both(give, step, NEAR))
     chunks = [part for step in range(devices) for part in chunks[step]]
     out = unpack(chunks, partner, devices)
     return out.reshape(SEC_DEV, STATES, 2, ROWS // terms, SECTOR)

time: 65.9 us -> 62.6 us (0.950)
  waiting for transfers between devices: 21.7 us -> 19 us
  local copies, waits for them, and re-layouts: 0.71 us -> 1.89 us
  other arithmetic: 0.99 us -> 0.08 us
  starting transfers between devices: 27.8 us -> 26.9 us
    ppermute x3, waiting for transfers between devices: 4.6 us -> 0.98 us  [exchange_both(): return lax.ppermute(x, ('sec', 'term'), pairs)]
    ppermute x19 -> x22, starting transfers between devices: 22.9 us -> 19.6 us  [exchange(): return lax.ppermute(x, axis, [(i, i ^ step) for i in range(size)])]
    ppermute x3, starting transfers between devices: 4.85 us -> 7.3 us  [exchange_both(): return lax.ppermute(x, ('sec', 'term'), pairs)]
    unnamed x26 -> x30, local copies, waits for them, and re-layouts: 0.66 us -> 1.78 us
    another operation x1 -> x0, other arithmetic: 0.91 us -> none  [paired_body(): left_all = jnp.stack([left_keep, exchange(left_give, 'term', 1)])]
    ppermute x19 -> x22, waiting for transfers between devices: 17.1 us -> 18 us  [exchange(): return lax.ppermute(x, axis, [(i, i ^ step) for i in range(size)])]
  transfers between devices with their start and end apart: 22 -> 25, of which waited for: 7 -> 7; matrix products, arithmetic and copies ran while one was open for 2% -> 0% of each run, Pallas kernels for 13% -> 19%
where the time goes in v3:
time: 62.6 us; the launch traced here: 62.3 us
  starting transfers between devices  26.9 us (43%)
  waiting for transfers between devices  19 us (30%)
  Pallas kernels  14.1 us (23%)
  local copies, waits for them, and re-layouts  1.89 us (3%)
    ppermute x22, starting transfers between devices, exchange(): return lax.ppermute(x, axis, [(i, i ^ step) for i in range(size)])  19.6 us
    ppermute x22, waiting for transfers between devices, exchange(): return lax.ppermute(x, axis, [(i, i ^ step) for i in range(size)])  18 us
    pallas_call x4, Pallas kernels, compute(): pl.pallas_call(functools.partial(compute_kernel, step, devices, terms), o...  8.94 us
    ppermute x3, starting transfers between devices, exchange_both(): return lax.ppermute(x, ('sec', 'term'), pairs)  7.3 us
    pallas_call x1, Pallas kernels, pack(): pl.pallas_call(functools.partial(pack_kernel, devices, terms), out_shape=...  2.82 us
    pallas_call x1, Pallas kernels, unpack(): pl.pallas_call(functools.partial(unpack_kernel, devices), out_shape=jax.S...  2.35 us
    unnamed x30, local copies, waits for them, and re-layouts  1.78 us
  transfers between devices with their start and end apart: 25, of which 7 were waited for; matrix products, arithmetic and copies ran while one was open for 0% of the time, Pallas kernels for 19%

profile of v3, /device:TPU:0, one launch (start us, length us, event | category | flops | bytes accessed | tf_op | source)
XLA Modules:
  0.0 62.3 jit_solution(10873166614708541641)
XLA Ops:
  0.0 0.5 collective-permute-start.2
  0.6 2.8 %pack.1 = (bf16[2,2,128,128]{3,2,1,0:T(8,128)(2,1)}, bf16[2,2,128,128]{3,2,1,0:T(8,128)(2,1)}, bf16[2,2,128,128]{3,2,1,0:T(8,128)(2,1)}) custom-call(s32[8,16]{1,0:T(8,128)} %partner.11, bf16[32,2,128,128]{3,2,1,0:T(8,128)(2,1)} %bitcast.2), custom_call_target="tpu_custom_call" | custom-call | bytes 4194304 | tf_op jit(solution)/shard_map/pack/pallas_call | solution.py:190
  3.4 2.7 %collective-permute-start.4 = (bf16[2,2,128,128]{3,2,1,0:T(8,128)(2,1)}, bf16[2,2,128,128]{3,2,1,0:T(8,128)(2,1)S(1)}, u32[]{:S(2)}, u32[]{:S(2)}) collective-permute-start(bf16[2,2,128,128]{3,2,1,0:T(8,128)(2,1)} %get-tuple-element.31), channel_id=1, source_target_pairs={{0,4},{4,0},{8,12},{12,8},{1,5},{5,1},{9,13},{13,9},{2,6},{6,2},{1... | collective-permute-start | bytes 393224 | tf_op jit(solution)/shard_map/ppermute | solution.py:131
  6.0 2.6 %collective-permute-start.5 = (bf16[2,2,128,128]{3,2,1,0:T(8,128)(2,1)}, bf16[2,2,128,128]{3,2,1,0:T(8,128)(2,1)S(1)}, u32[]{:S(2)}, u32[]{:S(2)}) collective-permute-start(bf16[2,2,128,128]{3,2,1,0:T(8,128)(2,1)} %get-tuple-element.32), channel_id=1, source_target_pairs={{0,8},{4,12},{8,0},{12,4},{1,9},{5,13},{9,1},{13,5},{2,10},{6,14},... | collective-permute-start | bytes 393224 | tf_op jit(solution)/shard_map/ppermute | solution.py:131
  8.6 0.0 collective-permute-start.6
  8.6 3.7 %collective-permute-done.4 = bf16[2,2,128,128]{3,2,1,0:T(8,128)(2,1)S(1)} collective-permute-done((bf16[2,2,128,128]{3,2,1,0:T(8,128)(2,1)}, bf16[2,2,128,128]{3,2,1,0:T(8,128)(2,1)S(1)}, u32[]{:S(2)}, u32[]{:S(2)}) %collective-permute-start.4) | collective-permute-done | bytes 131104 | tf_op jit(solution)/shard_map/ppermute | solution.py:131
  12.4 6.8 %collective-permute-done.5 = bf16[2,2,128,128]{3,2,1,0:T(8,128)(2,1)S(1)} collective-permute-done((bf16[2,2,128,128]{3,2,1,0:T(8,128)(2,1)}, bf16[2,2,128,128]{3,2,1,0:T(8,128)(2,1)S(1)}, u32[]{:S(2)}, u32[]{:S(2)}) %collective-permute-start.5) | collective-permute-done | bytes 131104 | tf_op jit(solution)/shard_map/ppermute | solution.py:131
  19.2 1.5 %collective-permute-start.12 = (bf16[2,2,128,128]{3,2,1,0:T(8,128)(2,1)S(1)}, bf16[2,2,128,128]{3,2,1,0:T(8,128)(2,1)S(1)}, u32[]{:S(2)}, u32[]{:S(2)}) collective-permute-start(bf16[2,2,128,128]{3,2,1,0:T(8,128)(2,1)S(1)} %collective-permute-done.5), channel_id=1, source_target_pairs={{0,2},{1,3},{2,0},{3,1},{4,6},{5,7},{6,4},{7,5},{8,10},{9,11},{10,... | collective-permute-start | bytes 393224 | tf_op jit(solution)/shard_map/ppermute | solution.py:131
  20.7 0.0 collective-permute-start.1
  20.7 0.5 collective-permute-start
  21.2 3.5 %collective-permute-start.10 = (bf16[2,12,32,128]{3,2,1,0:T(8,128)(2,1)}, bf16[2,12,32,128]{3,2,1,0:T(8,128)(2,1)S(1)}, u32[]{:S(2)}, u32[]{:S(2)}) collective-permute-start(bf16[2,12,32,128]{3,2,1,0:T(8,128)(2,1)} %refs_3_.1), channel_id=1, source_target_pairs={{0,8},{4,12},{8,0},{12,4},{1,9},{5,13},{9,1},{13,5},{2,10},{6,14},... | collective-permute-start | bytes 589832 | tf_op jit(solution)/shard_map/ppermute | solution.py:131
  24.7 0.0 collective-permute-done.12
  24.7 2.0 %collective-permute-start.8 = (bf16[2,12,32,128]{3,2,1,0:T(8,128)(2,1)}, bf16[2,12,32,128]{3,2,1,0:T(8,128)(2,1)S(1)}, u32[]{:S(2)}, u32[]{:S(2)}) collective-permute-start(bf16[2,12,32,128]{3,2,1,0:T(8,128)(2,1)} %refs_3_.1), channel_id=1, source_target_pairs={{0,4},{4,0},{8,12},{12,8},{1,5},{5,1},{9,13},{13,9},{2,6},{6,2},{1... | collective-permute-start | bytes 589832 | tf_op jit(solution)/shard_map/ppermute | solution.py:131
  26.7 0.0 collective-permute-done.refs_1_
  26.7 1.6 %collective-permute-start.9 = (bf16[2,2,128,128]{3,2,1,0:T(8,128)(2,1)S(1)}, bf16[2,2,128,128]{3,2,1,0:T(8,128)(2,1)S(1)}, u32[]{:S(2)}, u32[]{:S(2)}) collective-permute-start(bf16[2,2,128,128]{3,2,1,0:T(8,128)(2,1)S(1)} %collective-permute-done.6), channel_id=1, source_target_pairs={{0,2},{1,3},{2,0},{3,1},{4,6},{5,7},{6,4},{7,5},{8,10},{9,11},{10,... | collective-permute-start | bytes 393224 | tf_op jit(solution)/shard_map/ppermute | solution.py:131
  28.2 0.0 collective-permute-done.1.refs_4_
  28.2 0.5 collective-permute-start.7
  28.8 0.0 collective-permute-done.2.refs_6_.refs_9_
  28.8 0.0 copy-start.3
  28.8 1.1 %copy-done.3 = bf16[2,12,128,128]{3,2,1,0:T(8,128)(2,1)S(1)} copy-done((bf16[2,12,128,128]{3,2,1,0:T(8,128)(2,1)S(1)}, bf16[2,12,128,128]{3,2,1,0:T(8,128)(2,1)}, u32[]{:S(2)}) %copy-start.3) | copy-done | bytes 786456
  29.9 2.8 %products_0.1 = (bf16[8,2,8,128]{3,2,1,0:T(8,128)(2,1)S(1)}, bf16[8,2,8,128]{3,2,1,0:T(8,128)(2,1)S(1)}) custom-call(s32[8,16]{1,0:T(8,128)S(1)} %copy-done.2, s32[8]{0:T(128)S(1)} %copy-done.7, f32[12,16]{1,0:T(8,128)S(1)} %copy-done.6, f32[12,16]{1,0:T(8,128)S(1)} %collective-permute-done.refs_1_, bf16[32,2,128,128]{3,2,1,0:T(8,128)(2,1)S(1)} %bitcast.3, ...), custom_call_target="tpu_custom_call" | custom-call | flops 3221225472 | bytes 4194304 | tf_op jit(solution)/shard_map/products_0/pallas_call | solution.py:327
  32.8 1.5 %collective-permute-done.10.refs_6_ = bf16[2,12,32,128]{3,2,1,0:T(8,128)(2,1)S(1)} collective-permute-done((bf16[2,12,32,128]{3,2,1,0:T(8,128)(2,1)}, bf16[2,12,32,128]{3,2,1,0:T(8,128)(2,1)S(1)}, u32[]{:S(2)}, u32[]{:S(2)}) %collective-permute-start.10) | collective-permute-done | bytes 196640 | tf_op jit(solution)/shard_map/ppermute | solution.py:131
  34.3 0.0 collective-permute-start.13
  34.3 0.0 collective-permute-done.9
  34.3 0.1 collective-permute-start.11
  34.4 0.6 collective-permute-start.14
  35.0 0.8 %collective-permute-done.13 = bf16[4,2,128,128]{3,2,1,0:T(8,128)(2,1)S(1)} collective-permute-done((bf16[4,2,128,128]{3,2,1,0:T(8,128)(2,1)S(1)}, bf16[4,2,128,128]{3,2,1,0:T(8,128)(2,1)S(1)}, u32[]{:S(2)}, u32[]{:S(2)}) %collective-permute-start.13) | collective-permute-done | bytes 262176 | tf_op jit(solution)/shard_map/ppermute | solution.py:131
  35.8 0.5 collective-permute-start.3
  36.4 0.0 collective-permute-done.14.refs_7_
  36.4 2.0 %products_2.1 = (bf16[8,2,8,128]{3,2,1,0:T(8,128)(2,1)S(1)}, bf16[8,2,8,128]{3,2,1,0:T(8,128)(2,1)S(1)}) custom-call(s32[8,16]{1,0:T(8,128)S(1)} %copy-done.2, s32[8]{0:T(128)S(1)} %copy-done.7, f32[12,16]{1,0:T(8,128)S(1)} %copy-done.6, f32[12,16]{1,0:T(8,128)S(1)} %collective-permute-done.refs_1_, bf16[2,2,128,128]{3,2,1,0:T(8,128)(2,1)S(1)} %get-tuple-element.64.refs_2_, ...), custom_call_target="tpu_custom_call" | custom-call | flops 3221225472 | bytes 4194304 | tf_op jit(solution)/shard_map/products_2/pallas_call | solution.py:327
  38.4 3.3 %collective-permute-done.11.refs_6_ = bf16[2,12,32,128]{3,2,1,0:T(8,128)(2,1)S(1)} collective-permute-done((bf16[2,12,32,128]{3,2,1,0:T(8,128)(2,1)S(1)}, bf16[2,12,32,128]{3,2,1,0:T(8,128)(2,1)S(1)}, u32[]{:S(2)}, u32[]{:S(2)}) %collective-permute-start.11) | collective-permute-done | bytes 196640 | tf_op jit(solution)/shard_map/ppermute | solution.py:131
  41.7 0.4 collective-permute-start.18
  42.1 0.2 collective-permute-start.16
  42.4 0.0 collective-permute-done.3.refs_1_
  42.4 2.5 %collective-permute-start.19 = (bf16[8,2,8,128]{3,2,1,0:T(8,128)(2,1)S(1)}, bf16[8,2,8,128]{3,2,1,0:T(8,128)(2,1)S(1)}, u32[]{:S(2)}, u32[]{:S(2)}) collective-permute-start(bf16[8,2,8,128]{3,2,1,0:T(8,128)(2,1)S(1)} %get-tuple-element.48), channel_id=1, source_target_pairs={{0,10},{1,11},{2,8},{3,9},{4,14},{5,15},{6,12},{7,13},{8,2},{9,3},... | collective-permute-start | bytes 98312 | tf_op jit(solution)/shard_map/ppermute | solution.py:143
  44.9 0.0 collective-permute-done.15
  45.0 2.0 %products_3.1 = (bf16[8,2,8,128]{3,2,1,0:T(8,128)(2,1)S(1)}, bf16[8,2,8,128]{3,2,1,0:T(8,128)(2,1)S(1)}) custom-call(s32[8,16]{1,0:T(8,128)S(1)} %copy-done.2, s32[8]{0:T(128)S(1)} %copy-done.7, f32[12,16]{1,0:T(8,128)S(1)} %copy-done.6, f32[12,16]{1,0:T(8,128)S(1)} %collective-permute-done.refs_1_, bf16[2,2,128,128]{3,2,1,0:T(8,128)(2,1)S(1)} %get-tuple-element.60.refs_2_, ...), custom_call_target="tpu_custom_call" | custom-call | flops 3221225472 | bytes 4194304 | tf_op jit(solution)/shard_map/products_3/pallas_call | solution.py:327
  47.1 0.1 collective-permute-start.17
  47.1 2.1 %collective-permute-start.23 = (bf16[8,2,8,128]{3,2,1,0:T(8,128)(2,1)S(1)}, bf16[8,2,8,128]{3,2,1,0:T(8,128)(2,1)S(1)}, u32[]{:S(2)}, u32[]{:S(2)}) collective-permute-start(bf16[8,2,8,128]{3,2,1,0:T(8,128)(2,1)S(1)} %get-tuple-element.45), channel_id=1, source_target_pairs={{0,12},{4,8},{8,4},{12,0},{1,13},{5,9},{9,5},{13,1},{2,14},{6,10},... | collective-permute-start | bytes 98312 | tf_op jit(solution)/shard_map/ppermute | solution.py:131
  49.2 0.2 collective-permute-start.20
  49.4 2.8 %collective-permute-start.24 = (bf16[8,2,8,128]{3,2,1,0:T(8,128)(2,1)S(1)}, bf16[8,2,8,128]{3,2,1,0:T(8,128)(2,1)S(1)}, u32[]{:S(2)}, u32[]{:S(2)}) collective-permute-start(bf16[8,2,8,128]{3,2,1,0:T(8,128)(2,1)S(1)} %get-tuple-element.52), channel_id=1, source_target_pairs={{0,14},{1,15},{2,12},{3,13},{4,10},{5,11},{6,8},{7,9},{8,6},{9,7},... | collective-permute-start | bytes 98312 | tf_op jit(solution)/shard_map/ppermute | solution.py:143
  52.3 2.0 %products_1.1 = (bf16[8,2,8,128]{3,2,1,0:T(8,128)(2,1)S(1)}, bf16[8,2,8,128]{3,2,1,0:T(8,128)(2,1)S(1)}) custom-call(s32[8,16]{1,0:T(8,128)S(1)} %copy-done.2, s32[8]{0:T(128)S(1)} %copy-done.7, f32[12,16]{1,0:T(8,128)S(1)} %copy-done.6, f32[12,16]{1,0:T(8,128)S(1)} %collective-permute-done.refs_1_, bf16[2,2,128,128]{3,2,1,0:T(8,128)(2,1)S(1)} %get-tuple-element.56.refs_2_, ...), custom_call_target="tpu_custom_call" | custom-call | flops 3221225472 | bytes 4194304 | tf_op jit(solution)/shard_map/products_1/pallas_call | solution.py:327
  54.3 0.1 collective-permute-start.21
  54.4 2.0 %collective-permute-start.22 = (bf16[8,2,8,128]{3,2,1,0:T(8,128)(2,1)S(1)}, bf16[8,2,8,128]{3,2,1,0:T(8,128)(2,1)S(1)}, u32[]{:S(2)}, u32[]{:S(2)}) collective-permute-start(bf16[8,2,8,128]{3,2,1,0:T(8,128)(2,1)S(1)} %get-tuple-element.51), channel_id=1, source_target_pairs={{0,6},{1,7},{2,4},{3,5},{4,2},{5,3},{6,0},{7,1},{8,14},{9,15},{10,... | collective-permute-start | bytes 98312 | tf_op jit(solution)/shard_map/ppermute | solution.py:143
  56.4 1.9 %collective-permute-done.21.refs_2_ = bf16[8,2,8,128]{3,2,1,0:T(8,128)(2,1)S(1)} collective-permute-done((bf16[8,2,8,128]{3,2,1,0:T(8,128)(2,1)S(1)}, bf16[8,2,8,128]{3,2,1,0:T(8,128)(2,1)S(1)}, u32[]{:S(2)}, u32[]{:S(2)}) %collective-permute-start.21) | collective-permute-done | bytes 32800 | tf_op jit(solution)/shard_map/ppermute | solution.py:131
  58.3 1.0 %collective-permute-done.22.refs_3_ = bf16[8,2,8,128]{3,2,1,0:T(8,128)(2,1)S(1)} collective-permute-done((bf16[8,2,8,128]{3,2,1,0:T(8,128)(2,1)S(1)}, bf16[8,2,8,128]{3,2,1,0:T(8,128)(2,1)S(1)}, u32[]{:S(2)}, u32[]{:S(2)}) %collective-permute-start.22) | collective-permute-done | bytes 32800 | tf_op jit(solution)/shard_map/ppermute | solution.py:143
  59.3 0.6 copy-done.14
  59.9 2.4 %unpack.1 = bf16[32,2,8,128]{3,2,1,0:T(8,128)(2,1)} custom-call(s32[8,16]{1,0:T(8,128)} %partner.11, bf16[8,2,8,128]{3,2,1,0:T(8,128)(2,1)} %copy-done.1, bf16[8,2,8,128]{3,2,1,0:T(8,128)(2,1)} %copy-done.8, bf16[8,2,8,128]{3,2,1,0:T(8,128)(2,1)} %copy-done.13, bf16[8,2,8,128]{3,2,1,0:T(8,128)(2,1)} %copy-done.14, bf16[8,2,8,128]{3,2,1,0:T(8,128)(2,1)} %copy-done.9, ...), custom_call_target="tpu_custom_call" | custom-call | bytes 1048576 | tf_op jit(solution)/shard_map/unpack/pallas_call | solution.py:373
  (47 shorter events, 0.3 us)
Async XLA Ops:
  0.0 28.8 %copy-start = (bf16[2,16,2,128,128]{4,3,2,1,0:T(8,128)(2,1)S(1)}, bf16[2,16,2,128,128]{4,3,2,1,0:T(8,128)(2,1)}, u32[]{:S(2)}) copy-start(bf16[2,16,2,128,128]{4,3,2,1,0:T(8,128)(2,1)} %param.6) | copy-start | bytes 6291460
  0.0 28.8 %copy-start.2 = (s32[8,16]{1,0:T(8,128)S(1)}, s32[8,16]{1,0:T(8,128)}, u32[]{:S(2)}) copy-start(s32[8,16]{1,0:T(8,128)} %partner.11) | copy-start | bytes 1540
  0.0 28.8 %copy-start.5 = (bf16[2,12,32,128]{3,2,1,0:T(8,128)(2,1)S(1)}, bf16[2,12,32,128]{3,2,1,0:T(8,128)(2,1)}, u32[]{:S(2)}) copy-start(bf16[2,12,32,128]{3,2,1,0:T(8,128)(2,1)} %refs_3_.1) | copy-start | bytes 589828
  0.0 28.8 %copy-start.6 = (f32[12,16]{1,0:T(8,128)S(1)}, f32[12,16]{1,0:T(8,128)}, u32[]{:S(2)}) copy-start(f32[12,16]{1,0:T(8,128)} %refs_0_.7) | copy-start | bytes 2308
  0.0 28.8 %copy-start.7 = (s32[8]{0:T(128)S(1)}, s32[8]{0:T(128)}, u32[]{:S(2)}) copy-start(s32[8]{0:T(128)} %order.7) | copy-start | bytes 100
  0.0 28.8 %collective-permute-start.2 = (bf16[2,12,128,128]{3,2,1,0:T(8,128)(2,1)}, bf16[2,12,128,128]{3,2,1,0:T(8,128)(2,1)S(1)}, u32[]{:S(2)}, u32[]{:S(2)}) collective-permute-start(bf16[2,12,128,128]{3,2,1,0:T(8,128)(2,1)} %refs_8_.5), channel_id=1, source_target_pairs={{0,1},{1,0},{2,3},{3,2},{4,5},{5,4},{6,7},{7,6},{8,9},{9,8},{10,11... | collective-permute-start | bytes 2359304 | tf_op jit(solution)/shard_map/ppermute | solution.py:131
  3.4 9.0 %collective-permute-start.4 = (bf16[2,2,128,128]{3,2,1,0:T(8,128)(2,1)}, bf16[2,2,128,128]{3,2,1,0:T(8,128)(2,1)S(1)}, u32[]{:S(2)}, u32[]{:S(2)}) collective-permute-start(bf16[2,2,128,128]{3,2,1,0:T(8,128)(2,1)} %get-tuple-element.31), channel_id=1, source_target_pairs={{0,4},{4,0},{8,12},{12,8},{1,5},{5,1},{9,13},{13,9},{2,6},{6,2},{1... | collective-permute-start | bytes 393224 | tf_op jit(solution)/shard_map/ppermute | solution.py:131
  6.0 13.1 %collective-permute-start.5 = (bf16[2,2,128,128]{3,2,1,0:T(8,128)(2,1)}, bf16[2,2,128,128]{3,2,1,0:T(8,128)(2,1)S(1)}, u32[]{:S(2)}, u32[]{:S(2)}) collective-permute-start(bf16[2,2,128,128]{3,2,1,0:T(8,128)(2,1)} %get-tuple-element.32), channel_id=1, source_target_pairs={{0,8},{4,12},{8,0},{12,4},{1,9},{5,13},{9,1},{13,5},{2,10},{6,14},... | collective-permute-start | bytes 393224 | tf_op jit(solution)/shard_map/ppermute | solution.py:131
  8.6 10.5 %collective-permute-start.6 = (bf16[2,2,128,128]{3,2,1,0:T(8,128)(2,1)}, bf16[2,2,128,128]{3,2,1,0:T(8,128)(2,1)S(1)}, u32[]{:S(2)}, u32[]{:S(2)}) collective-permute-start(bf16[2,2,128,128]{3,2,1,0:T(8,128)(2,1)} %get-tuple-element.33), channel_id=1, source_target_pairs={{0,12},{4,8},{8,4},{12,0},{1,13},{5,9},{9,5},{13,1},{2,14},{6,10},... | collective-permute-start | bytes 393224 | tf_op jit(solution)/shard_map/ppermute | solution.py:131
  19.2 5.5 %collective-permute-start.12 = (bf16[2,2,128,128]{3,2,1,0:T(8,128)(2,1)S(1)}, bf16[2,2,128,128]{3,2,1,0:T(8,128)(2,1)S(1)}, u32[]{:S(2)}, u32[]{:S(2)}) collective-permute-start(bf16[2,2,128,128]{3,2,1,0:T(8,128)(2,1)S(1)} %collective-permute-done.5), channel_id=1, source_target_pairs={{0,2},{1,3},{2,0},{3,1},{4,6},{5,7},{6,4},{7,5},{8,10},{9,11},{10,... | collective-permute-start | bytes 393224 | tf_op jit(solution)/shard_map/ppermute | solution.py:131
  20.7 7.6 %collective-permute-start.1 = (bf16[2,12,32,128]{3,2,1,0:T(8,128)(2,1)}, bf16[2,12,32,128]{3,2,1,0:T(8,128)(2,1)S(1)}, u32[]{:S(2)}, u32[]{:S(2)}) collective-permute-start(bf16[2,12,32,128]{3,2,1,0:T(8,128)(2,1)} %refs_3_.1), channel_id=1, source_target_pairs={{0,1},{1,0},{2,3},{3,2},{4,5},{5,4},{6,7},{7,6},{8,9},{9,8},{10,11... | collective-permute-start | bytes 589832 | tf_op jit(solution)/shard_map/ppermute | solution.py:131
  20.7 6.0 %collective-permute-start = (f32[12,16]{1,0:T(8,128)}, f32[12,16]{1,0:T(8,128)S(1)}, u32[]{:S(2)}, u32[]{:S(2)}) collective-permute-start(f32[12,16]{1,0:T(8,128)} %refs_0_.7), channel_id=1, source_target_pairs={{0,1},{1,0},{2,3},{3,2},{4,5},{5,4},{6,7},{7,6},{8,9},{9,8},{10,11... | collective-permute-start | bytes 2312 | tf_op jit(solution)/shard_map/ppermute | solution.py:131
  21.2 13.1 %collective-permute-start.10 = (bf16[2,12,32,128]{3,2,1,0:T(8,128)(2,1)}, bf16[2,12,32,128]{3,2,1,0:T(8,128)(2,1)S(1)}, u32[]{:S(2)}, u32[]{:S(2)}) collective-permute-start(bf16[2,12,32,128]{3,2,1,0:T(8,128)(2,1)} %refs_3_.1), channel_id=1, source_target_pairs={{0,8},{4,12},{8,0},{12,4},{1,9},{5,13},{9,1},{13,5},{2,10},{6,14},... | collective-permute-start | bytes 589832 | tf_op jit(solution)/shard_map/ppermute | solution.py:131
  24.7 22.4 %collective-permute-start.8 = (bf16[2,12,32,128]{3,2,1,0:T(8,128)(2,1)}, bf16[2,12,32,128]{3,2,1,0:T(8,128)(2,1)S(1)}, u32[]{:S(2)}, u32[]{:S(2)}) collective-permute-start(bf16[2,12,32,128]{3,2,1,0:T(8,128)(2,1)} %refs_3_.1), channel_id=1, source_target_pairs={{0,4},{4,0},{8,12},{12,8},{1,5},{5,1},{9,13},{13,9},{2,6},{6,2},{1... | collective-permute-start | bytes 589832 | tf_op jit(solution)/shard_map/ppermute | solution.py:131
  26.7 7.6 %collective-permute-start.9 = (bf16[2,2,128,128]{3,2,1,0:T(8,128)(2,1)S(1)}, bf16[2,2,128,128]{3,2,1,0:T(8,128)(2,1)S(1)}, u32[]{:S(2)}, u32[]{:S(2)}) collective-permute-start(bf16[2,2,128,128]{3,2,1,0:T(8,128)(2,1)S(1)} %collective-permute-done.6), channel_id=1, source_target_pairs={{0,2},{1,3},{2,0},{3,1},{4,6},{5,7},{6,4},{7,5},{8,10},{9,11},{10,... | collective-permute-start | bytes 393224 | tf_op jit(solution)/shard_map/ppermute | solution.py:131
  28.2 13.5 %collective-permute-start.7 = (bf16[2,2,128,128]{3,2,1,0:T(8,128)(2,1)S(1)}, bf16[2,2,128,128]{3,2,1,0:T(8,128)(2,1)S(1)}, u32[]{:S(2)}, u32[]{:S(2)}) collective-permute-start(bf16[2,2,128,128]{3,2,1,0:T(8,128)(2,1)S(1)} %collective-permute-done.4), channel_id=1, source_target_pairs={{0,2},{1,3},{2,0},{3,1},{4,6},{5,7},{6,4},{7,5},{8,10},{9,11},{10,... | collective-permute-start | bytes 393224 | tf_op jit(solution)/shard_map/ppermute | solution.py:131
  28.8 1.1 %copy-start.3 = (bf16[2,12,128,128]{3,2,1,0:T(8,128)(2,1)S(1)}, bf16[2,12,128,128]{3,2,1,0:T(8,128)(2,1)}, u32[]{:S(2)}) copy-start(bf16[2,12,128,128]{3,2,1,0:T(8,128)(2,1)} %refs_8_.5) | copy-start | bytes 2359300
  29.9 6.4 %copy-start.4 = (bf16[2,12,128,128]{3,2,1,0:T(8,128)(2,1)S(1)}, bf16[2,12,128,128]{3,2,1,0:T(8,128)(2,1)}, u32[]{:S(2)}) copy-start(bf16[2,12,128,128]{3,2,1,0:T(8,128)(2,1)} %refs_8_.5) | copy-start | bytes 2359300
  32.8 5.6 %copy-start.1 = (bf16[8,2,8,128]{3,2,1,0:T(8,128)(2,1)}, bf16[8,2,8,128]{3,2,1,0:T(8,128)(2,1)S(1)}, u32[]{:S(2)}) copy-start(bf16[8,2,8,128]{3,2,1,0:T(8,128)(2,1)S(1)} %get-tuple-element.29.refs_0_) | copy-start | bytes 98308
  34.3 1.5 %collective-permute-start.13 = (bf16[4,2,128,128]{3,2,1,0:T(8,128)(2,1)S(1)}, bf16[4,2,128,128]{3,2,1,0:T(8,128)(2,1)S(1)}, u32[]{:S(2)}, u32[]{:S(2)}) collective-permute-start(bf16[4,2,128,128]{3,2,1,0:T(8,128)(2,1)S(1)} %pad_maximum_fusion.2), channel_id=1, source_target_pairs={{0,1},{1,0},{2,3},{3,2},{4,5},{5,4},{6,7},{7,6},{8,9},{9,8},{10,11... | collective-permute-start | bytes 786440 | tf_op jit(solution)/shard_map/ppermute | solution.py:131
  34.3 7.4 %collective-permute-start.11 = (bf16[2,12,32,128]{3,2,1,0:T(8,128)(2,1)S(1)}, bf16[2,12,32,128]{3,2,1,0:T(8,128)(2,1)S(1)}, u32[]{:S(2)}, u32[]{:S(2)}) collective-permute-start(bf16[2,12,32,128]{3,2,1,0:T(8,128)(2,1)S(1)} %collective-permute-done.10.refs_6_), channel_id=1, source_target_pairs={{0,4},{4,0},{8,12},{12,8},{1,5},{5,1},{9,13},{13,9},{2,6},{6,2},{1... | collective-permute-start | bytes 589832 | tf_op jit(solution)/shard_map/ppermute | solution.py:131
  34.4 2.0 %collective-permute-start.14 = (bf16[2,12,32,128]{3,2,1,0:T(8,128)(2,1)S(1)}, bf16[2,12,32,128]{3,2,1,0:T(8,128)(2,1)S(1)}, u32[]{:S(2)}, u32[]{:S(2)}) collective-permute-start(bf16[2,12,32,128]{3,2,1,0:T(8,128)(2,1)S(1)} %collective-permute-done.10.refs_6_), channel_id=1, source_target_pairs={{0,1},{1,0},{2,3},{3,2},{4,5},{5,4},{6,7},{7,6},{8,9},{9,8},{10,11... | collective-permute-start | bytes 589832 | tf_op jit(solution)/shard_map/ppermute | solution.py:131
  35.8 6.6 %collective-permute-start.3 = (bf16[8,2,8,128]{3,2,1,0:T(8,128)(2,1)S(1)}, bf16[8,2,8,128]{3,2,1,0:T(8,128)(2,1)S(1)}, u32[]{:S(2)}, u32[]{:S(2)}) collective-permute-start(bf16[8,2,8,128]{3,2,1,0:T(8,128)(2,1)S(1)} %get-tuple-element.30), channel_id=1, source_target_pairs={{0,2},{1,3},{2,0},{3,1},{4,6},{5,7},{6,4},{7,5},{8,10},{9,11},{10,... | collective-permute-start | bytes 98312 | tf_op jit(solution)/shard_map/ppermute | solution.py:131
  41.7 3.3 %collective-permute-start.15 = (bf16[4,2,128,128]{3,2,1,0:T(8,128)(2,1)S(1)}, bf16[4,2,128,128]{3,2,1,0:T(8,128)(2,1)S(1)}, u32[]{:S(2)}, u32[]{:S(2)}) collective-permute-start(bf16[4,2,128,128]{3,2,1,0:T(8,128)(2,1)S(1)} %pad_maximum_fusion.1), channel_id=1, source_target_pairs={{0,1},{1,0},{2,3},{3,2},{4,5},{5,4},{6,7},{7,6},{8,9},{9,8},{10,11... | collective-permute-start | bytes 786440 | tf_op jit(solution)/shard_map/ppermute | solution.py:131
  41.7 7.7 %collective-permute-start.18 = (bf16[8,2,8,128]{3,2,1,0:T(8,128)(2,1)S(1)}, bf16[8,2,8,128]{3,2,1,0:T(8,128)(2,1)S(1)}, u32[]{:S(2)}, u32[]{:S(2)}) collective-permute-start(bf16[8,2,8,128]{3,2,1,0:T(8,128)(2,1)S(1)} %get-tuple-element.41), channel_id=1, source_target_pairs={{0,8},{4,12},{8,0},{12,4},{1,9},{5,13},{9,1},{13,5},{2,10},{6,14},... | collective-permute-start | bytes 98312 | tf_op jit(solution)/shard_map/ppermute | solution.py:131
  42.1 2.9 %collective-permute-start.16 = (bf16[2,12,32,128]{3,2,1,0:T(8,128)(2,1)S(1)}, bf16[2,12,32,128]{3,2,1,0:T(8,128)(2,1)S(1)}, u32[]{:S(2)}, u32[]{:S(2)}) collective-permute-start(bf16[2,12,32,128]{3,2,1,0:T(8,128)(2,1)S(1)} %collective-permute-done.11.refs_6_), channel_id=1, source_target_pairs={{0,1},{1,0},{2,3},{3,2},{4,5},{5,4},{6,7},{7,6},{8,9},{9,8},{10,11... | collective-permute-start | bytes 589832 | tf_op jit(solution)/shard_map/ppermute | solution.py:131
  42.4 4.7 %copy-start.8 = (bf16[8,2,8,128]{3,2,1,0:T(8,128)(2,1)}, bf16[8,2,8,128]{3,2,1,0:T(8,128)(2,1)S(1)}, u32[]{:S(2)}) copy-start(bf16[8,2,8,128]{3,2,1,0:T(8,128)(2,1)S(1)} %collective-permute-done.3.refs_1_) | copy-start | bytes 98308
  42.4 7.0 %collective-permute-start.19 = (bf16[8,2,8,128]{3,2,1,0:T(8,128)(2,1)S(1)}, bf16[8,2,8,128]{3,2,1,0:T(8,128)(2,1)S(1)}, u32[]{:S(2)}, u32[]{:S(2)}) collective-permute-start(bf16[8,2,8,128]{3,2,1,0:T(8,128)(2,1)S(1)} %get-tuple-element.48), channel_id=1, source_target_pairs={{0,10},{1,11},{2,8},{3,9},{4,14},{5,15},{6,12},{7,13},{8,2},{9,3},... | collective-permute-start | bytes 98312 | tf_op jit(solution)/shard_map/ppermute | solution.py:143
  47.1 5.2 %collective-permute-start.17 = (bf16[4,2,128,128]{3,2,1,0:T(8,128)(2,1)S(1)}, bf16[4,2,128,128]{3,2,1,0:T(8,128)(2,1)S(1)}, u32[]{:S(2)}, u32[]{:S(2)}) collective-permute-start(bf16[4,2,128,128]{3,2,1,0:T(8,128)(2,1)S(1)} %pad_maximum_fusion), channel_id=1, source_target_pairs={{0,1},{1,0},{2,3},{3,2},{4,5},{5,4},{6,7},{7,6},{8,9},{9,8},{10,11... | collective-permute-start | bytes 786440 | tf_op jit(solution)/shard_map/ppermute | solution.py:131
  47.1 9.3 %collective-permute-start.23 = (bf16[8,2,8,128]{3,2,1,0:T(8,128)(2,1)S(1)}, bf16[8,2,8,128]{3,2,1,0:T(8,128)(2,1)S(1)}, u32[]{:S(2)}, u32[]{:S(2)}) collective-permute-start(bf16[8,2,8,128]{3,2,1,0:T(8,128)(2,1)S(1)} %get-tuple-element.45), channel_id=1, source_target_pairs={{0,12},{4,8},{8,4},{12,0},{1,13},{5,9},{9,5},{13,1},{2,14},{6,10},... | collective-permute-start | bytes 98312 | tf_op jit(solution)/shard_map/ppermute | solution.py:131
  49.2 3.0 %collective-permute-start.20 = (bf16[2,12,32,128]{3,2,1,0:T(8,128)(2,1)S(1)}, bf16[2,12,32,128]{3,2,1,0:T(8,128)(2,1)S(1)}, u32[]{:S(2)}, u32[]{:S(2)}) collective-permute-start(bf16[2,12,32,128]{3,2,1,0:T(8,128)(2,1)S(1)} %collective-permute-done.8.refs_6_), channel_id=1, source_target_pairs={{0,1},{1,0},{2,3},{3,2},{4,5},{5,4},{6,7},{7,6},{8,9},{9,8},{10,11... | collective-permute-start | bytes 589832 | tf_op jit(solution)/shard_map/ppermute | solution.py:131
  49.4 4.9 %copy-start.9 = (bf16[8,2,8,128]{3,2,1,0:T(8,128)(2,1)}, bf16[8,2,8,128]{3,2,1,0:T(8,128)(2,1)S(1)}, u32[]{:S(2)}) copy-start(bf16[8,2,8,128]{3,2,1,0:T(8,128)(2,1)S(1)} %collective-permute-done.18.refs_4_) | copy-start | bytes 98308
  49.4 4.9 %copy-start.10 = (bf16[8,2,8,128]{3,2,1,0:T(8,128)(2,1)}, bf16[8,2,8,128]{3,2,1,0:T(8,128)(2,1)S(1)}, u32[]{:S(2)}) copy-start(bf16[8,2,8,128]{3,2,1,0:T(8,128)(2,1)S(1)} %collective-permute-done.19.refs_5_) | copy-start | bytes 98308
  49.4 7.0 %collective-permute-start.24 = (bf16[8,2,8,128]{3,2,1,0:T(8,128)(2,1)S(1)}, bf16[8,2,8,128]{3,2,1,0:T(8,128)(2,1)S(1)}, u32[]{:S(2)}, u32[]{:S(2)}) collective-permute-start(bf16[8,2,8,128]{3,2,1,0:T(8,128)(2,1)S(1)} %get-tuple-element.52), channel_id=1, source_target_pairs={{0,14},{1,15},{2,12},{3,13},{4,10},{5,11},{6,8},{7,9},{8,6},{9,7},... | collective-permute-start | bytes 98312 | tf_op jit(solution)/shard_map/ppermute | solution.py:143
  54.3 4.0 %collective-permute-start.21 = (bf16[8,2,8,128]{3,2,1,0:T(8,128)(2,1)S(1)}, bf16[8,2,8,128]{3,2,1,0:T(8,128)(2,1)S(1)}, u32[]{:S(2)}, u32[]{:S(2)}) collective-permute-start(bf16[8,2,8,128]{3,2,1,0:T(8,128)(2,1)S(1)} %get-tuple-element.50), channel_id=1, source_target_pairs={{0,4},{4,0},{8,12},{12,8},{1,5},{5,1},{9,13},{13,9},{2,6},{6,2},{1... | collective-permute-start | bytes 98312 | tf_op jit(solution)/shard_map/ppermute | solution.py:131
  54.4 4.9 %collective-permute-start.22 = (bf16[8,2,8,128]{3,2,1,0:T(8,128)(2,1)S(1)}, bf16[8,2,8,128]{3,2,1,0:T(8,128)(2,1)S(1)}, u32[]{:S(2)}, u32[]{:S(2)}) collective-permute-start(bf16[8,2,8,128]{3,2,1,0:T(8,128)(2,1)S(1)} %get-tuple-element.51), channel_id=1, source_target_pairs={{0,6},{1,7},{2,4},{3,5},{4,2},{5,3},{6,0},{7,1},{8,14},{9,15},{10,... | collective-permute-start | bytes 98312 | tf_op jit(solution)/shard_map/ppermute | solution.py:143
  56.4 2.9 %copy-start.11 = (bf16[8,2,8,128]{3,2,1,0:T(8,128)(2,1)}, bf16[8,2,8,128]{3,2,1,0:T(8,128)(2,1)S(1)}, u32[]{:S(2)}) copy-start(bf16[8,2,8,128]{3,2,1,0:T(8,128)(2,1)S(1)} %collective-permute-done.23.refs_6_) | copy-start | bytes 98308
  56.4 2.9 %copy-start.12 = (bf16[8,2,8,128]{3,2,1,0:T(8,128)(2,1)}, bf16[8,2,8,128]{3,2,1,0:T(8,128)(2,1)S(1)}, u32[]{:S(2)}) copy-start(bf16[8,2,8,128]{3,2,1,0:T(8,128)(2,1)S(1)} %collective-permute-done.24.refs_7_) | copy-start | bytes 98308
  58.3 1.0 %copy-start.13 = (bf16[8,2,8,128]{3,2,1,0:T(8,128)(2,1)}, bf16[8,2,8,128]{3,2,1,0:T(8,128)(2,1)S(1)}, u32[]{:S(2)}) copy-start(bf16[8,2,8,128]{3,2,1,0:T(8,128)(2,1)S(1)} %collective-permute-done.21.refs_2_) | copy-start | bytes 98308
  59.3 0.6 copy-start.14

commit v4 on v3

--- a/solution.py
+++ b/solution.py
@@ -332,7 +332,7 @@
         + [VMEM] * (2 * NEAR),
         out_specs=[VMEM, VMEM],
         scratch_shapes=scratch,
-        compiler_params=pltpu.CompilerParams(vmem_limit_bytes=32 << 20),
+        compiler_params=pltpu.CompilerParams(vmem_limit_bytes=24 << 20),
         cost_estimate=pl.CostEstimate(
             flops=3 << 30, bytes_accessed=4 << 20, transcendentals=0
         ),
@@ -341,14 +341,9 @@
 
 
 def unpack_kernel(devices, partner, *refs):
-    chunks, (out, held, counts, table, sems) = refs[: 2 * devices], refs[2 * devices :]
+    chunks, (out, counts, table) = refs[: 2 * devices], refs[2 * devices :]
     capacity = SEC_DEV * STATES // devices
     me = lax.axis_index("sec")
-    copies = []
-    for i in range(2 * devices):
-        copy = pltpu.make_async_copy(chunks[i], held.at[i], sems.at[i])
-        copy.start()
-        copies.append(copy)
     for owner in range(devices):
         counts[owner] = 0
 
@@ -360,12 +355,10 @@
         return carry
 
     lax.fori_loop(0, SEC_DEV * STATES, place, 0, unroll=True)
-    for copy in copies:
-        copy.wait()
     for step in range(devices):
         for rank in range(capacity):
-            near = held[2 * step, rank].astype(jnp.float32)
-            far = held[2 * step + 1, rank].astype(jnp.float32)
+            near = chunks[2 * step][rank].astype(jnp.float32)
+            far = chunks[2 * step + 1][rank].astype(jnp.float32)
             out[table[(me ^ step) * capacity + rank]] = (near + far).astype(jnp.bfloat16)
 
 
@@ -373,14 +366,13 @@
     return pl.pallas_call(
         functools.partial(unpack_kernel, devices),
         out_shape=jax.ShapeDtypeStruct((SEC_DEV * STATES,) + chunks[0].shape[1:], jnp.bfloat16),
-        in_specs=[SMEM] + [ANY] * (2 * devices),
+        in_specs=[SMEM] + [VMEM] * (2 * devices),
         out_specs=VMEM,
         scratch_shapes=[
-            pltpu.VMEM((2 * devices,) + chunks[0].shape, RETURNED),
             pltpu.SMEM((devices,), jnp.int32),
             pltpu.SMEM((SEC_DEV * STATES,), jnp.int32),
-            pltpu.SemaphoreType.DMA((2 * devices,)),
         ],
+        compiler_params=pltpu.CompilerParams(vmem_limit_bytes=8 << 20),
         cost_estimate=pl.CostEstimate(flops=0, bytes_accessed=1 << 20, transcendentals=0),
         name="unpack",
     )(partner, *chunks)
@@ -402,18 +394,15 @@
             step, vectors, lefts, rights, coefs, sector_order, partner, devices, terms
         )
 
-    left_in = {}
-    held = {0: after(left_window, *every)}
-    bit = devices // 2
-    while bit:
-        for step in list(held):
-            held[step ^ bit] = left_in[step ^ bit] = exchange(held[step], "sec", bit)
-        bit //= 2
+    left_in = {2: exchange(left_window, "sec", 2)}
+    left_in[3] = exchange(after(left_in[2], *every), "sec", 1)
+    left_in[1] = exchange(after(left_window, *every), "sec", 1)
     keep, give = products(0, [wave], [left_window, exchange(left_window, "term", 1)])
     chunks = {0: (keep, exchange_both(give, 0, NEAR))}
+    first, cross_first = keep, chunks[0][1]
     waits = [keep]
     for step in steps:
-        x = exchange(after(arrived[step], *every), "term", NEAR)
+        x = exchange(after(arrived[step], left_in[2], arrived[2], first, cross_first), "term", NEAR)
         both = jnp.concatenate([arrived[step], x])
         both, left = lax.optimization_barrier((both, left_in[step], waits[0]))[:2]
         lefts = [left, exchange(left, "term", 1)]

time: 62.6 us -> 57.8 us (0.923)
  waiting for transfers between devices: 19 us -> 13.8 us
  local copies, waits for them, and re-layouts: 1.89 us -> 2.89 us
  Pallas kernels: 14.1 us -> 13.1 us
    ppermute x22, waiting for transfers between devices: 18 us -> 12.9 us  [exchange(): return lax.ppermute(x, axis, [(i, i ^ step) for i in range(size)])]
    ppermute x22, starting transfers between devices: 19.6 us -> 22.6 us  [exchange(): return lax.ppermute(x, axis, [(i, i ^ step) for i in range(size)])]
    ppermute x3, starting transfers between devices: 7.3 us -> 4.83 us  [exchange_both(): return lax.ppermute(x, ('sec', 'term'), pairs)]
    unnamed x30 -> x20, local copies, waits for them, and re-layouts: 1.78 us -> 2.78 us
    pallas_call x1, Pallas kernels: 2.35 us -> 1.45 us  [unpack(): pl.pallas_call(functools.partial(unpack_kernel, devices), out_shape=jax.S...]
  transfers between devices with their start and end apart: 25 -> 25, of which waited for: 7 -> 8; matrix products, arithmetic and copies ran while one was open for 0% -> 0% of each run, Pallas kernels for 19% -> 20%
where the time goes in v4:
time: 57.8 us; the launch traced here: 57.4 us
  starting transfers between devices  27.4 us (47%)
  waiting for transfers between devices  13.8 us (24%)
  Pallas kernels  13.1 us (23%)
  local copies, waits for them, and re-layouts  2.89 us (5%)
    ppermute x22, starting transfers between devices, exchange(): return lax.ppermute(x, axis, [(i, i ^ step) for i in range(size)])  22.6 us
    ppermute x22, waiting for transfers between devices, exchange(): return lax.ppermute(x, axis, [(i, i ^ step) for i in range(size)])  12.9 us
    pallas_call x4, Pallas kernels, compute(): pl.pallas_call(functools.partial(compute_kernel, step, devices, terms), o...  8.92 us
    ppermute x3, starting transfers between devices, exchange_both(): return lax.ppermute(x, ('sec', 'term'), pairs)  4.83 us
    unnamed x20, local copies, waits for them, and re-layouts  2.78 us
    pallas_call x1, Pallas kernels, pack(): pl.pallas_call(functools.partial(pack_kernel, devices, terms), out_shape=...  2.68 us
    pallas_call x1, Pallas kernels, unpack(): pl.pallas_call(functools.partial(unpack_kernel, devices), out_shape=jax.S...  1.45 us
  transfers between devices with their start and end apart: 25, of which 8 were waited for; matrix products, arithmetic and copies ran while one was open for 0% of the time, Pallas kernels for 20%

profile of v4, /device:TPU:0, one launch (start us, length us, event | category | flops | bytes accessed | tf_op | source)
XLA Modules:
  0.0 57.4 jit_solution(3884329609890108042)
XLA Ops:
  0.0 0.5 collective-permute-start.2
  0.5 0.1 collective-permute-start.1
  0.6 0.4 collective-permute-start
  1.0 3.7 %collective-permute-start.5 = (bf16[2,12,32,128]{3,2,1,0:T(8,128)(2,1)}, bf16[2,12,32,128]{3,2,1,0:T(8,128)(2,1)S(1)}, u32[]{:S(2)}, u32[]{:S(2)}) collective-permute-start(bf16[2,12,32,128]{3,2,1,0:T(8,128)(2,1)} %refs_3_.1), channel_id=1, source_target_pairs={{0,8},{4,12},{8,0},{12,4},{1,9},{5,13},{9,1},{13,5},{2,10},{6,14},... | collective-permute-start | bytes 589832 | tf_op jit(solution)/shard_map/ppermute | solution.py:131
  4.7 2.7 %pack.1 = (bf16[2,2,128,128]{3,2,1,0:T(8,128)(2,1)}, bf16[2,2,128,128]{3,2,1,0:T(8,128)(2,1)}, bf16[2,2,128,128]{3,2,1,0:T(8,128)(2,1)}) custom-call(s32[8,16]{1,0:T(8,128)} %partner.11, bf16[32,2,128,128]{3,2,1,0:T(8,128)(2,1)} %bitcast.2), custom_call_target="tpu_custom_call" | custom-call | bytes 4194304 | tf_op jit(solution)/shard_map/pack/pallas_call | solution.py:190
  7.4 0.1 collective-permute-start.6
  7.5 0.0 collective-permute-done.refs_1_
  7.5 0.0 collective-permute-done.1.refs_4_
  7.5 0.0 copy-start.2
  7.5 1.1 %copy-done.2 = bf16[2,12,128,128]{3,2,1,0:T(8,128)(2,1)S(1)} copy-done((bf16[2,12,128,128]{3,2,1,0:T(8,128)(2,1)S(1)}, bf16[2,12,128,128]{3,2,1,0:T(8,128)(2,1)}, u32[]{:S(2)}) %copy-start.2) | copy-done | bytes 786456
  8.7 0.9 %copy-done.4 = bf16[2,12,32,128]{3,2,1,0:T(8,128)(2,1)S(1)} copy-done((bf16[2,12,32,128]{3,2,1,0:T(8,128)(2,1)S(1)}, bf16[2,12,32,128]{3,2,1,0:T(8,128)(2,1)}, u32[]{:S(2)}) %copy-start.4) | copy-done | bytes 196632
  9.6 0.7 %copy-done.6 = f32[12,16]{1,0:T(8,128)S(1)} copy-done((f32[12,16]{1,0:T(8,128)S(1)}, f32[12,16]{1,0:T(8,128)}, u32[]{:S(2)}) %copy-start.6) | copy-done | bytes 792
  10.3 2.8 %products_0.1 = (bf16[8,2,8,128]{3,2,1,0:T(8,128)(2,1)S(1)}, bf16[8,2,8,128]{3,2,1,0:T(8,128)(2,1)S(1)}) custom-call(s32[8,16]{1,0:T(8,128)S(1)} %copy-done.1, s32[8]{0:T(128)S(1)} %copy-done.7, f32[12,16]{1,0:T(8,128)S(1)} %copy-done.6, f32[12,16]{1,0:T(8,128)S(1)} %collective-permute-done.refs_1_, bf16[32,2,128,128]{3,2,1,0:T(8,128)(2,1)S(1)} %bitcast.3, ...), custom_call_target="tpu_custom_call" | custom-call | flops 3221225472 | bytes 4194304 | tf_op jit(solution)/shard_map/products_0/pallas_call | solution.py:327
  13.1 0.0 copy-start.3
  13.2 1.9 %collective-permute-start.3 = (bf16[8,2,8,128]{3,2,1,0:T(8,128)(2,1)S(1)}, bf16[8,2,8,128]{3,2,1,0:T(8,128)(2,1)S(1)}, u32[]{:S(2)}, u32[]{:S(2)}) collective-permute-start(bf16[8,2,8,128]{3,2,1,0:T(8,128)(2,1)S(1)} %get-tuple-element.31), channel_id=1, source_target_pairs={{0,2},{1,3},{2,0},{3,1},{4,6},{5,7},{6,4},{7,5},{8,10},{9,11},{10,... | collective-permute-start | bytes 98312 | tf_op jit(solution)/shard_map/ppermute | solution.py:131
  15.0 3.6 %collective-permute-start.8 = (bf16[2,2,128,128]{3,2,1,0:T(8,128)(2,1)S(1)}, bf16[2,2,128,128]{3,2,1,0:T(8,128)(2,1)S(1)}, u32[]{:S(2)}, u32[]{:S(2)}) collective-permute-start(bf16[2,2,128,128]{3,2,1,0:T(8,128)(2,1)S(1)} %copy-done.9), channel_id=1, source_target_pairs={{0,12},{4,8},{8,4},{12,0},{1,13},{5,9},{9,5},{13,1},{2,14},{6,10},... | collective-permute-start | bytes 393224 | tf_op jit(solution)/shard_map/ppermute | solution.py:131
  18.6 0.0 collective-permute-start.4
  18.6 4.7 %collective-permute-done.6 = bf16[2,2,128,128]{3,2,1,0:T(8,128)(2,1)S(1)} collective-permute-done((bf16[2,2,128,128]{3,2,1,0:T(8,128)(2,1)}, bf16[2,2,128,128]{3,2,1,0:T(8,128)(2,1)S(1)}, u32[]{:S(2)}, u32[]{:S(2)}) %collective-permute-start.6) | collective-permute-done | bytes 131104 | tf_op jit(solution)/shard_map/ppermute | solution.py:131
  23.3 0.0 collective-permute-done.5.refs_6_
  23.3 0.0 collective-permute-done.3.refs_1_
  23.3 1.8 %collective-permute-start.12 = (bf16[2,2,128,128]{3,2,1,0:T(8,128)(2,1)S(1)}, bf16[2,2,128,128]{3,2,1,0:T(8,128)(2,1)S(1)}, u32[]{:S(2)}, u32[]{:S(2)}) collective-permute-start(bf16[2,2,128,128]{3,2,1,0:T(8,128)(2,1)S(1)} %collective-permute-done.6), channel_id=1, source_target_pairs={{0,2},{1,3},{2,0},{3,1},{4,6},{5,7},{6,4},{7,5},{8,10},{9,11},{10,... | collective-permute-start | bytes 393224 | tf_op jit(solution)/shard_map/ppermute | solution.py:131
  25.1 0.0 collective-permute-done.8
  25.1 0.3 collective-permute-start.10
  25.4 0.5 collective-permute-done.4
  25.9 2.3 %collective-permute-start.9 = (bf16[2,12,32,128]{3,2,1,0:T(8,128)(2,1)S(1)}, bf16[2,12,32,128]{3,2,1,0:T(8,128)(2,1)S(1)}, u32[]{:S(2)}, u32[]{:S(2)}) collective-permute-start(bf16[2,12,32,128]{3,2,1,0:T(8,128)(2,1)S(1)} %copy-done.5), channel_id=1, source_target_pairs={{0,4},{4,0},{8,12},{12,8},{1,5},{5,1},{9,13},{13,9},{2,6},{6,2},{1... | collective-permute-start | bytes 589832 | tf_op jit(solution)/shard_map/ppermute | solution.py:131
  28.2 0.1 collective-permute-start.11
  28.2 1.2 %collective-permute-start.7 = (bf16[2,2,128,128]{3,2,1,0:T(8,128)(2,1)S(1)}, bf16[2,2,128,128]{3,2,1,0:T(8,128)(2,1)S(1)}, u32[]{:S(2)}, u32[]{:S(2)}) collective-permute-start(bf16[2,2,128,128]{3,2,1,0:T(8,128)(2,1)S(1)} %collective-permute-done.4), channel_id=1, source_target_pairs={{0,2},{1,3},{2,0},{3,1},{4,6},{5,7},{6,4},{7,5},{8,10},{9,11},{10,... | collective-permute-start | bytes 393224 | tf_op jit(solution)/shard_map/ppermute | solution.py:131
  29.4 0.0 collective-permute-done.12
  29.5 0.1 collective-permute-start.13
  29.6 1.8 %collective-permute-done.10 = bf16[2,2,128,128]{3,2,1,0:T(8,128)(2,1)S(1)} collective-permute-done((bf16[2,2,128,128]{3,2,1,0:T(8,128)(2,1)S(1)}, bf16[2,2,128,128]{3,2,1,0:T(8,128)(2,1)S(1)}, u32[]{:S(2)}, u32[]{:S(2)}) %collective-permute-start.10) | collective-permute-done | bytes 131104 | tf_op jit(solution)/shard_map/ppermute | solution.py:131
  31.4 1.3 %collective-permute-done.14.refs_7_ = bf16[2,12,32,128]{3,2,1,0:T(8,128)(2,1)S(1)} collective-permute-done((bf16[2,12,32,128]{3,2,1,0:T(8,128)(2,1)S(1)}, bf16[2,12,32,128]{3,2,1,0:T(8,128)(2,1)S(1)}, u32[]{:S(2)}, u32[]{:S(2)}) %collective-permute-start.14) | collective-permute-done | bytes 196640 | tf_op jit(solution)/shard_map/ppermute | solution.py:131
  32.8 2.0 %products_2.1 = (bf16[8,2,8,128]{3,2,1,0:T(8,128)(2,1)S(1)}, bf16[8,2,8,128]{3,2,1,0:T(8,128)(2,1)S(1)}) custom-call(s32[8,16]{1,0:T(8,128)S(1)} %copy-done.1, s32[8]{0:T(128)S(1)} %copy-done.7, f32[12,16]{1,0:T(8,128)S(1)} %copy-done.6, f32[12,16]{1,0:T(8,128)S(1)} %collective-permute-done.refs_1_, bf16[2,2,128,128]{3,2,1,0:T(8,128)(2,1)S(1)} %get-tuple-element.66.refs_2_, ...), custom_call_target="tpu_custom_call" | custom-call | flops 3221225472 | bytes 4194304 | tf_op jit(solution)/shard_map/products_2/pallas_call | solution.py:327
  34.8 2.4 %collective-permute-done.11.refs_6_ = bf16[2,12,32,128]{3,2,1,0:T(8,128)(2,1)S(1)} collective-permute-done((bf16[2,12,32,128]{3,2,1,0:T(8,128)(2,1)S(1)}, bf16[2,12,32,128]{3,2,1,0:T(8,128)(2,1)S(1)}, u32[]{:S(2)}, u32[]{:S(2)}) %collective-permute-start.11) | collective-permute-done | bytes 196640 | tf_op jit(solution)/shard_map/ppermute | solution.py:131
  37.2 3.7 %collective-permute-start.18 = (bf16[8,2,8,128]{3,2,1,0:T(8,128)(2,1)S(1)}, bf16[8,2,8,128]{3,2,1,0:T(8,128)(2,1)S(1)}, u32[]{:S(2)}, u32[]{:S(2)}) collective-permute-start(bf16[8,2,8,128]{3,2,1,0:T(8,128)(2,1)S(1)} %get-tuple-element.43), channel_id=1, source_target_pairs={{0,8},{4,12},{8,0},{12,4},{1,9},{5,13},{9,1},{13,5},{2,10},{6,14},... | collective-permute-start | bytes 98312 | tf_op jit(solution)/shard_map/ppermute | solution.py:131
  41.0 0.2 collective-permute-start.16
  41.2 0.3 collective-permute-start.19
  41.6 0.8 %collective-permute-done.16.refs_7_ = bf16[2,12,32,128]{3,2,1,0:T(8,128)(2,1)S(1)} collective-permute-done((bf16[2,12,32,128]{3,2,1,0:T(8,128)(2,1)S(1)}, bf16[2,12,32,128]{3,2,1,0:T(8,128)(2,1)S(1)}, u32[]{:S(2)}, u32[]{:S(2)}) %collective-permute-start.16) | collective-permute-done | bytes 196640 | tf_op jit(solution)/shard_map/ppermute | solution.py:131
  42.4 2.0 %products_3.1 = (bf16[8,2,8,128]{3,2,1,0:T(8,128)(2,1)S(1)}, bf16[8,2,8,128]{3,2,1,0:T(8,128)(2,1)S(1)}) custom-call(s32[8,16]{1,0:T(8,128)S(1)} %copy-done.1, s32[8]{0:T(128)S(1)} %copy-done.7, f32[12,16]{1,0:T(8,128)S(1)} %copy-done.6, f32[12,16]{1,0:T(8,128)S(1)} %collective-permute-done.refs_1_, bf16[2,2,128,128]{3,2,1,0:T(8,128)(2,1)S(1)} %get-tuple-element.62.refs_2_, ...), custom_call_target="tpu_custom_call" | custom-call | flops 3221225472 | bytes 4194304 | tf_op jit(solution)/shard_map/products_3/pallas_call | solution.py:327
  44.4 0.3 collective-permute-start.17
  44.7 2.1 %collective-permute-start.23 = (bf16[8,2,8,128]{3,2,1,0:T(8,128)(2,1)S(1)}, bf16[8,2,8,128]{3,2,1,0:T(8,128)(2,1)S(1)}, u32[]{:S(2)}, u32[]{:S(2)}) collective-permute-start(bf16[8,2,8,128]{3,2,1,0:T(8,128)(2,1)S(1)} %get-tuple-element.47), channel_id=1, source_target_pairs={{0,12},{4,8},{8,4},{12,0},{1,13},{5,9},{9,5},{13,1},{2,14},{6,10},... | collective-permute-start | bytes 98312 | tf_op jit(solution)/shard_map/ppermute | solution.py:131
  46.9 0.2 collective-permute-start.20
  47.1 1.6 %collective-permute-start.24 = (bf16[8,2,8,128]{3,2,1,0:T(8,128)(2,1)S(1)}, bf16[8,2,8,128]{3,2,1,0:T(8,128)(2,1)S(1)}, u32[]{:S(2)}, u32[]{:S(2)}) collective-permute-start(bf16[8,2,8,128]{3,2,1,0:T(8,128)(2,1)S(1)} %get-tuple-element.54), channel_id=1, source_target_pairs={{0,14},{1,15},{2,12},{3,13},{4,10},{5,11},{6,8},{7,9},{8,6},{9,7},... | collective-permute-start | bytes 98312 | tf_op jit(solution)/shard_map/ppermute | solution.py:143
  48.8 2.0 %products_1.1 = (bf16[8,2,8,128]{3,2,1,0:T(8,128)(2,1)S(1)}, bf16[8,2,8,128]{3,2,1,0:T(8,128)(2,1)S(1)}) custom-call(s32[8,16]{1,0:T(8,128)S(1)} %copy-done.1, s32[8]{0:T(128)S(1)} %copy-done.7, f32[12,16]{1,0:T(8,128)S(1)} %copy-done.6, f32[12,16]{1,0:T(8,128)S(1)} %collective-permute-done.refs_1_, bf16[2,2,128,128]{3,2,1,0:T(8,128)(2,1)S(1)} %get-tuple-element.58.refs_2_, ...), custom_call_target="tpu_custom_call" | custom-call | flops 3221225472 | bytes 4194304 | tf_op jit(solution)/shard_map/products_1/pallas_call | solution.py:327
  50.8 0.1 collective-permute-start.21
  50.9 2.9 %collective-permute-start.22 = (bf16[8,2,8,128]{3,2,1,0:T(8,128)(2,1)S(1)}, bf16[8,2,8,128]{3,2,1,0:T(8,128)(2,1)S(1)}, u32[]{:S(2)}, u32[]{:S(2)}) collective-permute-start(bf16[8,2,8,128]{3,2,1,0:T(8,128)(2,1)S(1)} %get-tuple-element.53), channel_id=1, source_target_pairs={{0,6},{1,7},{2,4},{3,5},{4,2},{5,3},{6,0},{7,1},{8,14},{9,15},{10,... | collective-permute-start | bytes 98312 | tf_op jit(solution)/shard_map/ppermute | solution.py:143
  53.8 1.3 %collective-permute-done.21.refs_2_ = bf16[8,2,8,128]{3,2,1,0:T(8,128)(2,1)S(1)} collective-permute-done((bf16[8,2,8,128]{3,2,1,0:T(8,128)(2,1)S(1)}, bf16[8,2,8,128]{3,2,1,0:T(8,128)(2,1)S(1)}, u32[]{:S(2)}, u32[]{:S(2)}) %collective-permute-start.21) | collective-permute-done | bytes 32800 | tf_op jit(solution)/shard_map/ppermute | solution.py:131
  55.1 0.9 %collective-permute-done.22.refs_3_ = bf16[8,2,8,128]{3,2,1,0:T(8,128)(2,1)S(1)} collective-permute-done((bf16[8,2,8,128]{3,2,1,0:T(8,128)(2,1)S(1)}, bf16[8,2,8,128]{3,2,1,0:T(8,128)(2,1)S(1)}, u32[]{:S(2)}, u32[]{:S(2)}) %collective-permute-start.22) | collective-permute-done | bytes 32800 | tf_op jit(solution)/shard_map/ppermute | solution.py:143
  56.0 1.5 %unpack.1 = bf16[32,2,8,128]{3,2,1,0:T(8,128)(2,1)} custom-call(s32[8,16]{1,0:T(8,128)S(1)} %copy-done.1, bf16[8,2,8,128]{3,2,1,0:T(8,128)(2,1)S(1)} %get-tuple-element.30.refs_0_, bf16[8,2,8,128]{3,2,1,0:T(8,128)(2,1)S(1)} %collective-permute-done.3.refs_1_, bf16[8,2,8,128]{3,2,1,0:T(8,128)(2,1)S(1)} %collective-permute-done.21.refs_2_, ...), custom_call_target="tpu_custom_call" | custom-call | bytes 1048576 | tf_op jit(solution)/shard_map/unpack/pallas_call | solution.py:366
  (37 shorter events, 0.2 us)
Async XLA Ops:
  0.0 7.5 %copy-start = (bf16[2,16,2,128,128]{4,3,2,1,0:T(8,128)(2,1)S(1)}, bf16[2,16,2,128,128]{4,3,2,1,0:T(8,128)(2,1)}, u32[]{:S(2)}) copy-start(bf16[2,16,2,128,128]{4,3,2,1,0:T(8,128)(2,1)} %param.6) | copy-start | bytes 6291460
  0.0 7.5 %copy-start.1 = (s32[8,16]{1,0:T(8,128)S(1)}, s32[8,16]{1,0:T(8,128)}, u32[]{:S(2)}) copy-start(s32[8,16]{1,0:T(8,128)} %partner.11) | copy-start | bytes 1540
  0.0 7.5 %copy-start.7 = (s32[8]{0:T(128)S(1)}, s32[8]{0:T(128)}, u32[]{:S(2)}) copy-start(s32[8]{0:T(128)} %order.7) | copy-start | bytes 100
  0.0 7.5 %collective-permute-start.2 = (bf16[2,12,128,128]{3,2,1,0:T(8,128)(2,1)}, bf16[2,12,128,128]{3,2,1,0:T(8,128)(2,1)S(1)}, u32[]{:S(2)}, u32[]{:S(2)}) collective-permute-start(bf16[2,12,128,128]{3,2,1,0:T(8,128)(2,1)} %refs_8_.5), channel_id=1, source_target_pairs={{0,1},{1,0},{2,3},{3,2},{4,5},{5,4},{6,7},{7,6},{8,9},{9,8},{10,11... | collective-permute-start | bytes 2359304 | tf_op jit(solution)/shard_map/ppermute | solution.py:131
  0.5 7.0 %collective-permute-start.1 = (bf16[2,12,32,128]{3,2,1,0:T(8,128)(2,1)}, bf16[2,12,32,128]{3,2,1,0:T(8,128)(2,1)S(1)}, u32[]{:S(2)}, u32[]{:S(2)}) collective-permute-start(bf16[2,12,32,128]{3,2,1,0:T(8,128)(2,1)} %refs_3_.1), channel_id=1, source_target_pairs={{0,1},{1,0},{2,3},{3,2},{4,5},{5,4},{6,7},{7,6},{8,9},{9,8},{10,11... | collective-permute-start | bytes 589832 | tf_op jit(solution)/shard_map/ppermute | solution.py:131
  0.6 6.9 %collective-permute-start = (f32[12,16]{1,0:T(8,128)}, f32[12,16]{1,0:T(8,128)S(1)}, u32[]{:S(2)}, u32[]{:S(2)}) collective-permute-start(f32[12,16]{1,0:T(8,128)} %refs_0_.7), channel_id=1, source_target_pairs={{0,1},{1,0},{2,3},{3,2},{4,5},{5,4},{6,7},{7,6},{8,9},{9,8},{10,11... | collective-permute-start | bytes 2312 | tf_op jit(solution)/shard_map/ppermute | solution.py:131
  1.0 22.3 %collective-permute-start.5 = (bf16[2,12,32,128]{3,2,1,0:T(8,128)(2,1)}, bf16[2,12,32,128]{3,2,1,0:T(8,128)(2,1)S(1)}, u32[]{:S(2)}, u32[]{:S(2)}) collective-permute-start(bf16[2,12,32,128]{3,2,1,0:T(8,128)(2,1)} %refs_3_.1), channel_id=1, source_target_pairs={{0,8},{4,12},{8,0},{12,4},{1,9},{5,13},{9,1},{13,5},{2,10},{6,14},... | collective-permute-start | bytes 589832 | tf_op jit(solution)/shard_map/ppermute | solution.py:131
  7.4 16.0 %collective-permute-start.6 = (bf16[2,2,128,128]{3,2,1,0:T(8,128)(2,1)}, bf16[2,2,128,128]{3,2,1,0:T(8,128)(2,1)S(1)}, u32[]{:S(2)}, u32[]{:S(2)}) collective-permute-start(bf16[2,2,128,128]{3,2,1,0:T(8,128)(2,1)} %get-tuple-element.33), channel_id=1, source_target_pairs={{0,8},{4,12},{8,0},{12,4},{1,9},{5,13},{9,1},{13,5},{2,10},{6,14},... | collective-permute-start | bytes 393224 | tf_op jit(solution)/shard_map/ppermute | solution.py:131
  7.5 1.1 %copy-start.2 = (bf16[2,12,128,128]{3,2,1,0:T(8,128)(2,1)S(1)}, bf16[2,12,128,128]{3,2,1,0:T(8,128)(2,1)}, u32[]{:S(2)}) copy-start(bf16[2,12,128,128]{3,2,1,0:T(8,128)(2,1)} %refs_8_.5) | copy-start | bytes 2359300
  8.7 0.9 %copy-start.4 = (bf16[2,12,32,128]{3,2,1,0:T(8,128)(2,1)S(1)}, bf16[2,12,32,128]{3,2,1,0:T(8,128)(2,1)}, u32[]{:S(2)}) copy-start(bf16[2,12,32,128]{3,2,1,0:T(8,128)(2,1)} %refs_3_.1) | copy-start | bytes 589828
  9.6 0.7 %copy-start.6 = (f32[12,16]{1,0:T(8,128)S(1)}, f32[12,16]{1,0:T(8,128)}, u32[]{:S(2)}) copy-start(f32[12,16]{1,0:T(8,128)} %refs_0_.7) | copy-start | bytes 2308
  10.3 4.7 %copy-start.9 = (bf16[2,2,128,128]{3,2,1,0:T(8,128)(2,1)S(1)}, bf16[2,2,128,128]{3,2,1,0:T(8,128)(2,1)}, u32[]{:S(2)}) copy-start(bf16[2,2,128,128]{3,2,1,0:T(8,128)(2,1)} %get-tuple-element.35) | copy-start | bytes 393220
  10.3 8.3 %copy-start.8 = (bf16[2,2,128,128]{3,2,1,0:T(8,128)(2,1)S(1)}, bf16[2,2,128,128]{3,2,1,0:T(8,128)(2,1)}, u32[]{:S(2)}) copy-start(bf16[2,2,128,128]{3,2,1,0:T(8,128)(2,1)} %get-tuple-element.32) | copy-start | bytes 393220
  10.3 15.6 %copy-start.5 = (bf16[2,12,32,128]{3,2,1,0:T(8,128)(2,1)S(1)}, bf16[2,12,32,128]{3,2,1,0:T(8,128)(2,1)}, u32[]{:S(2)}) copy-start(bf16[2,12,32,128]{3,2,1,0:T(8,128)(2,1)} %refs_3_.1) | copy-start | bytes 589828
  13.1 19.6 %copy-start.3 = (bf16[2,12,128,128]{3,2,1,0:T(8,128)(2,1)S(1)}, bf16[2,12,128,128]{3,2,1,0:T(8,128)(2,1)}, u32[]{:S(2)}) copy-start(bf16[2,12,128,128]{3,2,1,0:T(8,128)(2,1)} %refs_8_.5) | copy-start | bytes 2359300
  13.2 10.2 %collective-permute-start.3 = (bf16[8,2,8,128]{3,2,1,0:T(8,128)(2,1)S(1)}, bf16[8,2,8,128]{3,2,1,0:T(8,128)(2,1)S(1)}, u32[]{:S(2)}, u32[]{:S(2)}) collective-permute-start(bf16[8,2,8,128]{3,2,1,0:T(8,128)(2,1)S(1)} %get-tuple-element.31), channel_id=1, source_target_pairs={{0,2},{1,3},{2,0},{3,1},{4,6},{5,7},{6,4},{7,5},{8,10},{9,11},{10,... | collective-permute-start | bytes 98312 | tf_op jit(solution)/shard_map/ppermute | solution.py:131
  15.0 10.1 %collective-permute-start.8 = (bf16[2,2,128,128]{3,2,1,0:T(8,128)(2,1)S(1)}, bf16[2,2,128,128]{3,2,1,0:T(8,128)(2,1)S(1)}, u32[]{:S(2)}, u32[]{:S(2)}) collective-permute-start(bf16[2,2,128,128]{3,2,1,0:T(8,128)(2,1)S(1)} %copy-done.9), channel_id=1, source_target_pairs={{0,12},{4,8},{8,4},{12,0},{1,13},{5,9},{9,5},{13,1},{2,14},{6,10},... | collective-permute-start | bytes 393224 | tf_op jit(solution)/shard_map/ppermute | solution.py:131
  18.6 7.2 %collective-permute-start.4 = (bf16[2,2,128,128]{3,2,1,0:T(8,128)(2,1)S(1)}, bf16[2,2,128,128]{3,2,1,0:T(8,128)(2,1)S(1)}, u32[]{:S(2)}, u32[]{:S(2)}) collective-permute-start(bf16[2,2,128,128]{3,2,1,0:T(8,128)(2,1)S(1)} %copy-done.8), channel_id=1, source_target_pairs={{0,4},{4,0},{8,12},{12,8},{1,5},{5,1},{9,13},{13,9},{2,6},{6,2},{1... | collective-permute-start | bytes 393224 | tf_op jit(solution)/shard_map/ppermute | solution.py:131
  23.3 6.1 %collective-permute-start.12 = (bf16[2,2,128,128]{3,2,1,0:T(8,128)(2,1)S(1)}, bf16[2,2,128,128]{3,2,1,0:T(8,128)(2,1)S(1)}, u32[]{:S(2)}, u32[]{:S(2)}) collective-permute-start(bf16[2,2,128,128]{3,2,1,0:T(8,128)(2,1)S(1)} %collective-permute-done.6), channel_id=1, source_target_pairs={{0,2},{1,3},{2,0},{3,1},{4,6},{5,7},{6,4},{7,5},{8,10},{9,11},{10,... | collective-permute-start | bytes 393224 | tf_op jit(solution)/shard_map/ppermute | solution.py:131
  25.1 6.2 %collective-permute-start.10 = (bf16[2,2,128,128]{3,2,1,0:T(8,128)(2,1)S(1)}, bf16[2,2,128,128]{3,2,1,0:T(8,128)(2,1)S(1)}, u32[]{:S(2)}, u32[]{:S(2)}) collective-permute-start(bf16[2,2,128,128]{3,2,1,0:T(8,128)(2,1)S(1)} %collective-permute-done.8), channel_id=1, source_target_pairs={{0,2},{1,3},{2,0},{3,1},{4,6},{5,7},{6,4},{7,5},{8,10},{9,11},{10,... | collective-permute-start | bytes 393224 | tf_op jit(solution)/shard_map/ppermute | solution.py:131
  25.9 18.6 %collective-permute-start.9 = (bf16[2,12,32,128]{3,2,1,0:T(8,128)(2,1)S(1)}, bf16[2,12,32,128]{3,2,1,0:T(8,128)(2,1)S(1)}, u32[]{:S(2)}, u32[]{:S(2)}) collective-permute-start(bf16[2,12,32,128]{3,2,1,0:T(8,128)(2,1)S(1)} %copy-done.5), channel_id=1, source_target_pairs={{0,4},{4,0},{8,12},{12,8},{1,5},{5,1},{9,13},{13,9},{2,6},{6,2},{1... | collective-permute-start | bytes 589832 | tf_op jit(solution)/shard_map/ppermute | solution.py:131
  28.2 9.0 %collective-permute-start.11 = (bf16[2,12,32,128]{3,2,1,0:T(8,128)(2,1)S(1)}, bf16[2,12,32,128]{3,2,1,0:T(8,128)(2,1)S(1)}, u32[]{:S(2)}, u32[]{:S(2)}) collective-permute-start(bf16[2,12,32,128]{3,2,1,0:T(8,128)(2,1)S(1)} %collective-permute-done.5.refs_6_), channel_id=1, source_target_pairs={{0,4},{4,0},{8,12},{12,8},{1,5},{5,1},{9,13},{13,9},{2,6},{6,2},{1... | collective-permute-start | bytes 589832 | tf_op jit(solution)/shard_map/ppermute | solution.py:131
  28.2 9.0 %collective-permute-start.7 = (bf16[2,2,128,128]{3,2,1,0:T(8,128)(2,1)S(1)}, bf16[2,2,128,128]{3,2,1,0:T(8,128)(2,1)S(1)}, u32[]{:S(2)}, u32[]{:S(2)}) collective-permute-start(bf16[2,2,128,128]{3,2,1,0:T(8,128)(2,1)S(1)} %collective-permute-done.4), channel_id=1, source_target_pairs={{0,2},{1,3},{2,0},{3,1},{4,6},{5,7},{6,4},{7,5},{8,10},{9,11},{10,... | collective-permute-start | bytes 393224 | tf_op jit(solution)/shard_map/ppermute | solution.py:131
  29.5 1.9 %collective-permute-start.13 = (bf16[4,2,128,128]{3,2,1,0:T(8,128)(2,1)S(1)}, bf16[4,2,128,128]{3,2,1,0:T(8,128)(2,1)S(1)}, u32[]{:S(2)}, u32[]{:S(2)}) collective-permute-start(bf16[4,2,128,128]{3,2,1,0:T(8,128)(2,1)S(1)} %pad_maximum_fusion.2), channel_id=1, source_target_pairs={{0,1},{1,0},{2,3},{3,2},{4,5},{5,4},{6,7},{7,6},{8,9},{9,8},{10,11... | collective-permute-start | bytes 786440 | tf_op jit(solution)/shard_map/ppermute | solution.py:131
  31.3 1.4 %collective-permute-start.14 = (bf16[2,12,32,128]{3,2,1,0:T(8,128)(2,1)S(1)}, bf16[2,12,32,128]{3,2,1,0:T(8,128)(2,1)S(1)}, u32[]{:S(2)}, u32[]{:S(2)}) collective-permute-start(bf16[2,12,32,128]{3,2,1,0:T(8,128)(2,1)S(1)} %collective-permute-done.5.refs_6_), channel_id=1, source_target_pairs={{0,1},{1,0},{2,3},{3,2},{4,5},{5,4},{6,7},{7,6},{8,9},{9,8},{10,11... | collective-permute-start | bytes 589832 | tf_op jit(solution)/shard_map/ppermute | solution.py:131
  37.2 4.3 %collective-permute-start.15 = (bf16[4,2,128,128]{3,2,1,0:T(8,128)(2,1)S(1)}, bf16[4,2,128,128]{3,2,1,0:T(8,128)(2,1)S(1)}, u32[]{:S(2)}, u32[]{:S(2)}) collective-permute-start(bf16[4,2,128,128]{3,2,1,0:T(8,128)(2,1)S(1)} %pad_maximum_fusion.1), channel_id=1, source_target_pairs={{0,1},{1,0},{2,3},{3,2},{4,5},{5,4},{6,7},{7,6},{8,9},{9,8},{10,11... | collective-permute-start | bytes 786440 | tf_op jit(solution)/shard_map/ppermute | solution.py:131
  37.2 9.8 %collective-permute-start.18 = (bf16[8,2,8,128]{3,2,1,0:T(8,128)(2,1)S(1)}, bf16[8,2,8,128]{3,2,1,0:T(8,128)(2,1)S(1)}, u32[]{:S(2)}, u32[]{:S(2)}) collective-permute-start(bf16[8,2,8,128]{3,2,1,0:T(8,128)(2,1)S(1)} %get-tuple-element.43), channel_id=1, source_target_pairs={{0,8},{4,12},{8,0},{12,4},{1,9},{5,13},{9,1},{13,5},{2,10},{6,14},... | collective-permute-start | bytes 98312 | tf_op jit(solution)/shard_map/ppermute | solution.py:131
  41.0 1.4 %collective-permute-start.16 = (bf16[2,12,32,128]{3,2,1,0:T(8,128)(2,1)S(1)}, bf16[2,12,32,128]{3,2,1,0:T(8,128)(2,1)S(1)}, u32[]{:S(2)}, u32[]{:S(2)}) collective-permute-start(bf16[2,12,32,128]{3,2,1,0:T(8,128)(2,1)S(1)} %collective-permute-done.11.refs_6_), channel_id=1, source_target_pairs={{0,1},{1,0},{2,3},{3,2},{4,5},{5,4},{6,7},{7,6},{8,9},{9,8},{10,11... | collective-permute-start | bytes 589832 | tf_op jit(solution)/shard_map/ppermute | solution.py:131
  41.2 5.9 %collective-permute-start.19 = (bf16[8,2,8,128]{3,2,1,0:T(8,128)(2,1)S(1)}, bf16[8,2,8,128]{3,2,1,0:T(8,128)(2,1)S(1)}, u32[]{:S(2)}, u32[]{:S(2)}) collective-permute-start(bf16[8,2,8,128]{3,2,1,0:T(8,128)(2,1)S(1)} %get-tuple-element.50), channel_id=1, source_target_pairs={{0,10},{1,11},{2,8},{3,9},{4,14},{5,15},{6,12},{7,13},{8,2},{9,3},... | collective-permute-start | bytes 98312 | tf_op jit(solution)/shard_map/ppermute | solution.py:143
  44.4 4.3 %collective-permute-start.17 = (bf16[4,2,128,128]{3,2,1,0:T(8,128)(2,1)S(1)}, bf16[4,2,128,128]{3,2,1,0:T(8,128)(2,1)S(1)}, u32[]{:S(2)}, u32[]{:S(2)}) collective-permute-start(bf16[4,2,128,128]{3,2,1,0:T(8,128)(2,1)S(1)} %pad_maximum_fusion), channel_id=1, source_target_pairs={{0,1},{1,0},{2,3},{3,2},{4,5},{5,4},{6,7},{7,6},{8,9},{9,8},{10,11... | collective-permute-start | bytes 786440 | tf_op jit(solution)/shard_map/ppermute | solution.py:131
  44.7 9.0 %collective-permute-start.23 = (bf16[8,2,8,128]{3,2,1,0:T(8,128)(2,1)S(1)}, bf16[8,2,8,128]{3,2,1,0:T(8,128)(2,1)S(1)}, u32[]{:S(2)}, u32[]{:S(2)}) collective-permute-start(bf16[8,2,8,128]{3,2,1,0:T(8,128)(2,1)S(1)} %get-tuple-element.47), channel_id=1, source_target_pairs={{0,12},{4,8},{8,4},{12,0},{1,13},{5,9},{9,5},{13,1},{2,14},{6,10},... | collective-permute-start | bytes 98312 | tf_op jit(solution)/shard_map/ppermute | solution.py:131
  46.9 1.9 %collective-permute-start.20 = (bf16[2,12,32,128]{3,2,1,0:T(8,128)(2,1)S(1)}, bf16[2,12,32,128]{3,2,1,0:T(8,128)(2,1)S(1)}, u32[]{:S(2)}, u32[]{:S(2)}) collective-permute-start(bf16[2,12,32,128]{3,2,1,0:T(8,128)(2,1)S(1)} %collective-permute-done.9.refs_6_), channel_id=1, source_target_pairs={{0,1},{1,0},{2,3},{3,2},{4,5},{5,4},{6,7},{7,6},{8,9},{9,8},{10,11... | collective-permute-start | bytes 589832 | tf_op jit(solution)/shard_map/ppermute | solution.py:131
  47.1 6.7 %collective-permute-start.24 = (bf16[8,2,8,128]{3,2,1,0:T(8,128)(2,1)S(1)}, bf16[8,2,8,128]{3,2,1,0:T(8,128)(2,1)S(1)}, u32[]{:S(2)}, u32[]{:S(2)}) collective-permute-start(bf16[8,2,8,128]{3,2,1,0:T(8,128)(2,1)S(1)} %get-tuple-element.54), channel_id=1, source_target_pairs={{0,14},{1,15},{2,12},{3,13},{4,10},{5,11},{6,8},{7,9},{8,6},{9,7},... | collective-permute-start | bytes 98312 | tf_op jit(solution)/shard_map/ppermute | solution.py:143
  50.8 4.2 %collective-permute-start.21 = (bf16[8,2,8,128]{3,2,1,0:T(8,128)(2,1)S(1)}, bf16[8,2,8,128]{3,2,1,0:T(8,128)(2,1)S(1)}, u32[]{:S(2)}, u32[]{:S(2)}) collective-permute-start(bf16[8,2,8,128]{3,2,1,0:T(8,128)(2,1)S(1)} %get-tuple-element.52), channel_id=1, source_target_pairs={{0,4},{4,0},{8,12},{12,8},{1,5},{5,1},{9,13},{13,9},{2,6},{6,2},{1... | collective-permute-start | bytes 98312 | tf_op jit(solution)/shard_map/ppermute | solution.py:131
  50.9 5.1 %collective-permute-start.22 = (bf16[8,2,8,128]{3,2,1,0:T(8,128)(2,1)S(1)}, bf16[8,2,8,128]{3,2,1,0:T(8,128)(2,1)S(1)}, u32[]{:S(2)}, u32[]{:S(2)}) collective-permute-start(bf16[8,2,8,128]{3,2,1,0:T(8,128)(2,1)S(1)} %get-tuple-element.53), channel_id=1, source_target_pairs={{0,6},{1,7},{2,4},{3,5},{4,2},{5,3},{6,0},{7,1},{8,14},{9,15},{10,... | collective-permute-start | bytes 98312 | tf_op jit(solution)/shard_map/ppermute | solution.py:143
